TPU v7x, 256 devices: a whole 4x4x8 slice. The times are simulated.
256 devices in a mesh: col: 32 (over x, z_lo, core), row: 8 (over z_hi, y).
Axes of the slice: x: 4, y: 4, z: 8 (z_hi: 2, z_lo: 4; z = z_hi * 4 + z_lo), core: 2. Of those that a mesh axis runs over, the one named last changes fastest.
Arguments:
- objects: float32 [2, 2, 4096, 16384], P(None, None, 'row', 'col'), may hold values from -6 to 6
- probe: float32 [2, 256, 256], replicated, may hold values from -6 to 6
- measurements: float32 [8, 32, 3, 256, 256], P('row', 'col'), may hold values from 0.2 to 2.5
- offsets: int32 [8, 32, 3, 2], P('row', 'col'), may hold values from 0 to 512
- counts: int32 [8, 32], P('row', 'col'), may hold values from 1 to 3
Outputs:
- gradients: float32 [2, 2, 4096, 16384], P(None, None, 'row', 'col')
Inputs may be any that keep to these rules, and one draw needn't show every extreme that they name: `offsets`: offsets place every window inside its tile with its border. Each tile uses its first counts positions.
All inputs are finite; a program needn't handle non-finite values.
Results may differ from a plain program's by a relative error of at most 0.0001.
Values sent between devices are 32-bit elements; how exact they have to be, the bound alone decides.
No kernel may reach another device: no remote copies, remote signals or barrier semaphores. Data moves between devices by JAX's collectives and lax.ppermute only.
A program may use at most 128 MiB of HBM per device.

v0:
```python
import math

import jax
import jax.numpy as jnp
from jax import lax
from jax.sharding import PartitionSpec as P

SAMPLES = 2
PROBE = 256
TILE = 512
BORDER = 128


smoothing = 0.5


def from_behind(x, axis, by):
    count = lax.axis_size(axis)
    pairs = [(i, i + by) for i in range(count) if 0 <= i + by < count]
    return lax.ppermute(x, axis, pairs)


def extended_2(cells, sides, width):
    for axis, dim in sides:
        count = lax.axis_size(axis)
        ends = count - 1
        head = lax.slice_in_dim(cells, 0, width, axis=dim)
        tail = lax.slice_in_dim(cells, cells.shape[dim] - width, cells.shape[dim], axis=dim)
        cells = jnp.concatenate(
            [
                lax.ppermute(tail, axis, [(i, (i + 1) % count) for i in range(ends)]),
                cells,
                lax.ppermute(head, axis, [((i + 1) % count, i) for i in range(ends)]),
            ],
            axis=dim,
        )
    return cells


def dft_tables(length):
    places = jnp.arange(length, dtype=jnp.int32)
    product = places[:, None] * places[None, :] % length
    angle = product.astype(jnp.float32) * (2.0 * math.pi / length)
    scale = 1.0 / math.sqrt(length)
    return (jnp.cos(angle) * scale, jnp.sin(angle) * scale)


def transform(real_part, imag_part, cosines, sines, direction):
    highest = lax.Precision.HIGHEST
    left_real = jnp.einsum(
        "kn,snm->skm", cosines, real_part, precision=highest
    ) - direction * jnp.einsum("kn,snm->skm", sines, imag_part, precision=highest)
    left_imag = jnp.einsum(
        "kn,snm->skm", cosines, imag_part, precision=highest
    ) + direction * jnp.einsum("kn,snm->skm", sines, real_part, precision=highest)
    out_real = jnp.einsum(
        "snm,mk->snk", left_real, cosines, precision=highest
    ) - direction * jnp.einsum("snm,mk->snk", left_imag, sines, precision=highest)
    out_imag = jnp.einsum(
        "snm,mk->snk", left_imag, cosines, precision=highest
    ) + direction * jnp.einsum("snm,mk->snk", left_real, sines, precision=highest)
    return (out_real, out_imag)


def fold_cols(gradient):
    width = gradient.shape[3]
    left_strip = gradient[:, :, :, :BORDER]
    right_strip = gradient[:, :, :, width - BORDER :]
    from_right = from_behind(left_strip, "col", -1)
    from_left = from_behind(right_strip, "col", 1)
    middle = gradient[:, :, :, BORDER : width - BORDER]
    inner_width = width - 2 * BORDER
    middle = middle.at[:, :, :, inner_width - BORDER :].add(from_right)
    return middle.at[:, :, :, :BORDER].add(from_left)


def fold_rows(gradient):
    height = gradient.shape[2]
    top_strip = gradient[:, :, :BORDER, :]
    bottom_strip = gradient[:, :, height - BORDER :, :]
    from_below = from_behind(top_strip, "row", -1)
    from_above = from_behind(bottom_strip, "row", 1)
    middle = gradient[:, :, BORDER : height - BORDER, :]
    inner_height = height - 2 * BORDER
    middle = middle.at[:, :, inner_height - BORDER :, :].add(from_below)
    return middle.at[:, :, :BORDER, :].add(from_above)


def body(objects, probe, measurements, offsets, counts):
    extended = extended_2(objects, (("row", 2), ("col", 3)), BORDER)
    cosines, sines = dft_tables(PROBE)
    probe_real = probe[0]
    probe_imag = probe[1]
    gradient = jnp.zeros(extended.shape, jnp.float32)
    anchor = jnp.zeros((), jnp.int32)
    tile = 0

    def visit(position, accum, tile=tile):
        row_start = tile * TILE + offsets[tile, 0, position, 0]
        col_start = offsets[tile, 0, position, 1]
        corner = (anchor, anchor, row_start, col_start)
        window = lax.dynamic_slice(extended, corner, (SAMPLES, 2, PROBE, PROBE))
        obj_real = window[:, 0]
        obj_imag = window[:, 1]
        wave_real = probe_real * obj_real - probe_imag * obj_imag
        wave_imag = probe_real * obj_imag + probe_imag * obj_real
        spec_real, spec_imag = transform(wave_real, wave_imag, cosines, sines, -1.0)
        amplitude = jnp.sqrt(spec_real * spec_real + spec_imag * spec_imag + smoothing)
        factor = 1.0 - measurements[tile, 0, position] / amplitude
        back_real, back_imag = transform(
            spec_real * factor, spec_imag * factor, cosines, sines, 1.0
        )
        grad_real = probe_real * back_real + probe_imag * back_imag
        grad_imag = probe_real * back_imag - probe_imag * back_real
        piece = jnp.stack([grad_real, grad_imag], axis=1)
        current = lax.dynamic_slice(accum, corner, (SAMPLES, 2, PROBE, PROBE))
        return lax.dynamic_update_slice(accum, current + piece, corner)

    gradient = lax.fori_loop(0, counts[tile, 0], visit, gradient)
    result = fold_rows(fold_cols(gradient))
    return result


def solution(mesh):
    in_specs = (
        P(None, None, "row", "col"),
        P(),
        P("row", "col", None, None, None),
        P("row", "col", None, None),
        P("row", "col"),
    )
    out_specs = P(None, None, "row", "col")
    return jax.shard_map(body, mesh=mesh, in_specs=in_specs, out_specs=out_specs, check_vma=False)
```

profile of v0, /device:TPU:161, one launch (start us, length us, event | category | flops | bytes accessed | tf_op | source)
XLA Modules:
  0.0 389.1 jit_solution(7241188835945972194)
XLA Ops:
  2.0 3.2 collective-permute-start
  5.3 8.1 %collective-permute-start.1 = (f32[2,2,128,512]{3,2,0,1:T(8,128)S(1)}, f32[2,2,128,512]{3,2,0,1:T(8,128)S(1)}, u32[]{:S(2)}, u32[]{:S(2)}) collective-permute-start(f32[2,2,128,512]{3,2,0,1:T(8,128)S(1)} %copy.51), channel_id=1, source_target_pairs={{1,0},{2,1},{3,2},{4,3},{5,4},{6,5},{7,6},{9,8},{10,9},{11,10},{12... | collective-permute-start | bytes 3145736 | tf_op jit(solution)/shard_map/ppermute | solution.py:33
  13.4 60.0 %collective-permute-done = f32[2,2,128,512]{3,2,0,1:T(8,128)S(1)} collective-permute-done((f32[2,2,128,512]{3,2,0,1:T(8,128)S(1)}, f32[2,2,128,512]{3,2,0,1:T(8,128)S(1)}, u32[]{:S(2)}, u32[]{:S(2)}) %collective-permute-start) | collective-permute-done | bytes 1048608 | tf_op jit(solution)/shard_map/ppermute | solution.py:31
  74.8 2.7 copy-done
  81.3 3.4 collective-permute-start.3
  84.8 14.2 %collective-permute-done.2 = f32[2,2,768,128]{3,2,0,1:T(8,128)S(1)} collective-permute-done((f32[2,2,768,128]{3,2,0,1:T(8,128)}, f32[2,2,768,128]{3,2,0,1:T(8,128)S(1)}, u32[]{:S(2)}, u32[]{:S(2)}) %collective-permute-start.2) | collective-permute-done | bytes 1572896 | tf_op jit(solution)/shard_map/ppermute | solution.py:31
  99.0 4.4 %collective-permute-done.3 = f32[2,2,768,128]{3,2,0,1:T(8,128)} collective-permute-done((f32[2,2,768,128]{3,2,0,1:T(8,128)}, f32[2,2,768,128]{3,2,0,1:T(8,128)}, u32[]{:S(2)}, u32[]{:S(2)}) %collective-permute-start.3) | collective-permute-done | bytes 1572896 | tf_op jit(solution)/shard_map/ppermute | solution.py:33
  103.4 7.8 %pad_maximum_fusion = f32[2,2,768,768]{3,2,0,1:T(8,128)} fusion(f32[2,2,768,128]{3,2,0,1:T(8,128)} %collective-permute-done.3, f32[2,2,768,512]{3,2,0,1:T(8,128)} %copy-done, f32[2,2,768,128]{3,2,0,1:T(8,128)S(1)} %collective-permute-done.2), kind=kLoop, calls=%fused_computation.147 | loop fusion | flops 4718592 | bytes 18874368 | tf_op jit(solution)/shard_map/concatenate | solution.py:29
  111.1 4.5 %broadcast_in_dim.2.clone = f32[2,2,768,768]{3,2,1,0:T(8,128)} broadcast(f32[]{:T(128)} %constant.135.clone.1), dimensions={} | broadcast | bytes 9437188 | tf_op jit(solution)/shard_map/broadcast_in_dim | solution.py:94
  115.6 178.2 %while.16 = (s32[]{:T(128)}, f32[2,2,768,768]{3,2,1,0:T(8,128)}, s32[]{:T(128)}, s32[1,1,3,2]{2,3,1,0:T(2,128)S(1)}, f32[1,256,256]{2,1,0:T(8,128)S(1)}, /*index...) while((s32[]{:T(128)}, f32[2,2,768,768]{3,2,1,0:T(8,128)}, ...), condition=%wide.region_1.2_spmd.clone.clone, body=%wide.region_0.1_spmd.clone.clone.sunk | while | flops 6465519616 | bytes 36176164 | solution.py:119
  167.5 2.0 fusion.237
  176.9 12.0 %dynamic_update_slice.6 = f32[2,2,768,768]{3,2,1,0:T(8,128)} dynamic-update-slice(f32[2,2,768,768]{3,2,1,0:T(8,128)} %get-tuple-element.317, f32[2,2,256,256]{3,2,1,0:T(8,128)S(1)} %copy.55, s32[]{:T(128)} %constant.134.clone.1..sunk, s32[]{:T(128)} %constant.134.clone.1..sunk, s32[]{:T(128)S(6)} %select_n.162, s32[]{:T(128)S(6)} %select_n.163) | dynamic-update-slice | bytes 2097156 | tf_op jit(solution)/shard_map/while/body/dynamic_update_slice | solution.py:117
  219.3 2.0 fusion.237
  228.8 12.3 %dynamic_update_slice.6 = f32[2,2,768,768]{3,2,1,0:T(8,128)} dynamic-update-slice(f32[2,2,768,768]{3,2,1,0:T(8,128)} %get-tuple-element.317, f32[2,2,256,256]{3,2,1,0:T(8,128)S(1)} %copy.55, s32[]{:T(128)} %constant.134.clone.1..sunk, s32[]{:T(128)} %constant.134.clone.1..sunk, s32[]{:T(128)S(6)} %select_n.162, s32[]{:T(128)S(6)} %select_n.163) | dynamic-update-slice | bytes 2097156 | tf_op jit(solution)/shard_map/while/body/dynamic_update_slice | solution.py:117
  280.9 12.1 %dynamic_update_slice.6 = f32[2,2,768,768]{3,2,1,0:T(8,128)} dynamic-update-slice(f32[2,2,768,768]{3,2,1,0:T(8,128)} %get-tuple-element.317, f32[2,2,256,256]{3,2,1,0:T(8,128)S(1)} %copy.55, s32[]{:T(128)} %constant.134.clone.1..sunk, s32[]{:T(128)} %constant.134.clone.1..sunk, s32[]{:T(128)S(6)} %select_n.162, s32[]{:T(128)S(6)} %select_n.163) | dynamic-update-slice | bytes 2097156 | tf_op jit(solution)/shard_map/while/body/dynamic_update_slice | solution.py:117
  293.8 2.1 fusion.131
  295.9 3.2 collective-permute-start.4
  299.1 2.4 collective-permute-start.5
  301.5 3.5 slice.166
  305.0 12.9 %collective-permute-done.4 = f32[2,2,768,128]{3,2,1,0:T(8,128)S(1)} collective-permute-done((f32[2,2,768,128]{3,2,1,0:T(8,128)S(1)}, f32[2,2,768,128]{3,2,1,0:T(8,128)S(1)}, u32[]{:S(2)}, u32[]{:S(2)}) %collective-permute-start.4) | collective-permute-done | bytes 1572896 | tf_op jit(solution)/shard_map/ppermute | solution.py:20
  320.2 16.8 %collective-permute-start.6 = (f32[2,2,128,512]{3,2,1,0:T(8,128)S(1)}, f32[2,2,128,512]{3,2,1,0:T(8,128)S(1)}, u32[]{:S(2)}, u32[]{:S(2)}) collective-permute-start(f32[2,2,128,512]{3,2,1,0:T(8,128)S(1)} %get-tuple-element.234), channel_id=1, source_target_pairs={{1,0},{2,1},{3,2},{4,3},{5,4},{6,5},{7,6},{9,8},{10,9},{11,10},{12... | collective-permute-start | bytes 3145736 | tf_op jit(solution)/shard_map/ppermute | solution.py:20
  339.4 36.6 %collective-permute-done.6 = f32[2,2,128,512]{3,2,1,0:T(8,128)S(1)} collective-permute-done((f32[2,2,128,512]{3,2,1,0:T(8,128)S(1)}, f32[2,2,128,512]{3,2,1,0:T(8,128)S(1)}, u32[]{:S(2)}, u32[]{:S(2)}) %collective-permute-start.6) | collective-permute-done | bytes 1048608 | tf_op jit(solution)/shard_map/ppermute | solution.py:20
  376.2 10.2 %collective-permute-done.7 = f32[2,2,128,512]{3,2,1,0:T(8,128)S(1)} collective-permute-done((f32[2,2,128,512]{3,2,1,0:T(8,128)S(1)}, f32[2,2,128,512]{3,2,1,0:T(8,128)S(1)}, u32[]{:S(2)}, u32[]{:S(2)}) %collective-permute-start.7) | collective-permute-done | bytes 1048608 | tf_op jit(solution)/shard_map/ppermute | solution.py:20
  386.3 2.4 fusion.129
  (87 shorter events, 113.7 us)
Async XLA Ops:
  0.0 73.5 %copy-start.1 = (f32[2,2,512,512]{3,2,1,0:T(8,128)S(1)}, f32[2,2,512,512]{3,2,1,0:T(8,128)}, u32[]{:S(2)}) copy-start(f32[2,2,512,512]{3,2,1,0:T(8,128)} %param.15) | copy-start | bytes 12582916
  2.0 71.4 %collective-permute-start = (f32[2,2,128,512]{3,2,0,1:T(8,128)S(1)}, f32[2,2,128,512]{3,2,0,1:T(8,128)S(1)}, u32[]{:S(2)}, u32[]{:S(2)}) collective-permute-start(f32[2,2,128,512]{3,2,0,1:T(8,128)S(1)} %copy.50), channel_id=1, source_target_pairs={{0,1},{1,2},{2,3},{3,4},{4,5},{5,6},{6,7},{8,9},{9,10},{10,11},{11... | collective-permute-start | bytes 3145736 | tf_op jit(solution)/shard_map/ppermute | solution.py:31
  5.3 69.4 %collective-permute-start.1 = (f32[2,2,128,512]{3,2,0,1:T(8,128)S(1)}, f32[2,2,128,512]{3,2,0,1:T(8,128)S(1)}, u32[]{:S(2)}, u32[]{:S(2)}) collective-permute-start(f32[2,2,128,512]{3,2,0,1:T(8,128)S(1)} %copy.51), channel_id=1, source_target_pairs={{1,0},{2,1},{3,2},{4,3},{5,4},{6,5},{7,6},{9,8},{10,9},{11,10},{12... | collective-permute-start | bytes 3145736 | tf_op jit(solution)/shard_map/ppermute | solution.py:33
  74.0 10.7 %copy-start.3 = (f32[2,256,256]{2,1,0:T(8,128)S(1)}, f32[2,256,256]{2,1,0:T(8,128)}, u32[]{:S(2)}) copy-start(f32[2,256,256]{2,1,0:T(8,128)} %param.16) | copy-start | bytes 1572868
  74.8 2.7 copy-start
  79.4 19.6 %collective-permute-start.2 = (f32[2,2,768,128]{3,2,0,1:T(8,128)}, f32[2,2,768,128]{3,2,0,1:T(8,128)S(1)}, u32[]{:S(2)}, u32[]{:S(2)}) collective-permute-start(f32[2,2,768,128]{3,2,0,1:T(8,128)} %get-tuple-element.235), channel_id=1, source_target_pairs={{0,8},{8,16},{16,24},{24,32},{32,40},{40,48},{48,56},{56,64},{64,7... | collective-permute-start | bytes 4718600 | tf_op jit(solution)/shard_map/ppermute | solution.py:31
  81.3 22.1 %collective-permute-start.3 = (f32[2,2,768,128]{3,2,0,1:T(8,128)}, f32[2,2,768,128]{3,2,0,1:T(8,128)}, u32[]{:S(2)}, u32[]{:S(2)}) collective-permute-start(f32[2,2,768,128]{3,2,0,1:T(8,128)} %get-tuple-element.236), channel_id=1, source_target_pairs={{8,0},{16,8},{24,16},{32,24},{40,32},{48,40},{56,48},{64,56},{72,6... | collective-permute-start | bytes 4718600 | tf_op jit(solution)/shard_map/ppermute | solution.py:33
  111.1 4.5 %copy-start.4 = (s32[1,1,3,2]{2,3,1,0:T(2,128)S(1)}, s32[1,1,3,2]{2,3,1,0:T(2,128)}, u32[]{:S(2)}) copy-start(s32[1,1,3,2]{2,3,1,0:T(2,128)} %param.18) | copy-start | bytes 76
  295.9 22.0 %collective-permute-start.4 = (f32[2,2,768,128]{3,2,1,0:T(8,128)S(1)}, f32[2,2,768,128]{3,2,1,0:T(8,128)S(1)}, u32[]{:S(2)}, u32[]{:S(2)}) collective-permute-start(f32[2,2,768,128]{3,2,1,0:T(8,128)S(1)} %get-tuple-element.232), channel_id=1, source_target_pairs={{8,0},{16,8},{24,16},{32,24},{40,32},{48,40},{56,48},{64,56},{72,6... | collective-permute-start | bytes 4718600 | tf_op jit(solution)/shard_map/ppermute | solution.py:20
  299.1 20.5 %collective-permute-start.5 = (f32[2,2,768,128]{3,2,1,0:T(8,128)S(1)}, f32[2,2,768,128]{3,2,1,0:T(8,128)S(1)}, u32[]{:S(2)}, u32[]{:S(2)}) collective-permute-start(f32[2,2,768,128]{3,2,1,0:T(8,128)S(1)} %get-tuple-element.231), channel_id=1, source_target_pairs={{0,8},{8,16},{16,24},{24,32},{32,40},{40,48},{48,56},{56,64},{64,7... | collective-permute-start | bytes 4718600 | tf_op jit(solution)/shard_map/ppermute | solution.py:20
  320.2 55.8 %collective-permute-start.6 = (f32[2,2,128,512]{3,2,1,0:T(8,128)S(1)}, f32[2,2,128,512]{3,2,1,0:T(8,128)S(1)}, u32[]{:S(2)}, u32[]{:S(2)}) collective-permute-start(f32[2,2,128,512]{3,2,1,0:T(8,128)S(1)} %get-tuple-element.234), channel_id=1, source_target_pairs={{1,0},{2,1},{3,2},{4,3},{5,4},{6,5},{7,6},{9,8},{10,9},{11,10},{12... | collective-permute-start | bytes 3145736 | tf_op jit(solution)/shard_map/ppermute | solution.py:20
  337.0 49.4 %collective-permute-start.7 = (f32[2,2,128,512]{3,2,1,0:T(8,128)S(1)}, f32[2,2,128,512]{3,2,1,0:T(8,128)S(1)}, u32[]{:S(2)}, u32[]{:S(2)}) collective-permute-start(f32[2,2,128,512]{3,2,1,0:T(8,128)S(1)} %get-tuple-element.233), channel_id=1, source_target_pairs={{0,1},{1,2},{2,3},{3,4},{4,5},{5,6},{6,7},{8,9},{9,10},{10,11},{11... | collective-permute-start | bytes 3145736 | tf_op jit(solution)/shard_map/ppermute | solution.py:20
  376.2 10.2 %copy-start.2 = (f32[2,2,512,512]{3,2,1,0:T(8,128)}, f32[2,2,512,512]{3,2,1,0:T(8,128)S(1)}, u32[]{:S(2)}) copy-start(f32[2,2,512,512]{3,2,1,0:T(8,128)S(1)} %fusion.130) | copy-start | bytes 12582916
where the time goes:
time: 394 us; the launch traced here: 389 us
  waiting for transfers between devices  139 us (35%)
  matrix products  89.8 us (23%)
  local copies, waits for them, and re-layouts  59.4 us (15%)
  starting transfers between devices  40.8 us (10%)
  loops' own time  36.3 us (9%)
  other arithmetic  23.1 us (6%)
    ppermute x2, waiting for transfers between devices, extended_2(): lax.ppermute(tail, axis, [(i, (i + 1) % count) for i in range(ends)])  74.2 us
    ppermute x4, waiting for transfers between devices, from_behind(): return lax.ppermute(x, axis, pairs)  59.7 us
    dynamic_update_slice x6, local copies, waits for them, and re-layouts, visit(): return lax.dynamic_update_slice(accum, current + piece, corner)  36.6 us
    another operation x1, loops' own time, body(): gradient = lax.fori_loop(0, counts[tile, 0], visit, gradient)  36.3 us
    ppermute x4, starting transfers between devices, from_behind(): return lax.ppermute(x, axis, pairs)  24.3 us
    ppermute x2, starting transfers between devices, extended_2(): lax.ppermute(head, axis, [((i + 1) % count, i) for i in range(ends)])  11.5 us
    dot_general x6, matrix products, transform(): jnp.einsum('kn,snm->skm', sines, real_part, precision=highest)  11.4 us
    dot_general x6, matrix products, transform(): jnp.einsum('kn,snm->skm', sines, imag_part, precision=highest)  11.4 us
  transfers between devices with their start and end apart: 8, of which 7 were waited for; matrix products, arithmetic and copies ran while one was open for 2% of the time, Pallas kernels for 0%

commit v1 on v0

v1 whole, which is shorter than its diff:
```python
import functools
import math

import jax
import jax.numpy as jnp
import ml_dtypes
import numpy as np
from jax import lax
from jax.experimental import pallas as pl
from jax.experimental.pallas import tpu as pltpu
from jax.sharding import PartitionSpec as P

SAMPLES = 2
POS = 3
PROBE = 256
TILE = 512
BORDER = 128
EXT = TILE + 2 * BORDER
SMOOTHING = 0.5


def dft_tables():
    places = np.arange(PROBE, dtype=np.int64)
    angle = (places[:, None] * places[None, :] % PROBE) * (2.0 * math.pi / PROBE)
    scale = 1.0 / math.sqrt(PROBE)
    cosines, sines = np.cos(angle) * scale, np.sin(angle) * scale
    forward = np.block([[cosines, -sines], [sines, cosines]]).astype(np.float32)
    high = forward.astype(ml_dtypes.bfloat16)
    low = (forward - high.astype(np.float32)).astype(ml_dtypes.bfloat16)
    return np.stack([high, low, high.T, low.T])


def split(x):
    high = x.astype(jnp.bfloat16)
    low = (x - high.astype(jnp.float32)).astype(jnp.bfloat16)
    return high, low


def dot(a, b):
    return jnp.dot(a, b, preferred_element_type=jnp.float32)


def right_product(x, high, low):
    xh, xl = split(x)
    return dot(xh, high) + dot(xl, high) + dot(xh, low)


def left_product(high, low, x):
    xh, xl = split(x)
    return dot(high, xh) + dot(high, xl) + dot(low, xh)


PLACES = {
    "center": (BORDER, BORDER, TILE, TILE),
    "top": (0, BORDER, BORDER, TILE),
    "bottom": (BORDER + TILE, BORDER, BORDER, TILE),
    "left": (0, 0, EXT, BORDER),
    "right": (0, BORDER + TILE, EXT, BORDER),
}


def gradient_kernel(offsets, counts, *refs):
    names = list(PLACES)
    n = len(names)
    pieces = dict(zip(names, refs[:n]))
    probe, measurements, tables = refs[n : n + 3]
    outs = dict(zip(names, refs[n + 3 : 2 * n + 3]))
    obj, grad, sem = refs[2 * n + 3 :]
    samples = obj.shape[0]

    def view(ref, name):
        r, c, h, w = PLACES[name]
        return ref.at[:, :, pl.ds(r, h), pl.ds(c, w)]

    loads = [
        pltpu.make_async_copy(pieces[k], view(obj, k), sem.at[i])
        for i, k in enumerate(names)
    ]
    for copy in loads:
        copy.start()
    grad[...] = jnp.zeros_like(grad)
    for copy in loads:
        copy.wait()

    lanes = lax.broadcasted_iota(jnp.int32, (PROBE, 128), 1)
    rows = lax.broadcasted_iota(jnp.int32, (8, 128), 0)

    def visit(q, carry):
        r0 = offsets[q * 2]
        c0 = offsets[q * 2 + 1]
        rt, ct = lax.rem(r0, 8), lax.rem(c0, 128)
        ra = pl.multiple_of(r0 - rt, 8)
        rz = pl.multiple_of(jnp.minimum(ra + PROBE, EXT - 8), 8)
        ca = pl.multiple_of(c0 - ct, 128)
        cb = pl.multiple_of(ca + 128, 128)
        cz = pl.multiple_of(jnp.minimum(ca + 256, EXT - 128), 128)
        early = lanes < ct
        above = rows < rt

        pr = pltpu.roll(pltpu.roll(probe[0], rt, 0), ct, 1)
        pi = pltpu.roll(pltpu.roll(probe[1], rt, 0), ct, 1)

        def block(s, k, col):
            head = jnp.where(
                above,
                obj[s, k, pl.ds(rz, 8), pl.ds(col, 128)],
                obj[s, k, pl.ds(ra, 8), pl.ds(col, 128)],
            )
            tail = obj[s, k, pl.ds(pl.multiple_of(ra + 8, 8), PROBE - 8), pl.ds(col, 128)]
            return jnp.concatenate([head, tail], axis=0)

        def frame(s, k):
            first = jnp.where(early, block(s, k, cz), block(s, k, ca))
            return jnp.concatenate([first, block(s, k, cb)], axis=1)

        def scatter(s, k, value):
            def add(col, v):
                grad[s, k, pl.ds(pl.multiple_of(ra + 8, 8), PROBE - 8), pl.ds(col, 128)] += v[8:]
                grad[s, k, pl.ds(ra, 8), pl.ds(col, 128)] += jnp.where(above, 0.0, v[:8])
                grad[s, k, pl.ds(rz, 8), pl.ds(col, 128)] += jnp.where(above, v[:8], 0.0)

            first = value[:, :128]
            add(ca, jnp.where(early, 0.0, first))
            add(cz, jnp.where(early, first, 0.0))
            add(cb, value[:, 128:])

        stacked = []
        for s in range(samples):
            o_r, o_i = frame(s, 0), frame(s, 1)
            stacked.append(
                jnp.concatenate([pr * o_r - pi * o_i, pr * o_i + pi * o_r], axis=1)
            )
        wave = jnp.concatenate(stacked, axis=0)
        half = right_product(wave, tables[0], tables[1])
        turned = jnp.concatenate(
            [
                jnp.concatenate(
                    [half[s * PROBE : (s + 1) * PROBE, k * PROBE : (k + 1) * PROBE] for s in range(samples)],
                    axis=1,
                )
                for k in range(2)
            ],
            axis=0,
        )
        spectrum = left_product(tables[2], tables[3], turned)
        s_r, s_i = spectrum[:PROBE], spectrum[PROBE:]
        m = measurements[q]
        m = jnp.concatenate([m] * samples, axis=1)
        factor = 1.0 - m * lax.rsqrt(s_r * s_r + s_i * s_i + SMOOTHING)
        scaled = jnp.concatenate([s_r * factor, s_i * factor], axis=0)
        back = left_product(tables[0], tables[1], scaled)
        back = jnp.concatenate(
            [
                jnp.concatenate(
                    [back[:PROBE, s * PROBE : (s + 1) * PROBE], back[PROBE:, s * PROBE : (s + 1) * PROBE]],
                    axis=1,
                )
                for s in range(samples)
            ],
            axis=0,
        )
        final = right_product(back, tables[2], tables[3])
        for s in range(samples):
            b_r = final[s * PROBE : (s + 1) * PROBE, :PROBE]
            b_i = final[s * PROBE : (s + 1) * PROBE, PROBE:]
            scatter(s, 0, pr * b_r + pi * b_i)
            scatter(s, 1, pr * b_i - pi * b_r)
        return carry

    lax.fori_loop(0, counts[0], visit, 0)
    stores = [
        pltpu.make_async_copy(view(grad, k), outs[k], sem.at[i])
        for i, k in enumerate(names)
    ]
    for copy in stores:
        copy.start()
    for copy in stores:
        copy.wait()


def window_gradients(pieces, probe, measurements, offsets, counts):
    samples = pieces["center"].shape[0]
    names = list(PLACES)
    shapes = [jax.ShapeDtypeStruct((samples, 2) + PLACES[k][2:], jnp.float32) for k in names]
    anywhere = pl.BlockSpec(memory_space=pl.ANY)
    inside = pl.BlockSpec(memory_space=pltpu.VMEM)
    scalars = pl.BlockSpec(memory_space=pltpu.SMEM)
    outs = pl.pallas_call(
        gradient_kernel,
        out_shape=shapes,
        in_specs=[scalars, scalars] + [anywhere] * len(names) + [inside] * 3,
        out_specs=[anywhere] * len(names),
        scratch_shapes=[
            pltpu.VMEM((samples, 2, EXT, EXT), jnp.float32),
            pltpu.VMEM((samples, 2, EXT, EXT), jnp.float32),
            pltpu.SemaphoreType.DMA((len(names),)),
        ],
        compiler_params=pltpu.CompilerParams(vmem_limit_bytes=56 * 1024 * 1024),
    )(
        offsets.reshape(-1),
        counts.reshape(-1),
        *[pieces[k] for k in names],
        probe,
        measurements,
        jnp.asarray(dft_tables()),
    )
    return dict(zip(names, outs))


def shifted(x, axis, by):
    count = lax.axis_size(axis)
    pairs = [(i, i + by) for i in range(count) if 0 <= i + by < count]
    return lax.ppermute(x, axis, pairs)


def body(objects, probe, measurements, offsets, counts):
    top = shifted(objects[:, :, TILE - BORDER :, :], "row", 1)
    bottom = shifted(objects[:, :, :BORDER, :], "row", -1)

    def column(lo):
        return jnp.concatenate([x[..., lo : lo + BORDER] for x in (top, objects, bottom)], axis=2)

    left = shifted(column(TILE - BORDER), "col", 1)
    right = shifted(column(0), "col", -1)
    pieces = dict(center=objects, top=top, bottom=bottom, left=left, right=right)
    g = window_gradients(pieces, probe, measurements[0, 0], offsets, counts)
    from_right = shifted(g["left"], "col", -1)
    from_left = shifted(g["right"], "col", 1)

    def folded(x, lo, hi):
        x = x.at[..., TILE - BORDER :].add(from_right[:, :, lo:hi])
        return x.at[..., :BORDER].add(from_left[:, :, lo:hi])

    from_below = shifted(folded(g["top"], 0, BORDER), "row", -1)
    from_above = shifted(folded(g["bottom"], BORDER + TILE, EXT), "row", 1)
    result = folded(g["center"], BORDER, BORDER + TILE)
    result = result.at[:, :, TILE - BORDER :].add(from_below)
    return result.at[:, :, :BORDER].add(from_above)


def solution(mesh):
    in_specs = (
        P(None, None, "row", "col"),
        P(),
        P("row", "col", None, None, None),
        P("row", "col", None, None),
        P("row", "col"),
    )
    out_specs = P(None, None, "row", "col")
    return jax.shard_map(body, mesh=mesh, in_specs=in_specs, out_specs=out_specs, check_vma=False)
```

time: 394 us -> 225 us (0.57)
  the two profiles are of different devices: /device:TPU:161 before, /device:TPU:60 now
where the time goes in v1:
time: 225 us; the launch traced here: 223 us
  waiting for transfers between devices  144 us (64%)
  starting transfers between devices  37.8 us (17%)
  Pallas kernels  22.3 us (10%)
  other arithmetic  14.8 us (7%)
  local copies, waits for them, and re-layouts  4.09 us (2%)
    ppermute x8, waiting for transfers between devices, shifted(): return lax.ppermute(x, axis, pairs)  144 us
    ppermute x8, starting transfers between devices, shifted(): return lax.ppermute(x, axis, pairs)  37.8 us
    pallas_call x1, Pallas kernels, window_gradients(): pl.pallas_call(gradient_kernel, out_shape=shapes, in_specs=[scalars, scal...  22.3 us
  transfers between devices with their start and end apart: 8, of which 6 were waited for; matrix products, arithmetic and copies ran while one was open for 4% of the time, Pallas kernels for 0%

profile of v1, /device:TPU:60, one launch (start us, length us, event | category | flops | bytes accessed | tf_op | source)
XLA Modules:
  0.0 223.5 jit_solution(17868250966225209326)
XLA Ops:
  0.0 1.9 fusion.9
  1.9 2.7 %collective-permute-start.1 = (f32[2,2,128,512]{3,2,1,0:T(8,128)S(1)}, f32[2,2,128,512]{3,2,1,0:T(8,128)S(1)}, u32[]{:S(2)}, u32[]{:S(2)}) collective-permute-start(f32[2,2,128,512]{3,2,1,0:T(8,128)S(1)} %get-tuple-element.113), channel_id=1, source_target_pairs={{1,0},{2,1},{3,2},{4,3},{5,4},{6,5},{7,6},{9,8},{10,9},{11,10},{12... | collective-permute-start | bytes 3145736 | tf_op jit(solution)/shard_map/ppermute | solution.py:213
  4.6 9.2 %collective-permute-start = (f32[2,2,128,512]{3,2,1,0:T(8,128)S(1)}, f32[2,2,128,512]{3,2,1,0:T(8,128)S(1)}, u32[]{:S(2)}, u32[]{:S(2)}) collective-permute-start(f32[2,2,128,512]{3,2,1,0:T(8,128)S(1)} %get-tuple-element.114), channel_id=1, source_target_pairs={{0,1},{1,2},{2,3},{3,4},{4,5},{5,6},{6,7},{8,9},{9,10},{10,11},{11... | collective-permute-start | bytes 3145736 | tf_op jit(solution)/shard_map/ppermute | solution.py:213
  14.0 60.3 %collective-permute-done.1.refs_2_ = f32[2,2,128,512]{3,2,1,0:T(8,128)S(1)} collective-permute-done((f32[2,2,128,512]{3,2,1,0:T(8,128)S(1)}, f32[2,2,128,512]{3,2,1,0:T(8,128)S(1)}, u32[]{:S(2)}, u32[]{:S(2)}) %collective-permute-start.1) | collective-permute-done | bytes 1048608 | tf_op jit(solution)/shard_map/ppermute | solution.py:213
  74.3 0.9 collective-permute-done.refs_1_
  75.3 1.5 pad_maximum_fusion
  76.8 1.9 collective-permute-start.2
  78.9 3.6 %collective-permute-start.3 = (f32[2,2,768,128]{3,2,1,0:T(8,128)S(1)}, f32[2,2,768,128]{3,2,1,0:T(8,128)S(1)}, u32[]{:S(2)}, u32[]{:S(2)}) collective-permute-start(f32[2,2,768,128]{3,2,1,0:T(8,128)S(1)} %pad_maximum_fusion.1), channel_id=1, source_target_pairs={{8,0},{16,8},{24,16},{32,24},{40,32},{48,40},{56,48},{64,56},{72,6... | collective-permute-start | bytes 4718600 | tf_op jit(solution)/shard_map/ppermute | solution.py:213
  83.9 15.0 %collective-permute-done.2.refs_3_ = f32[2,2,768,128]{3,2,1,0:T(8,128)} collective-permute-done((f32[2,2,768,128]{3,2,1,0:T(8,128)}, f32[2,2,768,128]{3,2,1,0:T(8,128)}, u32[]{:S(2)}, u32[]{:S(2)}) %collective-permute-start.2) | collective-permute-done | bytes 1572896 | tf_op jit(solution)/shard_map/ppermute | solution.py:213
  98.9 1.6 collective-permute-done.3.refs_4_
  100.4 1.2 copy-done.3
  101.6 22.3 %shard_map.64 = (f32[2,2,512,512]{3,2,1,0:T(8,128)}, f32[2,2,128,512]{3,2,1,0:T(8,128)}, f32[2,2,128,512]{3,2,1,0:T(8,128)}, f32[2,2,768,128]{3,2,1,0:T(8,128)}, f32[2,2,768,128]{3,2,1,0:T(8,128)}) custom-call(s32[6]{0:T(128)} %reshape.275.offsets, s32[1]{0:T(128)} %bitcast.2.counts, f32[2,2,512,512]{3,2,1,0:T(8,128)} %refs_0_.1, ...), custom_call_target="tpu_custom_call" | custom-call | tf_op jit(solution)/shard_map/pallas_call | solution.py:188
  123.9 3.8 %collective-permute-start.4 = (f32[2,2,768,128]{3,2,1,0:T(8,128)}, f32[2,2,768,128]{3,2,1,0:T(8,128)S(1)}, u32[]{:S(2)}, u32[]{:S(2)}) collective-permute-start(f32[2,2,768,128]{3,2,1,0:T(8,128)} %get-tuple-element.107), channel_id=1, source_target_pairs={{8,0},{16,8},{24,16},{32,24},{40,32},{48,40},{56,48},{64,56},{72,6... | collective-permute-start | bytes 4718600 | tf_op jit(solution)/shard_map/ppermute | solution.py:213
  127.7 1.9 collective-permute-start.5
  129.7 30.7 %collective-permute-done.4 = f32[2,2,768,128]{3,2,1,0:T(8,128)S(1)} collective-permute-done((f32[2,2,768,128]{3,2,1,0:T(8,128)}, f32[2,2,768,128]{3,2,1,0:T(8,128)S(1)}, u32[]{:S(2)}, u32[]{:S(2)}) %collective-permute-start.4) | collective-permute-done | bytes 1572896 | tf_op jit(solution)/shard_map/ppermute | solution.py:213
  160.4 2.0 fusion.5
  162.3 1.9 fusion.4
  164.2 1.9 collective-permute-start.6
  166.1 12.8 %collective-permute-start.7 = (f32[2,2,128,512]{3,2,1,0:T(8,128)}, f32[2,2,128,512]{3,2,1,0:T(8,128)S(1)}, u32[]{:S(2)}, u32[]{:S(2)}) collective-permute-start(f32[2,2,128,512]{3,2,1,0:T(8,128)} %get-tuple-element.115), channel_id=1, source_target_pairs={{0,1},{1,2},{2,3},{3,4},{4,5},{5,6},{6,7},{8,9},{9,10},{10,11},{11... | collective-permute-start | bytes 3145736 | tf_op jit(solution)/shard_map/ppermute | solution.py:213
  178.9 2.3 %fusion.3 = f32[2,2,512,512]{3,2,1,0:T(8,128)} fusion(f32[2,2,512,512]{3,2,1,0:T(8,128)} %get-tuple-element.106, f32[2,2,768,128]{3,2,1,0:T(8,128)S(1)} %collective-permute-done.4), kind=kLoop, calls=%fused_computation.9 | loop fusion | flops 262144 | bytes 3145728 | tf_op jit(solution)/shard_map/scatter-add | solution.py:231
  181.2 2.3 %fusion.2 = f32[2,2,512,512]{3,2,1,0:T(8,128)} fusion(f32[2,2,512,512]{3,2,1,0:T(8,128)} %fusion.3, f32[2,2,768,128]{3,2,1,0:T(8,128)S(1)} %collective-permute-done.5), kind=kLoop, calls=%fused_computation.7 | loop fusion | flops 262144 | bytes 3145728 | tf_op jit(solution)/shard_map/scatter-add | solution.py:232
  183.5 35.2 %collective-permute-done.6 = f32[2,2,128,512]{3,2,1,0:T(8,128)S(1)} collective-permute-done((f32[2,2,128,512]{3,2,1,0:T(8,128)}, f32[2,2,128,512]{3,2,1,0:T(8,128)S(1)}, u32[]{:S(2)}, u32[]{:S(2)}) %collective-permute-start.6) | collective-permute-done | bytes 1048608 | tf_op jit(solution)/shard_map/ppermute | solution.py:213
  218.7 2.4 %fusion.1 = f32[2,2,512,512]{3,2,1,0:T(8,128)} fusion(f32[2,2,512,512]{3,2,1,0:T(8,128)} %fusion.2, f32[2,2,128,512]{3,2,1,0:T(8,128)S(1)} %collective-permute-done.6), kind=kLoop, calls=%fused_computation.5 | loop fusion | flops 262144 | bytes 3145728 | tf_op jit(solution)/shard_map/scatter-add | solution.py:237
  221.1 2.4 %fusion = f32[2,2,512,512]{3,2,1,0:T(8,128)} fusion(f32[2,2,512,512]{3,2,1,0:T(8,128)} %fusion.1, f32[2,2,128,512]{3,2,1,0:T(8,128)S(1)} %collective-permute-done.7), kind=kLoop, calls=%fused_computation.3 | loop fusion | flops 262144 | bytes 3145728 | tf_op jit(solution)/shard_map/scatter-add | solution.py:238
  (17 shorter events, 1.1 us)
Async XLA Ops:
  0.0 13.8 %copy-start = (f32[2,2,512,512]{3,2,1,0:T(8,128)S(1)}, f32[2,2,512,512]{3,2,1,0:T(8,128)}, u32[]{:S(2)}) copy-start(f32[2,2,512,512]{3,2,1,0:T(8,128)} %refs_0_.1) | copy-start | bytes 12582916
  1.9 72.4 %collective-permute-start.1 = (f32[2,2,128,512]{3,2,1,0:T(8,128)S(1)}, f32[2,2,128,512]{3,2,1,0:T(8,128)S(1)}, u32[]{:S(2)}, u32[]{:S(2)}) collective-permute-start(f32[2,2,128,512]{3,2,1,0:T(8,128)S(1)} %get-tuple-element.113), channel_id=1, source_target_pairs={{1,0},{2,1},{3,2},{4,3},{5,4},{6,5},{7,6},{9,8},{10,9},{11,10},{12... | collective-permute-start | bytes 3145736 | tf_op jit(solution)/shard_map/ppermute | solution.py:213
  4.6 70.7 %collective-permute-start = (f32[2,2,128,512]{3,2,1,0:T(8,128)S(1)}, f32[2,2,128,512]{3,2,1,0:T(8,128)S(1)}, u32[]{:S(2)}, u32[]{:S(2)}) collective-permute-start(f32[2,2,128,512]{3,2,1,0:T(8,128)S(1)} %get-tuple-element.114), channel_id=1, source_target_pairs={{0,1},{1,2},{2,3},{3,4},{4,5},{5,6},{6,7},{8,9},{9,10},{10,11},{11... | collective-permute-start | bytes 3145736 | tf_op jit(solution)/shard_map/ppermute | solution.py:213
  74.3 2.5 %copy-start.1 = (f32[2,2,128,512]{3,2,1,0:T(8,128)}, f32[2,2,128,512]{3,2,1,0:T(8,128)S(1)}, u32[]{:S(2)}) copy-start(f32[2,2,128,512]{3,2,1,0:T(8,128)S(1)} %collective-permute-done.1.refs_2_) | copy-start | bytes 3145732
  75.2 1.6 copy-start.2
  76.8 22.0 %collective-permute-start.2 = (f32[2,2,768,128]{3,2,1,0:T(8,128)}, f32[2,2,768,128]{3,2,1,0:T(8,128)}, u32[]{:S(2)}, u32[]{:S(2)}) collective-permute-start(f32[2,2,768,128]{3,2,1,0:T(8,128)} %pad_maximum_fusion), channel_id=1, source_target_pairs={{0,8},{8,16},{16,24},{24,32},{32,40},{40,48},{48,56},{56,64},{64,7... | collective-permute-start | bytes 4718600 | tf_op jit(solution)/shard_map/ppermute | solution.py:213
  78.8 4.4 %copy-start.4 = (s32[1,1,3,2]{2,3,1,0:T(2,128)S(1)}, s32[1,1,3,2]{2,3,1,0:T(2,128)}, u32[]{:S(2)}) copy-start(s32[1,1,3,2]{2,3,1,0:T(2,128)} %param.25) | copy-start | bytes 76
  78.9 21.6 %collective-permute-start.3 = (f32[2,2,768,128]{3,2,1,0:T(8,128)S(1)}, f32[2,2,768,128]{3,2,1,0:T(8,128)S(1)}, u32[]{:S(2)}, u32[]{:S(2)}) collective-permute-start(f32[2,2,768,128]{3,2,1,0:T(8,128)S(1)} %pad_maximum_fusion.1), channel_id=1, source_target_pairs={{8,0},{16,8},{24,16},{32,24},{40,32},{48,40},{56,48},{64,56},{72,6... | collective-permute-start | bytes 4718600 | tf_op jit(solution)/shard_map/ppermute | solution.py:213
  100.4 1.2 copy-start.3
  123.9 36.5 %collective-permute-start.4 = (f32[2,2,768,128]{3,2,1,0:T(8,128)}, f32[2,2,768,128]{3,2,1,0:T(8,128)S(1)}, u32[]{:S(2)}, u32[]{:S(2)}) collective-permute-start(f32[2,2,768,128]{3,2,1,0:T(8,128)} %get-tuple-element.107), channel_id=1, source_target_pairs={{8,0},{16,8},{24,16},{32,24},{40,32},{48,40},{56,48},{64,56},{72,6... | collective-permute-start | bytes 4718600 | tf_op jit(solution)/shard_map/ppermute | solution.py:213
  127.7 34.6 %collective-permute-start.5 = (f32[2,2,768,128]{3,2,1,0:T(8,128)}, f32[2,2,768,128]{3,2,1,0:T(8,128)S(1)}, u32[]{:S(2)}, u32[]{:S(2)}) collective-permute-start(f32[2,2,768,128]{3,2,1,0:T(8,128)} %get-tuple-element.108), channel_id=1, source_target_pairs={{0,8},{8,16},{16,24},{24,32},{32,40},{40,48},{48,56},{56,64},{64,7... | collective-permute-start | bytes 4718600 | tf_op jit(solution)/shard_map/ppermute | solution.py:213
  164.2 54.5 %collective-permute-start.6 = (f32[2,2,128,512]{3,2,1,0:T(8,128)}, f32[2,2,128,512]{3,2,1,0:T(8,128)S(1)}, u32[]{:S(2)}, u32[]{:S(2)}) collective-permute-start(f32[2,2,128,512]{3,2,1,0:T(8,128)} %get-tuple-element.116), channel_id=1, source_target_pairs={{1,0},{2,1},{3,2},{4,3},{5,4},{6,5},{7,6},{9,8},{10,9},{11,10},{12... | collective-permute-start | bytes 3145736 | tf_op jit(solution)/shard_map/ppermute | solution.py:213
  166.1 55.0 %collective-permute-start.7 = (f32[2,2,128,512]{3,2,1,0:T(8,128)}, f32[2,2,128,512]{3,2,1,0:T(8,128)S(1)}, u32[]{:S(2)}, u32[]{:S(2)}) collective-permute-start(f32[2,2,128,512]{3,2,1,0:T(8,128)} %get-tuple-element.115), channel_id=1, source_target_pairs={{0,1},{1,2},{2,3},{3,4},{4,5},{5,6},{6,7},{8,9},{9,10},{10,11},{11... | collective-permute-start | bytes 3145736 | tf_op jit(solution)/shard_map/ppermute | solution.py:213

commit v2 on v1

--- a/solution.py
+++ b/solution.py
@@ -59,13 +59,13 @@
 }
 
 
-def gradient_kernel(offsets, counts, *refs):
+def gradient_kernel(sample, offsets, counts, *refs):
     names = list(PLACES)
     n = len(names)
     pieces = dict(zip(names, refs[:n]))
-    probe, measurements, tables = refs[n : n + 3]
+    fixed = refs[n : n + 3]
     outs = dict(zip(names, refs[n + 3 : 2 * n + 3]))
-    obj, grad, sem = refs[2 * n + 3 :]
+    obj, grad, probe, measurements, tables, sem = refs[2 * n + 3 :]
     samples = obj.shape[0]
 
     def view(ref, name):
@@ -73,8 +73,14 @@
         return ref.at[:, :, pl.ds(r, h), pl.ds(c, w)]
 
     loads = [
-        pltpu.make_async_copy(pieces[k], view(obj, k), sem.at[i])
+        pltpu.make_async_copy(
+            pieces[k].at[pl.ds(sample, 1)] if k == "center" else pieces[k], view(obj, k), sem.at[i]
+        )
         for i, k in enumerate(names)
+    ]
+    loads += [
+        pltpu.make_async_copy(src, dst, sem.at[n + i])
+        for i, (src, dst) in enumerate(zip(fixed, (probe, measurements, tables)))
     ]
     for copy in loads:
         copy.start()
@@ -178,64 +184,189 @@
         copy.wait()
 
 
-def window_gradients(pieces, probe, measurements, offsets, counts):
-    samples = pieces["center"].shape[0]
+def window_gradients(sample, pieces, probe, measurements, offsets, counts, tables):
     names = list(PLACES)
-    shapes = [jax.ShapeDtypeStruct((samples, 2) + PLACES[k][2:], jnp.float32) for k in names]
+    shapes = [jax.ShapeDtypeStruct((1, 2) + PLACES[k][2:], jnp.float32) for k in names]
     anywhere = pl.BlockSpec(memory_space=pl.ANY)
-    inside = pl.BlockSpec(memory_space=pltpu.VMEM)
     scalars = pl.BlockSpec(memory_space=pltpu.SMEM)
     outs = pl.pallas_call(
-        gradient_kernel,
+        functools.partial(gradient_kernel, sample),
         out_shape=shapes,
-        in_specs=[scalars, scalars] + [anywhere] * len(names) + [inside] * 3,
-        out_specs=[anywhere] * len(names),
+        in_specs=[scalars, scalars] + [anywhere] * (len(names) + 3),
+        out_specs=[pl.BlockSpec(memory_space=pltpu.HBM)] + [anywhere] * (len(names) - 1),
         scratch_shapes=[
-            pltpu.VMEM((samples, 2, EXT, EXT), jnp.float32),
-            pltpu.VMEM((samples, 2, EXT, EXT), jnp.float32),
-            pltpu.SemaphoreType.DMA((len(names),)),
+            pltpu.VMEM((1, 2, EXT, EXT), jnp.float32),
+            pltpu.VMEM((1, 2, EXT, EXT), jnp.float32),
+            pltpu.VMEM((2, PROBE, PROBE), jnp.float32),
+            pltpu.VMEM((POS, PROBE, PROBE), jnp.float32),
+            pltpu.VMEM((4, 2 * PROBE, 2 * PROBE), jnp.bfloat16),
+            pltpu.SemaphoreType.DMA((len(names) + 3,)),
         ],
-        compiler_params=pltpu.CompilerParams(vmem_limit_bytes=56 * 1024 * 1024),
+        compiler_params=pltpu.CompilerParams(vmem_limit_bytes=40 * 1024 * 1024),
+        cost_estimate=pl.CostEstimate(flops=10**10, bytes_accessed=3 * 10**7, transcendentals=0),
     )(
         offsets.reshape(-1),
         counts.reshape(-1),
         *[pieces[k] for k in names],
         probe,
         measurements,
-        jnp.asarray(dft_tables()),
+        tables,
     )
     return dict(zip(names, outs))
 
 
-def shifted(x, axis, by):
+def side_kernel(center, from_left, from_right, *refs):
+    out = refs[-1]
+    out[0, 0] = center[0, 0]
+    out[0, 0, :, :BORDER] += from_left[0, 0]
+    out[0, 0, :, TILE - BORDER :] += from_right[0, 0]
+
+
+def add_sides(sample, center, from_left, from_right, into=None):
+    part = BORDER
+
+    def block(width, first):
+        return pl.BlockSpec((1, 1, part, width), lambda k, i: (0, k, i + first, 0))
+
+    args = [center, from_left, from_right]
+    specs = [block(TILE, 0), block(BORDER, 1), block(BORDER, 1)]
+    aliases = {}
+    if into is not None:
+        aliases = {len(args): 0}
+        args.append(into)
+        specs.append(pl.BlockSpec(memory_space=pl.ANY))
+    return pl.pallas_call(
+        side_kernel,
+        out_shape=jax.ShapeDtypeStruct((SAMPLES, 2, TILE, TILE), jnp.float32),
+        grid=(2, TILE // part),
+        in_specs=specs,
+        out_specs=pl.BlockSpec((1, 1, part, TILE), lambda k, i: (sample, k, i, 0)),
+        input_output_aliases=aliases,
+        cost_estimate=pl.CostEstimate(flops=10**6, bytes_accessed=6 * 10**6, transcendentals=0),
+    )(*args)
+
+
+def edge_kernel(place, above0, below0, crossed0, above1, below1, held, out, band, got, sem):
+    row, last = place[0], place[1]
+    far = TILE - BORDER
+    loads = []
+    for s in range(SAMPLES):
+        for e, first in enumerate((0, far)):
+            loads.append((out.at[s, :, pl.ds(first, BORDER)], band.at[s, e]))
+    strips = (above0.at[0], below0.at[0], above1.at[0], below1.at[0], crossed0.at[0])
+    loads += [(src, got.at[i]) for i, src in enumerate(strips)]
+    loads = [pltpu.make_async_copy(a, b, sem.at[i]) for i, (a, b) in enumerate(loads)]
+    for copy in loads:
+        copy.start()
+    for copy in loads:
+        copy.wait()
+    band[0, 0] += jnp.where(row == TURN, got[4], jnp.where(row == 0, 0.0, got[0]))
+    band[0, 1] += jnp.where(row == TURN - 1, got[4], jnp.where(row == last, 0.0, got[1]))
+    band[1, 0] += got[2]
+    band[1, 1] += got[3]
+    stores = []
+    for s in range(SAMPLES):
+        for e, first in enumerate((0, far)):
+            i = len(stores)
+            stores.append(
+                pltpu.make_async_copy(band.at[s, e], out.at[s, :, pl.ds(first, BORDER)], sem.at[i])
+            )
+    for copy in stores:
+        copy.start()
+    for copy in stores:
+        copy.wait()
+
+
+def add_edges(place, out, above0, below0, crossed0, above1, below1):
+    anywhere = pl.BlockSpec(memory_space=pl.ANY)
+    return pl.pallas_call(
+        edge_kernel,
+        out_shape=jax.ShapeDtypeStruct(out.shape, out.dtype),
+        in_specs=[pl.BlockSpec(memory_space=pltpu.SMEM)] + [anywhere] * 6,
+        out_specs=anywhere,
+        scratch_shapes=[
+            pltpu.VMEM((SAMPLES, 2, 2, BORDER, TILE), jnp.float32),
+            pltpu.VMEM((5, 2, BORDER, TILE), jnp.float32),
+            pltpu.SemaphoreType.DMA((9,)),
+        ],
+        input_output_aliases={6: 0},
+        cost_estimate=pl.CostEstimate(flops=10**6, bytes_accessed=6 * 10**6, transcendentals=0),
+    )(place, above0, below0, crossed0, above1, below1, out)
+
+
+TURN = 4
+
+
+def moved(x, axis, pairs):
+    return lax.ppermute(x, axis, pairs)
+
+
+def steps(axis, by):
     count = lax.axis_size(axis)
-    pairs = [(i, i + by) for i in range(count) if 0 <= i + by < count]
-    return lax.ppermute(x, axis, pairs)
+    return [(i, i + by) for i in range(count) if 0 <= i + by < count]
+
+
+def detours():
+    last = lax.axis_size("row") - 1
+    down = [p for p in steps("row", 1) if p != (TURN - 1, TURN)] + [(TURN - 1, 0)]
+    up = [p for p in steps("row", -1) if p != (TURN, TURN - 1)] + [(TURN, last)]
+    return down, up, [(0, TURN), (last, TURN - 1)]
 
 
 def body(objects, probe, measurements, offsets, counts):
-    top = shifted(objects[:, :, TILE - BORDER :, :], "row", 1)
-    bottom = shifted(objects[:, :, :BORDER, :], "row", -1)
-
-    def column(lo):
-        return jnp.concatenate([x[..., lo : lo + BORDER] for x in (top, objects, bottom)], axis=2)
-
-    left = shifted(column(TILE - BORDER), "col", 1)
-    right = shifted(column(0), "col", -1)
-    pieces = dict(center=objects, top=top, bottom=bottom, left=left, right=right)
-    g = window_gradients(pieces, probe, measurements[0, 0], offsets, counts)
-    from_right = shifted(g["left"], "col", -1)
-    from_left = shifted(g["right"], "col", 1)
-
-    def folded(x, lo, hi):
-        x = x.at[..., TILE - BORDER :].add(from_right[:, :, lo:hi])
-        return x.at[..., :BORDER].add(from_left[:, :, lo:hi])
-
-    from_below = shifted(folded(g["top"], 0, BORDER), "row", -1)
-    from_above = shifted(folded(g["bottom"], BORDER + TILE, EXT), "row", 1)
-    result = folded(g["center"], BORDER, BORDER + TILE)
-    result = result.at[:, :, TILE - BORDER :].add(from_below)
-    return result.at[:, :, :BORDER].add(from_above)
+    row = lax.axis_index("row")
+    rows = lax.axis_size("row")
+    last = rows - 1
+    place = jnp.stack([row, jnp.int32(last)]).astype(jnp.int32)
+    down, up, over = detours()
+    tables = jnp.asarray(dft_tables())
+    args = (probe, measurements[0, 0], offsets, counts, tables)
+
+    low, high = objects[:, :, TILE - BORDER :], objects[:, :, :BORDER]
+    top1 = moved(low[1:], "row", down)
+    bottom1 = moved(high[1:], "row", up)
+    top0 = moved(low[:1], "row", steps("row", 1))
+    bottom0 = moved(high[:1], "row", steps("row", -1))
+    crossed1 = moved(jnp.where(row == 0, top1, bottom1), "row", over)
+    top1 = jnp.where(row == TURN, crossed1, jnp.where(row == 0, 0.0, top1))
+    bottom1 = jnp.where(row == TURN - 1, crossed1, jnp.where(row == last, 0.0, bottom1))
+
+    def sides(s, top, bottom):
+        def column(lo):
+            return jnp.concatenate(
+                [x[..., lo : lo + BORDER] for x in (top, objects[s : s + 1], bottom)], axis=2
+            )
+
+        left = moved(column(TILE - BORDER), "col", steps("col", 1))
+        right = moved(column(0), "col", steps("col", -1))
+        return dict(center=objects, top=top, bottom=bottom, left=left, right=right)
+
+    pieces0, pieces1 = lax.optimization_barrier(
+        (sides(0, top0, bottom0), sides(1, top1, bottom1))
+    )
+    g0 = window_gradients(0, pieces0, *args)
+    g1 = window_gradients(1, pieces1, *args)
+
+    def fold(g):
+        from_right = moved(g["left"], "col", steps("col", -1))
+        from_left = moved(g["right"], "col", steps("col", 1))
+
+        def folded(x, lo):
+            x = x.at[..., TILE - BORDER :].add(from_right[:, :, lo : lo + BORDER])
+            return x.at[..., :BORDER].add(from_left[:, :, lo : lo + BORDER])
+
+        return from_left, from_right, folded(g["top"], 0), folded(g["bottom"], BORDER + TILE)
+
+    left0, right0, first0, final0 = fold(g0)
+    above0 = moved(final0, "row", down)
+    below0 = moved(first0, "row", up)
+    crossed0 = moved(jnp.where(row == 0, above0, below0), "row", over)
+    left1, right1, first1, final1 = fold(g1)
+    above1 = moved(final1, "row", steps("row", 1))
+    below1 = moved(first1, "row", steps("row", -1))
+    out = add_sides(0, g0["center"], left0, right0)
+    out = add_sides(1, g1["center"], left1, right1, into=out)
+    return add_edges(place, out, above0, below0, crossed0, above1, below1)
 
 
 def solution(mesh):

time: 225 us -> 191 us (0.85)
  the two profiles are of different devices: /device:TPU:60 before, /device:TPU:61 now
where the time goes in v2:
time: 191 us; the launch traced here: 189 us
  starting transfers between devices  75.7 us (40%)
  waiting for transfers between devices  61 us (32%)
  Pallas kernels  35.7 us (19%)
  local copies, waits for them, and re-layouts  8.79 us (5%)
  other arithmetic  7.15 us (4%)
    ppermute x18, starting transfers between devices, moved(): return lax.ppermute(x, axis, pairs)  75.7 us
    ppermute x18, waiting for transfers between devices, moved(): return lax.ppermute(x, axis, pairs)  61 us
    pallas_call x2, Pallas kernels, window_gradients(): pl.pallas_call(functools.partial(gradient_kernel, sample), out_shape=shap...  19.3 us
    pallas_call x2, Pallas kernels, add_sides(): pl.pallas_call(side_kernel, out_shape=jax.ShapeDtypeStruct((SAMPLES, 2, T...  11.7 us
    pallas_call x1, Pallas kernels, add_edges(): pl.pallas_call(edge_kernel, out_shape=jax.ShapeDtypeStruct(out.shape, out...  4.59 us
    unnamed x39, local copies, waits for them, and re-layouts  4.42 us
    concatenate x4, other arithmetic, column(): jnp.concatenate([x[..., lo:lo + BORDER] for x in (top, objects[s:s + 1],...  3.83 us
  transfers between devices with their start and end apart: 18, of which 11 were waited for; matrix products, arithmetic and copies ran while one was open for 5% of the time, Pallas kernels for 11%

profile of v2, /device:TPU:61, one launch (start us, length us, event | category | flops | bytes accessed | tf_op | source)
XLA Modules:
  0.0 189.5 jit_solution(17546009821547026280)
XLA Ops:
  0.0 3.1 %fusion.9 = (f32[1,2,128,512]{3,2,1,0:T(8,128)}, f32[1,2,128,512]{3,2,1,0:T(8,128)}, f32[1,2,128,512]{3,2,1,0:T(8,128)}, f32[1,2,128,512]{3,2,1,0:T(8,128)}) fusion(f32[2,2,512,512]{3,2,1,0:T(8,128)} %refs_0_.1), kind=kLoop, calls=%fused_computation.26 | loop fusion | bytes 4194304 | tf_op jit(solution)/shard_map/slice | solution.py:327
  3.1 2.4 %collective-permute-start.5 = (f32[1,2,128,512]{3,2,1,0:T(8,128)}, f32[1,2,128,512]{3,2,1,0:T(8,128)S(1)}, u32[]{:S(2)}, u32[]{:S(2)}) collective-permute-start(f32[1,2,128,512]{3,2,1,0:T(8,128)} %get-tuple-element.145), channel_id=1, source_target_pairs={{1,0},{2,1},{3,2},{5,4},{6,5},{7,6},{4,7},{9,8},{10,9},{11,10},{13... | collective-permute-start | bytes 1572872 | tf_op jit(solution)/shard_map/ppermute | solution.py:301
  7.4 9.2 %collective-permute-start.1 = (f32[1,2,128,512]{3,2,1,0:T(8,128)}, f32[1,2,128,512]{3,2,1,0:T(8,128)S(1)}, u32[]{:S(2)}, u32[]{:S(2)}) collective-permute-start(f32[1,2,128,512]{3,2,1,0:T(8,128)} %get-tuple-element.147), channel_id=1, source_target_pairs={{0,1},{1,2},{2,3},{3,4},{4,5},{5,6},{6,7},{8,9},{9,10},{10,11},{11... | collective-permute-start | bytes 1572872 | tf_op jit(solution)/shard_map/ppermute | solution.py:301
  21.6 17.3 %collective-permute-done.1.refs_1_ = f32[1,2,128,512]{3,2,1,0:T(8,128)S(1)} collective-permute-done((f32[1,2,128,512]{3,2,1,0:T(8,128)}, f32[1,2,128,512]{3,2,1,0:T(8,128)S(1)}, u32[]{:S(2)}, u32[]{:S(2)}) %collective-permute-start.1) | collective-permute-done | bytes 524320 | tf_op jit(solution)/shard_map/ppermute | solution.py:301
  38.9 10.4 %collective-permute-done.refs_2_ = f32[1,2,128,512]{3,2,1,0:T(8,128)S(1)} collective-permute-done((f32[1,2,128,512]{3,2,1,0:T(8,128)}, f32[1,2,128,512]{3,2,1,0:T(8,128)S(1)}, u32[]{:S(2)}, u32[]{:S(2)}) %collective-permute-start) | collective-permute-done | bytes 524320 | tf_op jit(solution)/shard_map/ppermute | solution.py:301
  50.3 3.7 %collective-permute-start.2 = (f32[1,2,768,128]{3,2,1,0:T(8,128)}, f32[1,2,768,128]{3,2,1,0:T(8,128)}, u32[]{:S(2)}, u32[]{:S(2)}) collective-permute-start(f32[1,2,768,128]{3,2,1,0:T(8,128)} %pad_maximum_fusion), channel_id=1, source_target_pairs={{0,8},{8,16},{16,24},{24,32},{32,40},{40,48},{48,56},{56,64},{64,7... | collective-permute-start | bytes 2359304 | tf_op jit(solution)/shard_map/ppermute | solution.py:301
  55.0 2.0 %collective-permute-start.3 = (f32[1,2,768,128]{3,2,1,0:T(8,128)}, f32[1,2,768,128]{3,2,1,0:T(8,128)}, u32[]{:S(2)}, u32[]{:S(2)}) collective-permute-start(f32[1,2,768,128]{3,2,1,0:T(8,128)} %pad_maximum_fusion.1), channel_id=1, source_target_pairs={{8,0},{16,8},{24,16},{32,24},{40,32},{48,40},{56,48},{64,56},{72,6... | collective-permute-start | bytes 2359304 | tf_op jit(solution)/shard_map/ppermute | solution.py:301
  59.4 3.6 %collective-permute-start.7 = (f32[1,2,768,128]{3,2,1,0:T(8,128)}, f32[1,2,768,128]{3,2,1,0:T(8,128)}, u32[]{:S(2)}, u32[]{:S(2)}) collective-permute-start(f32[1,2,768,128]{3,2,1,0:T(8,128)} %pad_maximum_fusion.2), channel_id=1, source_target_pairs={{0,8},{8,16},{16,24},{24,32},{32,40},{40,48},{48,56},{56,64},{64,7... | collective-permute-start | bytes 2359304 | tf_op jit(solution)/shard_map/ppermute | solution.py:301
  66.7 3.2 %collective-permute-done.2.refs_3_ = f32[1,2,768,128]{3,2,1,0:T(8,128)} collective-permute-done((f32[1,2,768,128]{3,2,1,0:T(8,128)}, f32[1,2,768,128]{3,2,1,0:T(8,128)}, u32[]{:S(2)}, u32[]{:S(2)}) %collective-permute-start.2) | collective-permute-done | bytes 786464 | tf_op jit(solution)/shard_map/ppermute | solution.py:301
  69.9 4.3 %collective-permute-done.3.refs_4_ = f32[1,2,768,128]{3,2,1,0:T(8,128)} collective-permute-done((f32[1,2,768,128]{3,2,1,0:T(8,128)}, f32[1,2,768,128]{3,2,1,0:T(8,128)}, u32[]{:S(2)}, u32[]{:S(2)}) %collective-permute-start.3) | collective-permute-done | bytes 786464 | tf_op jit(solution)/shard_map/ppermute | solution.py:301
  74.2 11.4 %collective-permute-done.7.refs_3_ = f32[1,2,768,128]{3,2,1,0:T(8,128)} collective-permute-done((f32[1,2,768,128]{3,2,1,0:T(8,128)}, f32[1,2,768,128]{3,2,1,0:T(8,128)}, u32[]{:S(2)}, u32[]{:S(2)}) %collective-permute-start.7) | collective-permute-done | bytes 786464 | tf_op jit(solution)/shard_map/ppermute | solution.py:301
  87.3 9.7 %shard_map.64 = (f32[1,2,512,512]{3,2,1,0:T(8,128)S(1)}, f32[1,2,128,512]{3,2,1,0:T(8,128)S(1)}, f32[1,2,128,512]{3,2,1,0:T(8,128)S(1)}, f32[1,2,768,128]{3,2,1,0:T(8,128)S(1)}, f32[1,2,768,128]{3,2,1,0:T(8,128)S(1)}) custom-call(s32[6]{0:T(128)S(1)} %reshape.276.offsets, s32[1]{0:T(128)} %bitcast.3.counts, f32[2,2,512,512]{3,2,1,0:T(8,128)} %refs_0_.1, ...), custom_call_target="tpu_custom_call" | custom-call | flops 10000000000 | bytes 30000000 | tf_op jit(solution)/shard_map/pallas_call | solution.py:192
  100.3 7.5 %collective-permute-start.10 = (f32[1,2,768,128]{3,2,1,0:T(8,128)S(1)}, f32[1,2,768,128]{3,2,1,0:T(8,128)S(1)}, u32[]{:S(2)}, u32[]{:S(2)}) collective-permute-start(f32[1,2,768,128]{3,2,1,0:T(8,128)S(1)} %get-tuple-element.128), channel_id=1, source_target_pairs={{0,8},{8,16},{16,24},{24,32},{32,40},{40,48},{48,56},{56,64},{64,7... | collective-permute-start | bytes 2359304 | tf_op jit(solution)/shard_map/ppermute | solution.py:301
  107.9 9.6 %shard_map.65 = (f32[1,2,512,512]{3,2,1,0:T(8,128)S(1)}, f32[1,2,128,512]{3,2,1,0:T(8,128)S(1)}, f32[1,2,128,512]{3,2,1,0:T(8,128)S(1)}, f32[1,2,768,128]{3,2,1,0:T(8,128)S(1)}, f32[1,2,768,128]{3,2,1,0:T(8,128)S(1)}) custom-call(s32[6]{0:T(128)S(1)} %reshape.276.offsets, s32[1]{0:T(128)} %bitcast.4.counts, f32[2,2,512,512]{3,2,1,0:T(8,128)} %refs_0_.1, ...), custom_call_target="tpu_custom_call" | custom-call | flops 10000000000 | bytes 30000000 | tf_op jit(solution)/shard_map/pallas_call | solution.py:192
  120.7 5.7 %collective-permute-start.15 = (f32[1,2,768,128]{3,2,1,0:T(8,128)S(1)}, f32[1,2,768,128]{3,2,1,0:T(8,128)S(1)}, u32[]{:S(2)}, u32[]{:S(2)}) collective-permute-start(f32[1,2,768,128]{3,2,1,0:T(8,128)S(1)} %get-tuple-element.137), channel_id=1, source_target_pairs={{0,8},{8,16},{16,24},{24,32},{32,40},{40,48},{48,56},{56,64},{64,7... | collective-permute-start | bytes 2359304 | tf_op jit(solution)/shard_map/ppermute | solution.py:301
  127.9 3.9 %collective-permute-start.11 = (f32[1,2,128,512]{3,2,1,0:T(8,128)S(1)}, f32[1,2,128,512]{3,2,1,0:T(8,128)S(1)}, u32[]{:S(2)}, u32[]{:S(2)}) collective-permute-start(f32[1,2,128,512]{3,2,1,0:T(8,128)S(1)} %get-tuple-element.154), channel_id=1, source_target_pairs={{0,1},{1,2},{2,3},{4,5},{5,6},{6,7},{3,0},{8,9},{9,10},{10,11},{12... | collective-permute-start | bytes 1572872 | tf_op jit(solution)/shard_map/ppermute | solution.py:301
  131.8 2.7 %collective-permute-done.14.from_right = f32[1,2,768,128]{3,2,1,0:T(8,128)S(1)} collective-permute-done((f32[1,2,768,128]{3,2,1,0:T(8,128)S(1)}, f32[1,2,768,128]{3,2,1,0:T(8,128)S(1)}, u32[]{:S(2)}, u32[]{:S(2)}) %collective-permute-start.14) | collective-permute-done | bytes 786464 | tf_op jit(solution)/shard_map/ppermute | solution.py:301
  134.5 4.5 %collective-permute-done.15.from_left = f32[1,2,768,128]{3,2,1,0:T(8,128)S(1)} collective-permute-done((f32[1,2,768,128]{3,2,1,0:T(8,128)S(1)}, f32[1,2,768,128]{3,2,1,0:T(8,128)S(1)}, u32[]{:S(2)}, u32[]{:S(2)}) %collective-permute-start.15) | collective-permute-done | bytes 786464 | tf_op jit(solution)/shard_map/ppermute | solution.py:301
  141.0 22.3 %collective-permute-start.16 = (f32[1,2,128,512]{3,2,1,0:T(8,128)S(1)}, f32[1,2,128,512]{3,2,1,0:T(8,128)}, u32[]{:S(2)}, u32[]{:S(2)}) collective-permute-start(f32[1,2,128,512]{3,2,1,0:T(8,128)S(1)} %get-tuple-element.150), channel_id=1, source_target_pairs={{0,1},{1,2},{2,3},{3,4},{4,5},{5,6},{6,7},{8,9},{9,10},{10,11},{11... | collective-permute-start | bytes 1572872 | tf_op jit(solution)/shard_map/ppermute | solution.py:301
  166.2 5.9 %shard_map.66.refs_0_ = f32[2,2,512,512]{3,2,1,0:T(8,128)} custom-call(f32[1,2,512,512]{3,2,1,0:T(8,128)} %copy-done, f32[1,2,768,128]{3,2,1,0:T(8,128)} %copy-done.16, f32[1,2,768,128]{3,2,1,0:T(8,128)} %copy-done.15), custom_call_target="tpu_custom_call" | custom-call | flops 1000000 | bytes 6000000 | tf_op jit(solution)/shard_map/pallas_call | solution.py:238
  172.1 5.9 %shard_map.67.held = f32[2,2,512,512]{3,2,1,0:T(8,128)} custom-call(f32[1,2,512,512]{3,2,1,0:T(8,128)} %copy-done.1, f32[1,2,768,128]{3,2,1,0:T(8,128)} %copy-done.14, f32[1,2,768,128]{3,2,1,0:T(8,128)} %copy-done.13, f32[2,2,512,512]{3,2,1,0:T(8,128)} %shard_map.66.refs_0_), custom_call_target="tpu_custom_call", output_to_operand_aliasing={{}: (3, {})} | custom-call | flops 1000000 | bytes 6000000 | tf_op jit(solution)/shard_map/pallas_call | solution.py:238
  178.0 2.0 %collective-permute-done.16.above1 = f32[1,2,128,512]{3,2,1,0:T(8,128)} collective-permute-done((f32[1,2,128,512]{3,2,1,0:T(8,128)S(1)}, f32[1,2,128,512]{3,2,1,0:T(8,128)}, u32[]{:S(2)}, u32[]{:S(2)}) %collective-permute-start.16) | collective-permute-done | bytes 524320 | tf_op jit(solution)/shard_map/ppermute | solution.py:301
  180.0 4.9 %collective-permute-done.13.crossed0 = f32[1,2,128,512]{3,2,1,0:T(8,128)} collective-permute-done((f32[1,2,128,512]{3,2,1,0:T(8,128)}, f32[1,2,128,512]{3,2,1,0:T(8,128)}, u32[]{:S(2)}, u32[]{:S(2)}) %collective-permute-start.13) | collective-permute-done | bytes 524320 | tf_op jit(solution)/shard_map/ppermute | solution.py:301
  184.9 4.6 %shard_map.68 = f32[2,2,512,512]{3,2,1,0:T(8,128)} custom-call(s32[2]{0:T(128)} %pad_add_fusion.place, f32[1,2,128,512]{3,2,1,0:T(8,128)} %copy-done.8, f32[1,2,128,512]{3,2,1,0:T(8,128)} %copy-done.7, f32[1,2,128,512]{3,2,1,0:T(8,128)} %collective-permute-done.13.crossed0, ...), custom_call_target="tpu_custom_call", output_to_operand_aliasing={{}: (6, {})} | custom-call | flops 1000000 | bytes 6000000 | tf_op jit(solution)/shard_map/pallas_call | solution.py:282
  (74 shorter events, 28.9 us)
Async XLA Ops:
  3.1 16.7 %collective-permute-start.5 = (f32[1,2,128,512]{3,2,1,0:T(8,128)}, f32[1,2,128,512]{3,2,1,0:T(8,128)S(1)}, u32[]{:S(2)}, u32[]{:S(2)}) collective-permute-start(f32[1,2,128,512]{3,2,1,0:T(8,128)} %get-tuple-element.145), channel_id=1, source_target_pairs={{1,0},{2,1},{3,2},{5,4},{6,5},{7,6},{4,7},{9,8},{10,9},{11,10},{13... | collective-permute-start | bytes 1572872 | tf_op jit(solution)/shard_map/ppermute | solution.py:301
  5.5 14.6 %collective-permute-start.4 = (f32[1,2,128,512]{3,2,1,0:T(8,128)}, f32[1,2,128,512]{3,2,1,0:T(8,128)S(1)}, u32[]{:S(2)}, u32[]{:S(2)}) collective-permute-start(f32[1,2,128,512]{3,2,1,0:T(8,128)} %get-tuple-element.146), channel_id=1, source_target_pairs={{0,1},{1,2},{2,3},{4,5},{5,6},{6,7},{3,0},{8,9},{9,10},{10,11},{12... | collective-permute-start | bytes 1572872 | tf_op jit(solution)/shard_map/ppermute | solution.py:301
  7.4 31.5 %collective-permute-start.1 = (f32[1,2,128,512]{3,2,1,0:T(8,128)}, f32[1,2,128,512]{3,2,1,0:T(8,128)S(1)}, u32[]{:S(2)}, u32[]{:S(2)}) collective-permute-start(f32[1,2,128,512]{3,2,1,0:T(8,128)} %get-tuple-element.147), channel_id=1, source_target_pairs={{0,1},{1,2},{2,3},{3,4},{4,5},{5,6},{6,7},{8,9},{9,10},{10,11},{11... | collective-permute-start | bytes 1572872 | tf_op jit(solution)/shard_map/ppermute | solution.py:301
  16.6 32.7 %collective-permute-start = (f32[1,2,128,512]{3,2,1,0:T(8,128)}, f32[1,2,128,512]{3,2,1,0:T(8,128)S(1)}, u32[]{:S(2)}, u32[]{:S(2)}) collective-permute-start(f32[1,2,128,512]{3,2,1,0:T(8,128)} %get-tuple-element.148), channel_id=1, source_target_pairs={{1,0},{2,1},{3,2},{4,3},{5,4},{6,5},{7,6},{9,8},{10,9},{11,10},{12... | collective-permute-start | bytes 1572872 | tf_op jit(solution)/shard_map/ppermute | solution.py:301
  19.7 34.2 %copy-start.9 = (f32[1,2,128,512]{3,2,1,0:T(8,128)}, f32[1,2,128,512]{3,2,1,0:T(8,128)S(1)}, u32[]{:S(2)}) copy-start(f32[1,2,128,512]{3,2,1,0:T(8,128)S(1)} %collective-permute-done.5) | copy-start | bytes 1572868
  20.0 33.9 %copy-start.10 = (f32[1,2,128,512]{3,2,1,0:T(8,128)}, f32[1,2,128,512]{3,2,1,0:T(8,128)S(1)}, u32[]{:S(2)}) copy-start(f32[1,2,128,512]{3,2,1,0:T(8,128)S(1)} %collective-permute-done.4) | copy-start | bytes 1572868
  20.1 38.3 %copy-start.12 = (f32[1,2,512,128]{3,2,1,0:T(8,128)S(1)}, f32[1,2,512,128]{3,2,1,0:T(8,128)}, u32[]{:S(2)}) copy-start(f32[1,2,512,128]{3,2,1,0:T(8,128)} %get-tuple-element.142) | copy-start | bytes 1572868
  20.1 36.8 %collective-permute-start.6 = (f32[1,2,128,512]{3,2,1,0:T(8,128)S(1)}, f32[1,2,128,512]{3,2,1,0:T(8,128)S(1)}, u32[]{:S(2)}, u32[]{:S(2)}) collective-permute-start(f32[1,2,128,512]{3,2,1,0:T(8,128)S(1)} %broadcast_select_fusion.1), channel_id=1, source_target_pairs={{0,4},{7,3},{8,12},{15,11},{16,20},{23,19},{24,28},{31,27},{32,36}... | collective-permute-start | bytes 1572872 | tf_op jit(solution)/shard_map/ppermute | solution.py:301
  50.3 19.7 %collective-permute-start.2 = (f32[1,2,768,128]{3,2,1,0:T(8,128)}, f32[1,2,768,128]{3,2,1,0:T(8,128)}, u32[]{:S(2)}, u32[]{:S(2)}) collective-permute-start(f32[1,2,768,128]{3,2,1,0:T(8,128)} %pad_maximum_fusion), channel_id=1, source_target_pairs={{0,8},{8,16},{16,24},{24,32},{32,40},{40,48},{48,56},{56,64},{64,7... | collective-permute-start | bytes 2359304 | tf_op jit(solution)/shard_map/ppermute | solution.py:301
  55.0 19.3 %collective-permute-start.3 = (f32[1,2,768,128]{3,2,1,0:T(8,128)}, f32[1,2,768,128]{3,2,1,0:T(8,128)}, u32[]{:S(2)}, u32[]{:S(2)}) collective-permute-start(f32[1,2,768,128]{3,2,1,0:T(8,128)} %pad_maximum_fusion.1), channel_id=1, source_target_pairs={{8,0},{16,8},{24,16},{32,24},{40,32},{48,40},{56,48},{64,56},{72,6... | collective-permute-start | bytes 2359304 | tf_op jit(solution)/shard_map/ppermute | solution.py:301
  59.4 26.3 %collective-permute-start.7 = (f32[1,2,768,128]{3,2,1,0:T(8,128)}, f32[1,2,768,128]{3,2,1,0:T(8,128)}, u32[]{:S(2)}, u32[]{:S(2)}) collective-permute-start(f32[1,2,768,128]{3,2,1,0:T(8,128)} %pad_maximum_fusion.2), channel_id=1, source_target_pairs={{0,8},{8,16},{16,24},{24,32},{32,40},{40,48},{48,56},{56,64},{64,7... | collective-permute-start | bytes 2359304 | tf_op jit(solution)/shard_map/ppermute | solution.py:301
  63.9 21.8 %collective-permute-start.8 = (f32[1,2,768,128]{3,2,1,0:T(8,128)}, f32[1,2,768,128]{3,2,1,0:T(8,128)}, u32[]{:S(2)}, u32[]{:S(2)}) collective-permute-start(f32[1,2,768,128]{3,2,1,0:T(8,128)} %pad_maximum_fusion.3), channel_id=1, source_target_pairs={{8,0},{16,8},{24,16},{32,24},{40,32},{48,40},{56,48},{64,56},{72,6... | collective-permute-start | bytes 2359304 | tf_op jit(solution)/shard_map/ppermute | solution.py:301
  98.4 28.0 %collective-permute-start.9 = (f32[1,2,768,128]{3,2,1,0:T(8,128)S(1)}, f32[1,2,768,128]{3,2,1,0:T(8,128)S(1)}, u32[]{:S(2)}, u32[]{:S(2)}) collective-permute-start(f32[1,2,768,128]{3,2,1,0:T(8,128)S(1)} %get-tuple-element.127), channel_id=1, source_target_pairs={{8,0},{16,8},{24,16},{32,24},{40,32},{48,40},{56,48},{64,56},{72,6... | collective-permute-start | bytes 2359304 | tf_op jit(solution)/shard_map/ppermute | solution.py:301
  100.3 26.2 %collective-permute-start.10 = (f32[1,2,768,128]{3,2,1,0:T(8,128)S(1)}, f32[1,2,768,128]{3,2,1,0:T(8,128)S(1)}, u32[]{:S(2)}, u32[]{:S(2)}) collective-permute-start(f32[1,2,768,128]{3,2,1,0:T(8,128)S(1)} %get-tuple-element.128), channel_id=1, source_target_pairs={{0,8},{8,16},{16,24},{24,32},{32,40},{40,48},{48,56},{56,64},{64,7... | collective-permute-start | bytes 2359304 | tf_op jit(solution)/shard_map/ppermute | solution.py:301
  118.8 15.6 %collective-permute-start.14 = (f32[1,2,768,128]{3,2,1,0:T(8,128)S(1)}, f32[1,2,768,128]{3,2,1,0:T(8,128)S(1)}, u32[]{:S(2)}, u32[]{:S(2)}) collective-permute-start(f32[1,2,768,128]{3,2,1,0:T(8,128)S(1)} %get-tuple-element.136), channel_id=1, source_target_pairs={{8,0},{16,8},{24,16},{32,24},{40,32},{48,40},{56,48},{64,56},{72,6... | collective-permute-start | bytes 2359304 | tf_op jit(solution)/shard_map/ppermute | solution.py:301
  120.7 18.2 %collective-permute-start.15 = (f32[1,2,768,128]{3,2,1,0:T(8,128)S(1)}, f32[1,2,768,128]{3,2,1,0:T(8,128)S(1)}, u32[]{:S(2)}, u32[]{:S(2)}) collective-permute-start(f32[1,2,768,128]{3,2,1,0:T(8,128)S(1)} %get-tuple-element.137), channel_id=1, source_target_pairs={{0,8},{8,16},{16,24},{24,32},{32,40},{40,48},{48,56},{56,64},{64,7... | collective-permute-start | bytes 2359304 | tf_op jit(solution)/shard_map/ppermute | solution.py:301
  126.4 37.9 %copy-start.15 = (f32[1,2,768,128]{3,2,1,0:T(8,128)}, f32[1,2,768,128]{3,2,1,0:T(8,128)S(1)}, u32[]{:S(2)}) copy-start(f32[1,2,768,128]{3,2,1,0:T(8,128)S(1)} %collective-permute-done.9.from_right) | copy-start | bytes 2359300
  126.5 39.1 %copy-start.16 = (f32[1,2,768,128]{3,2,1,0:T(8,128)}, f32[1,2,768,128]{3,2,1,0:T(8,128)S(1)}, u32[]{:S(2)}) copy-start(f32[1,2,768,128]{3,2,1,0:T(8,128)S(1)} %collective-permute-done.10.from_left) | copy-start | bytes 2359300
  126.6 36.7 %collective-permute-start.12 = (f32[1,2,128,512]{3,2,1,0:T(8,128)S(1)}, f32[1,2,128,512]{3,2,1,0:T(8,128)S(1)}, u32[]{:S(2)}, u32[]{:S(2)}) collective-permute-start(f32[1,2,128,512]{3,2,1,0:T(8,128)S(1)} %get-tuple-element.153), channel_id=1, source_target_pairs={{1,0},{2,1},{3,2},{5,4},{6,5},{7,6},{4,7},{9,8},{10,9},{11,10},{13... | collective-permute-start | bytes 1572872 | tf_op jit(solution)/shard_map/ppermute | solution.py:301
  127.9 35.3 %collective-permute-start.11 = (f32[1,2,128,512]{3,2,1,0:T(8,128)S(1)}, f32[1,2,128,512]{3,2,1,0:T(8,128)S(1)}, u32[]{:S(2)}, u32[]{:S(2)}) collective-permute-start(f32[1,2,128,512]{3,2,1,0:T(8,128)S(1)} %get-tuple-element.154), channel_id=1, source_target_pairs={{0,1},{1,2},{2,3},{4,5},{5,6},{6,7},{3,0},{8,9},{9,10},{10,11},{12... | collective-permute-start | bytes 1572872 | tf_op jit(solution)/shard_map/ppermute | solution.py:301
  134.5 37.7 %copy-start.13 = (f32[1,2,768,128]{3,2,1,0:T(8,128)}, f32[1,2,768,128]{3,2,1,0:T(8,128)S(1)}, u32[]{:S(2)}) copy-start(f32[1,2,768,128]{3,2,1,0:T(8,128)S(1)} %collective-permute-done.14.from_right) | copy-start | bytes 2359300
  139.0 39.0 %collective-permute-start.17 = (f32[1,2,128,512]{3,2,1,0:T(8,128)S(1)}, f32[1,2,128,512]{3,2,1,0:T(8,128)S(1)}, u32[]{:S(2)}, u32[]{:S(2)}) collective-permute-start(f32[1,2,128,512]{3,2,1,0:T(8,128)S(1)} %get-tuple-element.149), channel_id=1, source_target_pairs={{1,0},{2,1},{3,2},{4,3},{5,4},{6,5},{7,6},{9,8},{10,9},{11,10},{12... | collective-permute-start | bytes 1572872 | tf_op jit(solution)/shard_map/ppermute | solution.py:301
  141.0 39.0 %collective-permute-start.16 = (f32[1,2,128,512]{3,2,1,0:T(8,128)S(1)}, f32[1,2,128,512]{3,2,1,0:T(8,128)}, u32[]{:S(2)}, u32[]{:S(2)}) collective-permute-start(f32[1,2,128,512]{3,2,1,0:T(8,128)S(1)} %get-tuple-element.150), channel_id=1, source_target_pairs={{0,1},{1,2},{2,3},{3,4},{4,5},{5,6},{6,7},{8,9},{9,10},{10,11},{11... | collective-permute-start | bytes 1572872 | tf_op jit(solution)/shard_map/ppermute | solution.py:301
  164.3 20.6 %collective-permute-start.13 = (f32[1,2,128,512]{3,2,1,0:T(8,128)}, f32[1,2,128,512]{3,2,1,0:T(8,128)}, u32[]{:S(2)}, u32[]{:S(2)}) collective-permute-start(f32[1,2,128,512]{3,2,1,0:T(8,128)} %broadcast_select_fusion), channel_id=1, source_target_pairs={{0,4},{7,3},{8,12},{15,11},{16,20},{23,19},{24,28},{31,27},{32,36}... | collective-permute-start | bytes 1572872 | tf_op jit(solution)/shard_map/ppermute | solution.py:301
  (13 other events, 181.9 us)

commit v3 on v1

--- a/solution.py
+++ b/solution.py
@@ -50,37 +50,107 @@
     return dot(high, xh) + dot(high, xl) + dot(low, xh)
 
 
-PLACES = {
-    "center": (BORDER, BORDER, TILE, TILE),
-    "top": (0, BORDER, BORDER, TILE),
-    "bottom": (BORDER + TILE, BORDER, BORDER, TILE),
-    "left": (0, 0, EXT, BORDER),
-    "right": (0, BORDER + TILE, EXT, BORDER),
-}
-
-
-def gradient_kernel(offsets, counts, *refs):
-    names = list(PLACES)
-    n = len(names)
-    pieces = dict(zip(names, refs[:n]))
-    probe, measurements, tables = refs[n : n + 3]
-    outs = dict(zip(names, refs[n + 3 : 2 * n + 3]))
-    obj, grad, sem = refs[2 * n + 3 :]
-    samples = obj.shape[0]
-
-    def view(ref, name):
-        r, c, h, w = PLACES[name]
-        return ref.at[:, :, pl.ds(r, h), pl.ds(c, w)]
-
-    loads = [
-        pltpu.make_async_copy(pieces[k], view(obj, k), sem.at[i])
-        for i, k in enumerate(names)
-    ]
-    for copy in loads:
-        copy.start()
+FAR = BORDER + TILE
+TURN = 4
+
+
+def spots(place, far):
+    row_a = jnp.where(lax.rem(place[0], 2) == 0, far, 0)
+    col_a = jnp.where(place[2] == 0, far, 0)
+    return [pl.multiple_of(v, BORDER) for v in (row_a, far - row_a, col_a, far - col_a)]
+
+
+def regions(place):
+    ra, rb, ca, cb = spots(place, FAR)
+    return [
+        (0, SAMPLES, BORDER, TILE, BORDER, TILE),
+        (0, SAMPLES, ra, BORDER, BORDER, TILE),
+        (0, 1, rb, BORDER, BORDER, TILE),
+        (1, 1, rb, BORDER, BORDER, TILE),
+        (0, SAMPLES, BORDER, TILE, ca, BORDER),
+        (0, SAMPLES, BORDER, TILE, cb, BORDER),
+        (0, SAMPLES, ra, BORDER, ca, BORDER),
+        (0, SAMPLES, rb, BORDER, ca, BORDER),
+        (0, SAMPLES, ra, BORDER, cb, BORDER),
+        (0, SAMPLES, rb, BORDER, cb, BORDER),
+    ]
+
+
+def region_of(array, region):
+    s, n, r, h, c, w = region
+    return array.at[pl.ds(s, n), :, pl.ds(r, h), pl.ds(c, w)]
+
+
+def halves(ref):
+    return [ref.at[:, :, pl.ds(h * BORDER, BORDER)] for h in range(2)]
+
+
+def turns(place):
+    row = place[0]
+    return (row == TURN) | (row == TURN - 1), (row == 0) | (row == place[1])
+
+
+def load_pieces(place, obj, refs, sem):
+    center, strip_a, strip_b0, strip_b1, crossed, side_a, side_b, end_a, end_b = refs
+    sources = [center, strip_a, strip_b0, strip_b1, side_a, side_b] + halves(end_a) + halves(end_b)
+    at_turn, at_end = turns(place)
+    where = regions(place)
+    copies = [
+        pltpu.make_async_copy(src, region_of(obj, region), sem.at[i])
+        for i, (src, region) in enumerate(zip(sources, where))
+    ]
+    for i, copy in enumerate(copies):
+        if i != 3:
+            copy.start()
+    relayed = pltpu.make_async_copy(crossed, region_of(obj, where[3]), sem.at[3])
+
+    @pl.when(at_turn)
+    def _():
+        relayed.start()
+
+    @pl.when(jnp.logical_not(at_turn))
+    def _():
+        copies[3].start()
+
+    def wait():
+        for copy in copies:
+            copy.wait()
+
+        @pl.when(at_end)
+        def _():
+            region_of(obj, where[3])[...] = jnp.zeros((1, 2, BORDER, TILE), jnp.float32)
+
+    return wait
+
+
+def store_pieces(place, grad, refs, sem):
+    center, strip_a, strip_b0, strip_b1, side_a, side_b, end_a, end_b = refs
+    targets = [center, strip_a, strip_b0, strip_b1, side_a, side_b] + halves(end_a) + halves(end_b)
+    copies = [
+        pltpu.make_async_copy(region_of(grad, region), dst, sem.at[i])
+        for i, (dst, region) in enumerate(zip(targets, regions(place)))
+    ]
+    for copy in copies[::-1]:
+        copy.start()
+    for copy in copies:
+        copy.wait()
+
+
+def gradient_kernel(place, offsets, counts, *refs):
+    ins, fixed, outs = refs[:9], refs[9:12], refs[12:20]
+    obj, grad, probe, measurements, tables, sem = refs[20:]
+    samples = SAMPLES
+    fixed_loads = [
+        pltpu.make_async_copy(src, dst, sem.at[16 + i])
+        for i, (src, dst) in enumerate(zip(fixed, (probe, measurements, tables)))
+    ]
+    for copy in fixed_loads:
+        copy.start()
+    wait = load_pieces(place, obj, ins, sem)
     grad[...] = jnp.zeros_like(grad)
-    for copy in loads:
-        copy.wait()
+    for copy in fixed_loads:
+        copy.wait()
+    wait()
 
     lanes = lax.broadcasted_iota(jnp.int32, (PROBE, 128), 1)
     rows = lax.broadcasted_iota(jnp.int32, (8, 128), 0)
@@ -168,74 +238,167 @@
         return carry
 
     lax.fori_loop(0, counts[0], visit, 0)
-    stores = [
-        pltpu.make_async_copy(view(grad, k), outs[k], sem.at[i])
-        for i, k in enumerate(names)
-    ]
-    for copy in stores:
-        copy.start()
-    for copy in stores:
-        copy.wait()
-
-
-def window_gradients(pieces, probe, measurements, offsets, counts):
-    samples = pieces["center"].shape[0]
-    names = list(PLACES)
-    shapes = [jax.ShapeDtypeStruct((samples, 2) + PLACES[k][2:], jnp.float32) for k in names]
+    store_pieces(place, grad, outs, sem)
+
+
+def window_gradients(place, pieces, probe, measurements, offsets, counts, tables):
+    def shape(*dims):
+        return jax.ShapeDtypeStruct(dims, jnp.float32)
+
+    strip, side = shape(1, 2, BORDER, TILE), shape(SAMPLES, 2, TILE, BORDER)
+    end = shape(SAMPLES, 2, 2 * BORDER, BORDER)
+    shapes = [shape(SAMPLES, 2, TILE, TILE), shape(SAMPLES, 2, BORDER, TILE)]
+    shapes += [strip] * 2 + [side] * 2 + [end] * 2
     anywhere = pl.BlockSpec(memory_space=pl.ANY)
-    inside = pl.BlockSpec(memory_space=pltpu.VMEM)
     scalars = pl.BlockSpec(memory_space=pltpu.SMEM)
-    outs = pl.pallas_call(
+    return pl.pallas_call(
         gradient_kernel,
         out_shape=shapes,
-        in_specs=[scalars, scalars] + [anywhere] * len(names) + [inside] * 3,
-        out_specs=[anywhere] * len(names),
+        in_specs=[scalars] * 3 + [anywhere] * (len(pieces) + 3),
+        out_specs=[pl.BlockSpec(memory_space=pltpu.HBM)] + [anywhere] * 7,
         scratch_shapes=[
-            pltpu.VMEM((samples, 2, EXT, EXT), jnp.float32),
-            pltpu.VMEM((samples, 2, EXT, EXT), jnp.float32),
-            pltpu.SemaphoreType.DMA((len(names),)),
+            pltpu.VMEM((SAMPLES, 2, EXT, EXT), jnp.float32),
+            pltpu.VMEM((SAMPLES, 2, EXT, EXT), jnp.float32),
+            pltpu.VMEM((2, PROBE, PROBE), jnp.float32),
+            pltpu.VMEM((POS, PROBE, PROBE), jnp.float32),
+            pltpu.VMEM((4, 2 * PROBE, 2 * PROBE), jnp.bfloat16),
+            pltpu.SemaphoreType.DMA((20,)),
         ],
-        compiler_params=pltpu.CompilerParams(vmem_limit_bytes=56 * 1024 * 1024),
-    )(
-        offsets.reshape(-1),
-        counts.reshape(-1),
-        *[pieces[k] for k in names],
-        probe,
-        measurements,
-        jnp.asarray(dft_tables()),
+        compiler_params=pltpu.CompilerParams(vmem_limit_bytes=48 * 1024 * 1024),
+        cost_estimate=pl.CostEstimate(flops=10**10, bytes_accessed=3 * 10**7, transcendentals=0),
+    )(place, offsets.reshape(-1), counts.reshape(-1), *pieces, probe, measurements, tables)
+
+
+def side_kernel(place, side_a, side_b, held, out, band, got, sem):
+    starts = spots(place, TILE - BORDER)[2:]
+    loads = []
+    for e, (src, first) in enumerate(zip((side_a, side_b), starts)):
+        loads.append((out.at[:, :, :, pl.ds(first, BORDER)], band.at[e]))
+        loads.append((src, got.at[e]))
+    loads = [pltpu.make_async_copy(a, b, sem.at[i]) for i, (a, b) in enumerate(loads)]
+    for copy in loads:
+        copy.start()
+    for copy in loads:
+        copy.wait()
+    band[...] += got[...]
+    stores = [
+        pltpu.make_async_copy(band.at[e], out.at[:, :, :, pl.ds(first, BORDER)], sem.at[e])
+        for e, first in enumerate(starts)
+    ]
+    for copy in stores:
+        copy.start()
+    for copy in stores:
+        copy.wait()
+
+
+def edge_kernel(place, strip_a, strip_b0, strip_b1, crossed, held, out, band, got, sem):
+    starts = spots(place, TILE - BORDER)[:2]
+    at_turn, at_end = turns(place)
+    bands = [
+        (out.at[s, :, pl.ds(first, BORDER)], band.at[e, s])
+        for e, first in enumerate(starts)
+        for s in range(SAMPLES)
+    ]
+    strips = (strip_a.at[0], strip_a.at[1], strip_b0.at[0], strip_b1.at[0], crossed.at[0])
+    loads = bands + [(src, got.at[i]) for i, src in enumerate(strips)]
+    loads = [pltpu.make_async_copy(a, b, sem.at[i]) for i, (a, b) in enumerate(loads)]
+    for copy in loads:
+        copy.start()
+    for copy in loads:
+        copy.wait()
+    band[0, 0] += got[0]
+    band[0, 1] += got[1]
+    band[1, 0] += got[2]
+    band[1, 1] += jnp.where(at_turn, got[4], jnp.where(at_end, 0.0, got[3]))
+    stores = [pltpu.make_async_copy(b, a, sem.at[i]) for i, (a, b) in enumerate(bands)]
+    for copy in stores:
+        copy.start()
+    for copy in stores:
+        copy.wait()
+
+
+def add_in_place(kernel, place, out, parts, scratch, sems):
+    anywhere = pl.BlockSpec(memory_space=pl.ANY)
+    held = pl.BlockSpec(memory_space=pltpu.HBM)
+    return pl.pallas_call(
+        kernel,
+        out_shape=jax.ShapeDtypeStruct(out.shape, out.dtype),
+        in_specs=[pl.BlockSpec(memory_space=pltpu.SMEM)] + [anywhere] * len(parts) + [held],
+        out_specs=held,
+        scratch_shapes=[pltpu.VMEM(shape, jnp.float32) for shape in scratch]
+        + [pltpu.SemaphoreType.DMA((sems,))],
+        input_output_aliases={len(parts) + 1: 0},
+        cost_estimate=pl.CostEstimate(flops=10**6, bytes_accessed=6 * 10**6, transcendentals=0),
+    )(place, *parts, out)
+
+
+def pairs(axis, first):
+    count = lax.axis_size(axis)
+    lower = range(first, count - 1, 2)
+    return [(i, i + 1) for i in lower] + [(i + 1, i) for i in lower]
+
+
+def body(objects, probe, measurements, offsets, counts):
+    row, core = lax.axis_index("row"), lax.rem(lax.axis_index("col"), 2)
+    last = lax.axis_size("row") - 1
+    place = jnp.stack([row, jnp.int32(last), core]).astype(jnp.int32)
+    even, inner = lax.rem(row, 2) == 0, core == 0
+    at_turn, at_end = (row == TURN) | (row == TURN - 1), (row == 0) | (row == last)
+    turn = ((TURN - 1, TURN), (TURN, TURN - 1))
+    detour = [p for p in pairs("row", 1) if p not in turn] + [(TURN - 1, 0), (TURN, last)]
+    over = [(0, TURN), (last, TURN - 1)]
+    far = TILE - BORDER
+
+    def rows_of(first, x):
+        return lax.ppermute(x, "row", pairs("row", first))
+
+    def cols_of(first, x):
+        return lax.ppermute(x, "col", pairs("col", first))
+
+    def routed(x):
+        got = lax.ppermute(x, "row", detour)
+        return got, lax.ppermute(got, "row", over)
+
+    def ends(x):
+        low, high = x[..., :BORDER], x[..., far:]
+        return jnp.where(inner, high, low), jnp.where(inner, low, high)
+
+    low, high = objects[:, :, far:], objects[:, :, :BORDER]
+    send_a, send_b = jnp.where(even, low, high), jnp.where(even, high, low)
+    strip_b1, crossed = routed(send_b[1:])
+    strip_b0 = rows_of(1, send_b[:1])
+    strip_a = rows_of(0, send_a)
+    side_a, side_b = ends(objects)
+    side_b = cols_of(1, side_b)
+    side_a = cols_of(0, side_a)
+    shown = jnp.where(at_turn, crossed, jnp.where(at_end, 0.0, strip_b1))
+    strips = jnp.concatenate([strip_a, jnp.concatenate([strip_b0, shown], axis=0)], axis=2)
+    end_a, end_b = ends(strips)
+    end_b = cols_of(1, end_b)
+    end_a = cols_of(0, end_a)
+    pieces = (objects, strip_a, strip_b0, strip_b1, crossed, side_a, side_b, end_a, end_b)
+    out, strip_a, strip_b0, strip_b1, side_a, side_b, end_a, end_b = window_gradients(
+        place, pieces, probe, measurements[0, 0], offsets, counts, jnp.asarray(dft_tables())
     )
-    return dict(zip(names, outs))
-
-
-def shifted(x, axis, by):
-    count = lax.axis_size(axis)
-    pairs = [(i, i + by) for i in range(count) if 0 <= i + by < count]
-    return lax.ppermute(x, axis, pairs)
-
-
-def body(objects, probe, measurements, offsets, counts):
-    top = shifted(objects[:, :, TILE - BORDER :, :], "row", 1)
-    bottom = shifted(objects[:, :, :BORDER, :], "row", -1)
-
-    def column(lo):
-        return jnp.concatenate([x[..., lo : lo + BORDER] for x in (top, objects, bottom)], axis=2)
-
-    left = shifted(column(TILE - BORDER), "col", 1)
-    right = shifted(column(0), "col", -1)
-    pieces = dict(center=objects, top=top, bottom=bottom, left=left, right=right)
-    g = window_gradients(pieces, probe, measurements[0, 0], offsets, counts)
-    from_right = shifted(g["left"], "col", -1)
-    from_left = shifted(g["right"], "col", 1)
-
-    def folded(x, lo, hi):
-        x = x.at[..., TILE - BORDER :].add(from_right[:, :, lo:hi])
-        return x.at[..., :BORDER].add(from_left[:, :, lo:hi])
-
-    from_below = shifted(folded(g["top"], 0, BORDER), "row", -1)
-    from_above = shifted(folded(g["bottom"], BORDER + TILE, EXT), "row", 1)
-    result = folded(g["center"], BORDER, BORDER + TILE)
-    result = result.at[:, :, TILE - BORDER :].add(from_below)
-    return result.at[:, :, :BORDER].add(from_above)
+
+    end_b = cols_of(1, end_b)
+    end_a = cols_of(0, end_a)
+    end_high, end_low = jnp.where(inner, end_a, end_b), jnp.where(inner, end_b, end_a)
+
+    def folded(x, samples, part):
+        held = slice(part * BORDER, (part + 1) * BORDER)
+        x = x.at[..., far:].add(end_high[samples, :, held])
+        return x.at[..., :BORDER].add(end_low[samples, :, held])
+
+    strip_b1, crossed = routed(folded(strip_b1, slice(1, 2), 1))
+    strip_b0 = rows_of(1, folded(strip_b0, slice(0, 1), 1))
+    side_b = cols_of(1, side_b)
+    strip_a = rows_of(0, folded(strip_a, slice(0, 2), 0))
+    side_a = cols_of(0, side_a)
+    tall, wide = (2, SAMPLES, 2, TILE, BORDER), (2, SAMPLES, 2, BORDER, TILE)
+    out = add_in_place(side_kernel, place, out, (side_a, side_b), (tall, tall), 4)
+    parts = (strip_a, strip_b0, strip_b1, crossed)
+    return add_in_place(edge_kernel, place, out, parts, (wide, (5, 2, BORDER, TILE)), 9)
 
 
 def solution(mesh):

time: 225 us -> 175 us (0.78)
  waiting for transfers between devices: 144 us -> 93.9 us
  starting transfers between devices: 37.8 us -> 42.2 us
  other arithmetic: 14.8 us -> 12.5 us
    ppermute x8 -> x16, waiting for transfers between devices: 144 us -> 93.9 us  [the longest x8 49.1 us: cols_of(): return lax.ppermute(x, 'col', pairs('col', first))]
    scatter-add x6 -> x4, other arithmetic: 13.3 us -> 3.59 us  [the longest x2 1.8 us: folded(): x = x.at[..., far:].add(end_high[samples, :, held])]
    select_n x0 -> x6, other arithmetic: none -> 8.85 us  [the longest x3 5.92 us: ends(): return (jnp.where(inner, high, low), jnp.where(inner, low, high))]
    ppermute x8 -> x16, starting transfers between devices: 37.8 us -> 42.2 us  [the longest x8 20.3 us: cols_of(): return lax.ppermute(x, 'col', pairs('col', first))]
    pallas_call x1 -> x3, Pallas kernels: 22.3 us -> 21 us  [the longest x1 12 us: window_gradients(): pl.pallas_call(gradient_kernel, out_shape=shapes, in_specs=[scalars] * 3...]
  transfers between devices with their start and end apart: 8 -> 16, of which waited for: 6 -> 9; matrix products, arithmetic and copies ran while one was open for 4% -> 6% of each run, Pallas kernels for 0% -> 3%
where the time goes in v3:
time: 175 us; the launch traced here: 174 us
  waiting for transfers between devices  93.9 us (54%)
  starting transfers between devices  42.2 us (24%)
  Pallas kernels  21 us (12%)
  other arithmetic  12.5 us (7%)
  local copies, waits for them, and re-layouts  3.1 us (2%)
    ppermute x8, waiting for transfers between devices, cols_of(): return lax.ppermute(x, 'col', pairs('col', first))  49.1 us
    ppermute x2, waiting for transfers between devices, routed(): return (got, lax.ppermute(got, 'row', over))  23.1 us
    ppermute x8, starting transfers between devices, cols_of(): return lax.ppermute(x, 'col', pairs('col', first))  20.3 us
    ppermute x2, waiting for transfers between devices, routed(): got = lax.ppermute(x, 'row', detour)  18 us
    ppermute x4, starting transfers between devices, rows_of(): return lax.ppermute(x, 'row', pairs('row', first))  15.9 us
    pallas_call x1, Pallas kernels, window_gradients(): pl.pallas_call(gradient_kernel, out_shape=shapes, in_specs=[scalars] * 3...  12 us
    pallas_call x2, Pallas kernels, add_in_place(): pl.pallas_call(kernel, out_shape=jax.ShapeDtypeStruct(out.shape, out.dtyp...  9.02 us
    select_n x3, other arithmetic, ends(): return (jnp.where(inner, high, low), jnp.where(inner, low, high))  5.92 us
  transfers between devices with their start and end apart: 16, of which 9 were waited for; matrix products, arithmetic and copies ran while one was open for 6% of the time, Pallas kernels for 3%

profile of v3, /device:TPU:60, one launch (start us, length us, event | category | flops | bytes accessed | tf_op | source)
XLA Modules:
  0.0 173.6 jit_solution(14811065742521951868)
XLA Ops:
  0.0 2.8 %slice_select_fusion.2 = (f32[2,2,128,512]{3,2,1,0:T(8,128)S(1)}, f32[2,2,128,512]{3,2,1,0:T(8,128)}) fusion(f32[2,2,512,512]{3,2,1,0:T(8,128)} %refs_0_.1, pred[]{:T(512)S(6)} %eq.18), kind=kLoop, calls=%fused_computation.2 | loop fusion | flops 524288 | bytes 4194305 | tf_op jit(solution)/shard_map/jit(_where)/select_n | solution.py:367
  2.9 2.2 %collective-permute-start.2 = (f32[1,2,128,512]{3,2,1,0:T(8,128)S(1)}, f32[1,2,128,512]{3,2,1,0:T(8,128)S(1)}, u32[]{:S(2)}, u32[]{:S(2)}) collective-permute-start(f32[1,2,128,512]{3,2,1,0:T(8,128)S(1)} %get-tuple-element.102), channel_id=1, source_target_pairs={{1,2},{5,6},{2,1},{6,5},{3,0},{4,7},{9,10},{13,14},{10,9},{14,13},... | collective-permute-start | bytes 1572872 | tf_op jit(solution)/shard_map/ppermute | solution.py:359
  6.0 10.1 %collective-permute-done.2.refs_3_ = f32[1,2,128,512]{3,2,1,0:T(8,128)S(1)} collective-permute-done((f32[1,2,128,512]{3,2,1,0:T(8,128)S(1)}, f32[1,2,128,512]{3,2,1,0:T(8,128)S(1)}, u32[]{:S(2)}, u32[]{:S(2)}) %collective-permute-start.2) | collective-permute-done | bytes 524320 | tf_op jit(solution)/shard_map/ppermute | solution.py:359
  17.4 10.6 %collective-permute-start.1 = (f32[1,2,128,512]{3,2,1,0:T(8,128)S(1)}, f32[1,2,128,512]{3,2,1,0:T(8,128)S(1)}, u32[]{:S(2)}, u32[]{:S(2)}) collective-permute-start(f32[1,2,128,512]{3,2,1,0:T(8,128)S(1)} %get-tuple-element.103), channel_id=1, source_target_pairs={{1,2},{3,4},{5,6},{2,1},{4,3},{6,5},{9,10},{11,12},{13,14},{10,9},... | collective-permute-start | bytes 1572872 | tf_op jit(solution)/shard_map/ppermute | solution.py:353
  28.1 3.1 %slice_select_fusion = (f32[2,2,512,128]{3,2,1,0:T(8,128)}, f32[2,2,512,128]{3,2,1,0:T(8,128)}) fusion(f32[2,2,512,512]{3,2,1,0:T(8,128)} %refs_0_.1, pred[]{:T(512)S(6)} %eq.19), kind=kLoop, calls=%fused_computation | loop fusion | flops 524288 | bytes 4194305 | tf_op jit(solution)/shard_map/jit(_where)/select_n | solution.py:364
  31.2 2.0 %collective-permute-start.5 = (f32[2,2,512,128]{3,2,1,0:T(8,128)}, f32[2,2,512,128]{3,2,1,0:T(8,128)}, u32[]{:S(2)}, u32[]{:S(2)}) collective-permute-start(f32[2,2,512,128]{3,2,1,0:T(8,128)} %get-tuple-element.96), channel_id=1, source_target_pairs={{8,16},{24,32},{40,48},{56,64},{72,80},{88,96},{104,112},{120,128}... | collective-permute-start | bytes 3145736 | tf_op jit(solution)/shard_map/ppermute | solution.py:356
  34.5 19.5 %collective-permute-done.3.refs_4_ = f32[1,2,128,512]{3,2,1,0:T(8,128)S(1)} collective-permute-done((f32[1,2,128,512]{3,2,1,0:T(8,128)S(1)}, f32[1,2,128,512]{3,2,1,0:T(8,128)S(1)}, u32[]{:S(2)}, u32[]{:S(2)}) %collective-permute-start.3) | collective-permute-done | bytes 524320 | tf_op jit(solution)/shard_map/ppermute | solution.py:360
  54.1 2.0 %broadcast_select_fusion.2 = (f32[2,2,256,128]{3,2,1,0:T(8,128)}, f32[2,2,256,128]{3,2,1,0:T(8,128)S(1)}, f32[2,2,256,128]{3,2,1,0:T(8,128)S(1)}) fusion(pred[]{:T(512)S(6)} %eq.19, f32[1,2,128,512]{3,2,1,0:T(8,128)S(1)} %select_select_fusion, f32[1,2,128,512]{3,2,1,0:T(8,128)S(1)} %collective-permute-done.1.refs_2_, ...), kind=kLoop, calls=%fused_computation.14 | loop fusion | flops 655360 | bytes 3670017 | tf_op jit(solution)/shard_map/jit(_where)/select_n | solution.py:364
  56.9 1.9 %collective-permute-start.7 = (f32[2,2,256,128]{3,2,1,0:T(8,128)}, f32[2,2,256,128]{3,2,1,0:T(8,128)}, u32[]{:S(2)}, u32[]{:S(2)}) collective-permute-start(f32[2,2,256,128]{3,2,1,0:T(8,128)} %get-tuple-element.93), channel_id=1, source_target_pairs={{8,16},{24,32},{40,48},{56,64},{72,80},{88,96},{104,112},{120,128}... | collective-permute-start | bytes 1572872 | tf_op jit(solution)/shard_map/ppermute | solution.py:356
  59.8 14.3 %collective-permute-done.5.refs_6_ = f32[2,2,512,128]{3,2,1,0:T(8,128)} collective-permute-done((f32[2,2,512,128]{3,2,1,0:T(8,128)}, f32[2,2,512,128]{3,2,1,0:T(8,128)}, u32[]{:S(2)}, u32[]{:S(2)}) %collective-permute-start.5) | collective-permute-done | bytes 1048608 | tf_op jit(solution)/shard_map/ppermute | solution.py:356
  74.9 8.5 %collective-permute-done.7.refs_8_ = f32[2,2,256,128]{3,2,1,0:T(8,128)} collective-permute-done((f32[2,2,256,128]{3,2,1,0:T(8,128)}, f32[2,2,256,128]{3,2,1,0:T(8,128)}, u32[]{:S(2)}, u32[]{:S(2)}) %collective-permute-start.7) | collective-permute-done | bytes 524320 | tf_op jit(solution)/shard_map/ppermute | solution.py:356
  84.5 12.0 %shard_map.64 = (f32[2,2,512,512]{3,2,1,0:T(8,128)}, f32[2,2,128,512]{3,2,1,0:T(8,128)}, f32[1,2,128,512]{3,2,1,0:T(8,128)S(1)}, f32[1,2,128,512]{3,2,1,0:T(8,12...) custom-call(s32[3]{0:T(128)S(1)} %pad_add_fusion.place, ...), custom_call_target="tpu_custom_call" | custom-call | flops 10000000000 | bytes 30000000 | tf_op jit(solution)/shard_map/pallas_call | solution.py:254
  96.5 9.5 %collective-permute-start.8 = (f32[2,2,256,128]{3,2,1,0:T(8,128)S(1)}, f32[2,2,256,128]{3,2,1,0:T(8,128)S(1)}, u32[]{:S(2)}, u32[]{:S(2)}) collective-permute-start(f32[2,2,256,128]{3,2,1,0:T(8,128)S(1)} %get-tuple-element.86), channel_id=1, source_target_pairs={{0,8},{16,24},{32,40},{48,56},{64,72},{80,88},{96,104},{112,120},{... | collective-permute-start | bytes 1572872 | tf_op jit(solution)/shard_map/ppermute | solution.py:356
  106.0 3.0 %collective-permute-start.9 = (f32[2,2,256,128]{3,2,1,0:T(8,128)S(1)}, f32[2,2,256,128]{3,2,1,0:T(8,128)S(1)}, u32[]{:S(2)}, u32[]{:S(2)}) collective-permute-start(f32[2,2,256,128]{3,2,1,0:T(8,128)S(1)} %get-tuple-element.87), channel_id=1, source_target_pairs={{8,16},{24,32},{40,48},{56,64},{72,80},{88,96},{104,112},{120,128}... | collective-permute-start | bytes 1572872 | tf_op jit(solution)/shard_map/ppermute | solution.py:356
  109.1 2.5 %collective-permute-start.15 = (f32[2,2,512,128]{3,2,1,0:T(8,128)}, f32[2,2,512,128]{3,2,1,0:T(8,128)S(1)}, u32[]{:S(2)}, u32[]{:S(2)}) collective-permute-start(f32[2,2,512,128]{3,2,1,0:T(8,128)} %get-tuple-element.91), channel_id=1, source_target_pairs={{8,16},{24,32},{40,48},{56,64},{72,80},{88,96},{104,112},{120,128}... | collective-permute-start | bytes 3145736 | tf_op jit(solution)/shard_map/ppermute | solution.py:356
  111.6 10.3 %collective-permute-done.9 = f32[2,2,256,128]{3,2,1,0:T(8,128)S(1)} collective-permute-done((f32[2,2,256,128]{3,2,1,0:T(8,128)S(1)}, f32[2,2,256,128]{3,2,1,0:T(8,128)S(1)}, u32[]{:S(2)}, u32[]{:S(2)}) %collective-permute-start.9) | collective-permute-done | bytes 524320 | tf_op jit(solution)/shard_map/ppermute | solution.py:356
  122.0 1.7 %fusion.1 = f32[2,2,128,512]{3,2,1,0:T(8,128)} fusion(f32[2,2,128,512]{3,2,1,0:T(8,128)} %get-tuple-element.85, f32[2,2,256,128]{3,2,1,0:T(8,128)S(1)} %get-tuple-element.101), kind=kLoop, calls=%fused_computation.11 | loop fusion | flops 65536 | bytes 786432 | tf_op jit(solution)/shard_map/scatter-add | solution.py:390
  127.1 4.1 %collective-permute-start.11 = (f32[1,2,128,512]{3,2,1,0:T(8,128)S(1)}, f32[1,2,128,512]{3,2,1,0:T(8,128)}, u32[]{:S(2)}, u32[]{:S(2)}) collective-permute-start(f32[1,2,128,512]{3,2,1,0:T(8,128)S(1)} %get-tuple-element.105), channel_id=1, source_target_pairs={{1,2},{3,4},{5,6},{2,1},{4,3},{6,5},{9,10},{11,12},{13,14},{10,9},... | collective-permute-start | bytes 1572872 | tf_op jit(solution)/shard_map/ppermute | solution.py:353
  131.2 7.9 %collective-permute-done.12.strip_b1 = f32[1,2,128,512]{3,2,1,0:T(8,128)S(1)} collective-permute-done((f32[1,2,128,512]{3,2,1,0:T(8,128)S(1)}, f32[1,2,128,512]{3,2,1,0:T(8,128)S(1)}, u32[]{:S(2)}, u32[]{:S(2)}) %collective-permute-start.12) | collective-permute-done | bytes 524320 | tf_op jit(solution)/shard_map/ppermute | solution.py:359
  140.4 15.9 %collective-permute-done.15.side_b = f32[2,2,512,128]{3,2,1,0:T(8,128)S(1)} collective-permute-done((f32[2,2,512,128]{3,2,1,0:T(8,128)}, f32[2,2,512,128]{3,2,1,0:T(8,128)S(1)}, u32[]{:S(2)}, u32[]{:S(2)}) %collective-permute-start.15) | collective-permute-done | bytes 1048608 | tf_op jit(solution)/shard_map/ppermute | solution.py:356
  157.4 4.4 %shard_map.65.held = f32[2,2,512,512]{3,2,1,0:T(8,128)} custom-call(s32[3]{0:T(128)} %copy-done, f32[2,2,512,128]{3,2,1,0:T(8,128)} %copy-done.5, f32[2,2,512,128]{3,2,1,0:T(8,128)} %copy-done.6, f32[2,2,512,512]{3,2,1,0:T(8,128)} %get-tuple-element.92.held), custom_call_target="tpu_custom_call", output_to_operand_aliasing={{}: (3, {})} | custom-call | flops 1000000 | bytes 6000000 | tf_op jit(solution)/shard_map/pallas_call | solution.py:323
  161.8 3.6 %collective-permute-done.11.strip_b0 = f32[1,2,128,512]{3,2,1,0:T(8,128)} collective-permute-done((f32[1,2,128,512]{3,2,1,0:T(8,128)S(1)}, f32[1,2,128,512]{3,2,1,0:T(8,128)}, u32[]{:S(2)}, u32[]{:S(2)}) %collective-permute-start.11) | collective-permute-done | bytes 524320 | tf_op jit(solution)/shard_map/ppermute | solution.py:353
  165.4 3.6 %collective-permute-done.13.crossed = f32[1,2,128,512]{3,2,1,0:T(8,128)} collective-permute-done((f32[1,2,128,512]{3,2,1,0:T(8,128)S(1)}, f32[1,2,128,512]{3,2,1,0:T(8,128)}, u32[]{:S(2)}, u32[]{:S(2)}) %collective-permute-start.13) | collective-permute-done | bytes 524320 | tf_op jit(solution)/shard_map/ppermute | solution.py:360
  169.0 4.6 %shard_map.66 = f32[2,2,512,512]{3,2,1,0:T(8,128)} custom-call(s32[3]{0:T(128)} %copy-done, f32[2,2,128,512]{3,2,1,0:T(8,128)} %collective-permute-done.10.strip_a, f32[1,2,128,512]{3,2,1,0:T(8,128)} %collective-permute-done.11.strip_b0, f32[1,2,128,512]{3,2,1,0:T(8,128)} %copy-done.7, ...), custom_call_target="tpu_custom_call", output_to_operand_aliasing={{}: (5, {})} | custom-call | flops 1000000 | bytes 6000000 | tf_op jit(solution)/shard_map/pallas_call | solution.py:323
  (43 shorter events, 12.4 us)
Async XLA Ops:
  2.9 13.3 %collective-permute-start.2 = (f32[1,2,128,512]{3,2,1,0:T(8,128)S(1)}, f32[1,2,128,512]{3,2,1,0:T(8,128)S(1)}, u32[]{:S(2)}, u32[]{:S(2)}) collective-permute-start(f32[1,2,128,512]{3,2,1,0:T(8,128)S(1)} %get-tuple-element.102), channel_id=1, source_target_pairs={{1,2},{5,6},{2,1},{6,5},{3,0},{4,7},{9,10},{13,14},{10,9},{14,13},... | collective-permute-start | bytes 1572872 | tf_op jit(solution)/shard_map/ppermute | solution.py:359
  5.0 49.1 %collective-permute-start = (f32[2,2,128,512]{3,2,1,0:T(8,128)}, f32[2,2,128,512]{3,2,1,0:T(8,128)}, u32[]{:S(2)}, u32[]{:S(2)}) collective-permute-start(f32[2,2,128,512]{3,2,1,0:T(8,128)} %get-tuple-element.99), channel_id=1, source_target_pairs={{0,1},{2,3},{4,5},{6,7},{1,0},{3,2},{5,4},{7,6},{8,9},{10,11},{12,... | collective-permute-start | bytes 3145736 | tf_op jit(solution)/shard_map/ppermute | solution.py:353
  16.2 37.8 %collective-permute-start.3 = (f32[1,2,128,512]{3,2,1,0:T(8,128)S(1)}, f32[1,2,128,512]{3,2,1,0:T(8,128)S(1)}, u32[]{:S(2)}, u32[]{:S(2)}) collective-permute-start(f32[1,2,128,512]{3,2,1,0:T(8,128)S(1)} %collective-permute-done.2.refs_3_), channel_id=1, source_target_pairs={{0,4},{7,3},{8,12},{15,11},{16,20},{23,19},{24,28},{31,27},{32,36}... | collective-permute-start | bytes 1572872 | tf_op jit(solution)/shard_map/ppermute | solution.py:360
  17.4 36.6 %collective-permute-start.1 = (f32[1,2,128,512]{3,2,1,0:T(8,128)S(1)}, f32[1,2,128,512]{3,2,1,0:T(8,128)S(1)}, u32[]{:S(2)}, u32[]{:S(2)}) collective-permute-start(f32[1,2,128,512]{3,2,1,0:T(8,128)S(1)} %get-tuple-element.103), channel_id=1, source_target_pairs={{1,2},{3,4},{5,6},{2,1},{4,3},{6,5},{9,10},{11,12},{13,14},{10,9},... | collective-permute-start | bytes 1572872 | tf_op jit(solution)/shard_map/ppermute | solution.py:353
  31.2 28.3 %copy-start.8 = (s32[1,1,3,2]{2,3,1,0:T(2,128)S(1)}, s32[1,1,3,2]{2,3,1,0:T(2,128)}, u32[]{:S(2)}) copy-start(s32[1,1,3,2]{2,3,1,0:T(2,128)} %param.21) | copy-start | bytes 76
  31.2 52.2 %copy-start.1 = (f32[1,1,3,256,256]{4,3,2,1,0:T(8,128)S(1)}, f32[1,1,3,256,256]{4,3,2,1,0:T(8,128)}, u32[]{:S(2)}) copy-start(f32[1,1,3,256,256]{4,3,2,1,0:T(8,128)} %param.20) | copy-start | bytes 2359300
  31.2 52.2 %copy-start.2 = (f32[2,256,256]{2,1,0:T(8,128)S(1)}, f32[2,256,256]{2,1,0:T(8,128)}, u32[]{:S(2)}) copy-start(f32[2,256,256]{2,1,0:T(8,128)} %refs_9_.1) | copy-start | bytes 1572868
  31.2 42.9 %collective-permute-start.5 = (f32[2,2,512,128]{3,2,1,0:T(8,128)}, f32[2,2,512,128]{3,2,1,0:T(8,128)}, u32[]{:S(2)}, u32[]{:S(2)}) collective-permute-start(f32[2,2,512,128]{3,2,1,0:T(8,128)} %get-tuple-element.96), channel_id=1, source_target_pairs={{8,16},{24,32},{40,48},{56,64},{72,80},{88,96},{104,112},{120,128}... | collective-permute-start | bytes 3145736 | tf_op jit(solution)/shard_map/ppermute | solution.py:356
  33.2 40.8 %collective-permute-start.4 = (f32[2,2,512,128]{3,2,1,0:T(8,128)}, f32[2,2,512,128]{3,2,1,0:T(8,128)}, u32[]{:S(2)}, u32[]{:S(2)}) collective-permute-start(f32[2,2,512,128]{3,2,1,0:T(8,128)} %get-tuple-element.97), channel_id=1, source_target_pairs={{0,8},{16,24},{32,40},{48,56},{64,72},{80,88},{96,104},{112,120},{... | collective-permute-start | bytes 3145736 | tf_op jit(solution)/shard_map/ppermute | solution.py:356
  56.9 17.2 %collective-permute-start.6 = (f32[2,2,256,128]{3,2,1,0:T(8,128)}, f32[2,2,256,128]{3,2,1,0:T(8,128)S(1)}, u32[]{:S(2)}, u32[]{:S(2)}) collective-permute-start(f32[2,2,256,128]{3,2,1,0:T(8,128)} %broadcast_select_fusion.3), channel_id=1, source_target_pairs={{0,8},{16,24},{32,40},{48,56},{64,72},{80,88},{96,104},{112,120},{... | collective-permute-start | bytes 1572872 | tf_op jit(solution)/shard_map/ppermute | solution.py:356
  56.9 26.5 %collective-permute-start.7 = (f32[2,2,256,128]{3,2,1,0:T(8,128)}, f32[2,2,256,128]{3,2,1,0:T(8,128)}, u32[]{:S(2)}, u32[]{:S(2)}) collective-permute-start(f32[2,2,256,128]{3,2,1,0:T(8,128)} %get-tuple-element.93), channel_id=1, source_target_pairs={{8,16},{24,32},{40,48},{56,64},{72,80},{88,96},{104,112},{120,128}... | collective-permute-start | bytes 1572872 | tf_op jit(solution)/shard_map/ppermute | solution.py:356
  59.8 36.7 %copy-start = (s32[3]{0:T(128)}, s32[3]{0:T(128)S(1)}, u32[]{:S(2)}) copy-start(s32[3]{0:T(128)S(1)} %pad_add_fusion.place) | copy-start | bytes 40
  83.4 1.0 copy-start.4
  96.5 15.1 %collective-permute-start.8 = (f32[2,2,256,128]{3,2,1,0:T(8,128)S(1)}, f32[2,2,256,128]{3,2,1,0:T(8,128)S(1)}, u32[]{:S(2)}, u32[]{:S(2)}) collective-permute-start(f32[2,2,256,128]{3,2,1,0:T(8,128)S(1)} %get-tuple-element.86), channel_id=1, source_target_pairs={{0,8},{16,24},{32,40},{48,56},{64,72},{80,88},{96,104},{112,120},{... | collective-permute-start | bytes 1572872 | tf_op jit(solution)/shard_map/ppermute | solution.py:356
  106.0 16.0 %collective-permute-start.9 = (f32[2,2,256,128]{3,2,1,0:T(8,128)S(1)}, f32[2,2,256,128]{3,2,1,0:T(8,128)S(1)}, u32[]{:S(2)}, u32[]{:S(2)}) collective-permute-start(f32[2,2,256,128]{3,2,1,0:T(8,128)S(1)} %get-tuple-element.87), channel_id=1, source_target_pairs={{8,16},{24,32},{40,48},{56,64},{72,80},{88,96},{104,112},{120,128}... | collective-permute-start | bytes 1572872 | tf_op jit(solution)/shard_map/ppermute | solution.py:356
  109.0 31.4 %collective-permute-start.14 = (f32[2,2,512,128]{3,2,1,0:T(8,128)}, f32[2,2,512,128]{3,2,1,0:T(8,128)S(1)}, u32[]{:S(2)}, u32[]{:S(2)}) collective-permute-start(f32[2,2,512,128]{3,2,1,0:T(8,128)} %get-tuple-element.90), channel_id=1, source_target_pairs={{0,8},{16,24},{32,40},{48,56},{64,72},{80,88},{96,104},{112,120},{... | collective-permute-start | bytes 3145736 | tf_op jit(solution)/shard_map/ppermute | solution.py:356
  109.1 47.3 %collective-permute-start.15 = (f32[2,2,512,128]{3,2,1,0:T(8,128)}, f32[2,2,512,128]{3,2,1,0:T(8,128)S(1)}, u32[]{:S(2)}, u32[]{:S(2)}) collective-permute-start(f32[2,2,512,128]{3,2,1,0:T(8,128)} %get-tuple-element.91), channel_id=1, source_target_pairs={{8,16},{24,32},{40,48},{56,64},{72,80},{88,96},{104,112},{120,128}... | collective-permute-start | bytes 3145736 | tf_op jit(solution)/shard_map/ppermute | solution.py:356
  125.6 13.5 %collective-permute-start.12 = (f32[1,2,128,512]{3,2,1,0:T(8,128)S(1)}, f32[1,2,128,512]{3,2,1,0:T(8,128)S(1)}, u32[]{:S(2)}, u32[]{:S(2)}) collective-permute-start(f32[1,2,128,512]{3,2,1,0:T(8,128)S(1)} %get-tuple-element.104), channel_id=1, source_target_pairs={{1,2},{5,6},{2,1},{6,5},{3,0},{4,7},{9,10},{13,14},{10,9},{14,13},... | collective-permute-start | bytes 1572872 | tf_op jit(solution)/shard_map/ppermute | solution.py:359
  127.0 38.5 %collective-permute-start.10 = (f32[2,2,128,512]{3,2,1,0:T(8,128)}, f32[2,2,128,512]{3,2,1,0:T(8,128)}, u32[]{:S(2)}, u32[]{:S(2)}) collective-permute-start(f32[2,2,128,512]{3,2,1,0:T(8,128)} %fusion), channel_id=1, source_target_pairs={{0,1},{2,3},{4,5},{6,7},{1,0},{3,2},{5,4},{7,6},{8,9},{10,11},{12,... | collective-permute-start | bytes 3145736 | tf_op jit(solution)/shard_map/ppermute | solution.py:353
  127.1 38.4 %collective-permute-start.11 = (f32[1,2,128,512]{3,2,1,0:T(8,128)S(1)}, f32[1,2,128,512]{3,2,1,0:T(8,128)}, u32[]{:S(2)}, u32[]{:S(2)}) collective-permute-start(f32[1,2,128,512]{3,2,1,0:T(8,128)S(1)} %get-tuple-element.105), channel_id=1, source_target_pairs={{1,2},{3,4},{5,6},{2,1},{4,3},{6,5},{9,10},{11,12},{13,14},{10,9},... | collective-permute-start | bytes 1572872 | tf_op jit(solution)/shard_map/ppermute | solution.py:353
  139.1 29.9 %copy-start.7 = (f32[1,2,128,512]{3,2,1,0:T(8,128)}, f32[1,2,128,512]{3,2,1,0:T(8,128)S(1)}, u32[]{:S(2)}) copy-start(f32[1,2,128,512]{3,2,1,0:T(8,128)S(1)} %collective-permute-done.12.strip_b1) | copy-start | bytes 1572868
  139.1 29.9 %collective-permute-start.13 = (f32[1,2,128,512]{3,2,1,0:T(8,128)S(1)}, f32[1,2,128,512]{3,2,1,0:T(8,128)}, u32[]{:S(2)}, u32[]{:S(2)}) collective-permute-start(f32[1,2,128,512]{3,2,1,0:T(8,128)S(1)} %collective-permute-done.12.strip_b1), channel_id=1, source_target_pairs={{0,4},{7,3},{8,12},{15,11},{16,20},{23,19},{24,28},{31,27},{32,36}... | collective-permute-start | bytes 1572872 | tf_op jit(solution)/shard_map/ppermute | solution.py:360
  140.4 16.0 %copy-start.5 = (f32[2,2,512,128]{3,2,1,0:T(8,128)}, f32[2,2,512,128]{3,2,1,0:T(8,128)S(1)}, u32[]{:S(2)}) copy-start(f32[2,2,512,128]{3,2,1,0:T(8,128)S(1)} %collective-permute-done.14.side_a) | copy-start | bytes 3145732
  156.4 1.0 copy-start.6
  (1 other events, 0.8 us)

commit v4 on v3

--- a/solution.py
+++ b/solution.py
@@ -19,15 +19,39 @@
 SMOOTHING = 0.5
 
 
+HALF = PROBE // 2
+
+
 def dft_tables():
-    places = np.arange(PROBE, dtype=np.int64)
-    angle = (places[:, None] * places[None, :] % PROBE) * (2.0 * math.pi / PROBE)
+    places = np.arange(HALF, dtype=np.int64)
+    angle = (places[:, None] * places[None, :] % HALF) * (2.0 * math.pi / HALF)
     scale = 1.0 / math.sqrt(PROBE)
     cosines, sines = np.cos(angle) * scale, np.sin(angle) * scale
     forward = np.block([[cosines, -sines], [sines, cosines]]).astype(np.float32)
     high = forward.astype(ml_dtypes.bfloat16)
     low = (forward - high.astype(np.float32)).astype(ml_dtypes.bfloat16)
     return np.stack([high, low, high.T, low.T])
+
+
+def twiddles():
+    angle = np.arange(HALF) * (2.0 * math.pi / PROBE)
+    lanes = [np.broadcast_to(x, (HALF, HALF)) for x in (np.cos(angle), -np.sin(angle))]
+    return np.stack(lanes + [x.T for x in lanes]).astype(np.float32)
+
+
+def butterfly(xr, xi, wr, wi, axis):
+    (ar, br), (ai, bi) = jnp.split(xr, 2, axis), jnp.split(xi, 2, axis)
+    dr, di = ar - br, ai - bi
+    return (ar + br, ai + bi), (dr * wr - di * wi, dr * wi + di * wr)
+
+
+def unfold(a, b, wr, wi, axis):
+    (ar, ai), (br, bi) = a, b
+    tr, ti = br * wr + bi * wi, bi * wr - br * wi
+    return (
+        jnp.concatenate([ar + tr, ar - tr], axis=axis),
+        jnp.concatenate([ai + ti, ai - ti], axis=axis),
+    )
 
 
 def split(x):
@@ -136,13 +160,39 @@
         copy.wait()
 
 
+def part_kernel(measured, order, out):
+    pick = order[...]
+    for q in range(POS):
+        x = measured[q]
+        total = jnp.zeros((PROBE, PROBE), jnp.float32)
+        for _ in range(3):
+            piece = x.astype(jnp.bfloat16)
+            x = x - piece.astype(jnp.float32)
+            total += dot(dot(pick, piece).astype(jnp.bfloat16), pick.T)
+        for p in range(2):
+            for r in range(2):
+                lanes = pl.ds((p * 2 + r) * HALF, HALF)
+                out[q, :, lanes] = total[r * HALF : (r + 1) * HALF, p * HALF : (p + 1) * HALF]
+
+
+def parted_measurements(measured):
+    order = np.zeros((PROBE, PROBE), np.float32)
+    for k in range(PROBE):
+        order[k, k * 2 % PROBE + k * 2 // PROBE] = 1.0
+    return pl.pallas_call(
+        part_kernel,
+        out_shape=jax.ShapeDtypeStruct((POS, HALF, 2 * PROBE), jnp.float32),
+        cost_estimate=pl.CostEstimate(flops=10**9, bytes_accessed=10**6, transcendentals=0),
+    )(measured, jnp.asarray(order.astype(ml_dtypes.bfloat16)))
+
+
 def gradient_kernel(place, offsets, counts, *refs):
-    ins, fixed, outs = refs[:9], refs[9:12], refs[12:20]
-    obj, grad, probe, measurements, tables, sem = refs[20:]
+    ins, fixed, outs = refs[:9], refs[9:13], refs[13:21]
+    obj, grad, probe, measurements, tables, twiddle, sem = refs[21:]
     samples = SAMPLES
     fixed_loads = [
         pltpu.make_async_copy(src, dst, sem.at[16 + i])
-        for i, (src, dst) in enumerate(zip(fixed, (probe, measurements, tables)))
+        for i, (src, dst) in enumerate(zip(fixed, (probe, measurements, tables, twiddle)))
     ]
     for copy in fixed_loads:
         copy.start()
@@ -194,45 +244,43 @@
             add(cz, jnp.where(early, first, 0.0))
             add(cb, value[:, 128:])
 
-        stacked = []
+        lane_r, lane_i = twiddle[0, 0:1], twiddle[1, 0:1]
+        row_r, row_i = twiddle[2], twiddle[3]
+        waves = []
         for s in range(samples):
             o_r, o_i = frame(s, 0), frame(s, 1)
-            stacked.append(
-                jnp.concatenate([pr * o_r - pi * o_i, pr * o_i + pi * o_r], axis=1)
-            )
-        wave = jnp.concatenate(stacked, axis=0)
-        half = right_product(wave, tables[0], tables[1])
-        turned = jnp.concatenate(
-            [
-                jnp.concatenate(
-                    [half[s * PROBE : (s + 1) * PROBE, k * PROBE : (k + 1) * PROBE] for s in range(samples)],
-                    axis=1,
-                )
-                for k in range(2)
-            ],
-            axis=0,
-        )
-        spectrum = left_product(tables[2], tables[3], turned)
-        s_r, s_i = spectrum[:PROBE], spectrum[PROBE:]
-        m = measurements[q]
-        m = jnp.concatenate([m] * samples, axis=1)
+            waves.append((pr * o_r - pi * o_i, pr * o_i + pi * o_r))
+        parts = [butterfly(*wave, lane_r, lane_i, 1) for wave in waves]
+        stacked = [
+            jnp.concatenate(parts[s][p], axis=1) for p in range(2) for s in range(samples)
+        ]
+        half = right_product(jnp.concatenate(stacked, axis=0), tables[0], tables[1])
+        blocks = []
+        for s in range(samples):
+            for p in range(2):
+                y = half[(p * samples + s) * PROBE : (p * samples + s + 1) * PROBE]
+                for pair in butterfly(y[:, :HALF], y[:, HALF:], row_r, row_i, 0):
+                    blocks.append(jnp.concatenate(pair, axis=0))
+        spectrum = left_product(tables[2], tables[3], jnp.concatenate(blocks, axis=1))
+        s_r, s_i = spectrum[:HALF], spectrum[HALF:]
+        m = jnp.concatenate([measurements[q]] * samples, axis=1)
         factor = 1.0 - m * lax.rsqrt(s_r * s_r + s_i * s_i + SMOOTHING)
         scaled = jnp.concatenate([s_r * factor, s_i * factor], axis=0)
         back = left_product(tables[0], tables[1], scaled)
-        back = jnp.concatenate(
-            [
-                jnp.concatenate(
-                    [back[:PROBE, s * PROBE : (s + 1) * PROBE], back[PROBE:, s * PROBE : (s + 1) * PROBE]],
-                    axis=1,
-                )
-                for s in range(samples)
-            ],
-            axis=0,
-        )
-        final = right_product(back, tables[2], tables[3])
+        stacked = []
+        for p in range(2):
+            for s in range(samples):
+                at = (s * 2 + p) * PROBE
+                a, b = back[:, at : at + HALF], back[:, at + HALF : at + PROBE]
+                pair = unfold((a[:HALF], a[HALF:]), (b[:HALF], b[HALF:]), row_r, row_i, 0)
+                stacked.append(jnp.concatenate(pair, axis=1))
+        final = right_product(jnp.concatenate(stacked, axis=0), tables[2], tables[3])
         for s in range(samples):
-            b_r = final[s * PROBE : (s + 1) * PROBE, :PROBE]
-            b_i = final[s * PROBE : (s + 1) * PROBE, PROBE:]
+            a = final[s * PROBE : (s + 1) * PROBE]
+            b = final[(samples + s) * PROBE : (samples + s + 1) * PROBE]
+            b_r, b_i = unfold(
+                (a[:, :HALF], a[:, HALF:]), (b[:, :HALF], b[:, HALF:]), lane_r, lane_i, 1
+            )
             scatter(s, 0, pr * b_r + pi * b_i)
             scatter(s, 1, pr * b_i - pi * b_r)
         return carry
@@ -254,19 +302,20 @@
     return pl.pallas_call(
         gradient_kernel,
         out_shape=shapes,
-        in_specs=[scalars] * 3 + [anywhere] * (len(pieces) + 3),
+        in_specs=[scalars] * 3 + [anywhere] * (len(pieces) + 4),
         out_specs=[pl.BlockSpec(memory_space=pltpu.HBM)] + [anywhere] * 7,
         scratch_shapes=[
             pltpu.VMEM((SAMPLES, 2, EXT, EXT), jnp.float32),
             pltpu.VMEM((SAMPLES, 2, EXT, EXT), jnp.float32),
             pltpu.VMEM((2, PROBE, PROBE), jnp.float32),
-            pltpu.VMEM((POS, PROBE, PROBE), jnp.float32),
-            pltpu.VMEM((4, 2 * PROBE, 2 * PROBE), jnp.bfloat16),
+            pltpu.VMEM((POS, HALF, 2 * PROBE), jnp.float32),
+            pltpu.VMEM((4, PROBE, PROBE), jnp.bfloat16),
+            pltpu.VMEM((4, HALF, HALF), jnp.float32),
             pltpu.SemaphoreType.DMA((20,)),
         ],
         compiler_params=pltpu.CompilerParams(vmem_limit_bytes=48 * 1024 * 1024),
         cost_estimate=pl.CostEstimate(flops=10**10, bytes_accessed=3 * 10**7, transcendentals=0),
-    )(place, offsets.reshape(-1), counts.reshape(-1), *pieces, probe, measurements, tables)
+    )(place, offsets.reshape(-1), counts.reshape(-1), *pieces, probe, measurements, *tables)
 
 
 def side_kernel(place, side_a, side_b, held, out, band, got, sem):
@@ -300,19 +349,26 @@
         for s in range(SAMPLES)
     ]
     strips = (strip_a.at[0], strip_a.at[1], strip_b0.at[0], strip_b1.at[0], crossed.at[0])
-    loads = bands + [(src, got.at[i]) for i, src in enumerate(strips)]
-    loads = [pltpu.make_async_copy(a, b, sem.at[i]) for i, (a, b) in enumerate(loads)]
-    for copy in loads:
-        copy.start()
-    for copy in loads:
-        copy.wait()
-    band[0, 0] += got[0]
-    band[0, 1] += got[1]
-    band[1, 0] += got[2]
-    band[1, 1] += jnp.where(at_turn, got[4], jnp.where(at_end, 0.0, got[3]))
-    stores = [pltpu.make_async_copy(b, a, sem.at[i]) for i, (a, b) in enumerate(bands)]
-    for copy in stores:
-        copy.start()
+    count = len(bands)
+    early = [pltpu.make_async_copy(a, b, sem.at[i]) for i, (a, b) in enumerate(bands)]
+    late = [
+        pltpu.make_async_copy(src, got.at[i], sem.at[count + i]) for i, src in enumerate(strips)
+    ]
+    for i in range(count):
+        early[i].start()
+        late[i].start()
+    late[count].start()
+    stores = []
+    for i, (a, b) in enumerate(bands):
+        early[i].wait()
+        late[i].wait()
+        if i < count - 1:
+            b[...] += got[i]
+        else:
+            late[count].wait()
+            b[...] += jnp.where(at_turn, got[count], jnp.where(at_end, 0.0, got[i]))
+        stores.append(pltpu.make_async_copy(b, a, sem.at[i]))
+        stores[-1].start()
     for copy in stores:
         copy.wait()
 
@@ -355,9 +411,9 @@
     def cols_of(first, x):
         return lax.ppermute(x, "col", pairs("col", first))
 
-    def routed(x):
-        got = lax.ppermute(x, "row", detour)
-        return got, lax.ppermute(got, "row", over)
+    def routed(x, *others):
+        got, *others = lax.optimization_barrier((lax.ppermute(x, "row", detour), *others))
+        return got, lax.ppermute(got, "row", over), *others
 
     def ends(x):
         low, high = x[..., :BORDER], x[..., far:]
@@ -365,20 +421,20 @@
 
     low, high = objects[:, :, far:], objects[:, :, :BORDER]
     send_a, send_b = jnp.where(even, low, high), jnp.where(even, high, low)
-    strip_b1, crossed = routed(send_b[1:])
+    side_a, side_b = ends(objects)
+    strip_b1, crossed, side_b = routed(send_b[1:], cols_of(1, side_b))
     strip_b0 = rows_of(1, send_b[:1])
     strip_a = rows_of(0, send_a)
-    side_a, side_b = ends(objects)
-    side_b = cols_of(1, side_b)
     side_a = cols_of(0, side_a)
     shown = jnp.where(at_turn, crossed, jnp.where(at_end, 0.0, strip_b1))
     strips = jnp.concatenate([strip_a, jnp.concatenate([strip_b0, shown], axis=0)], axis=2)
     end_a, end_b = ends(strips)
     end_b = cols_of(1, end_b)
     end_a = cols_of(0, end_a)
+    parted = parted_measurements(measurements[0, 0])
     pieces = (objects, strip_a, strip_b0, strip_b1, crossed, side_a, side_b, end_a, end_b)
     out, strip_a, strip_b0, strip_b1, side_a, side_b, end_a, end_b = window_gradients(
-        place, pieces, probe, measurements[0, 0], offsets, counts, jnp.asarray(dft_tables())
+        place, pieces, probe, parted, offsets, counts, [jnp.asarray(dft_tables()), jnp.asarray(twiddles())]
     )
 
     end_b = cols_of(1, end_b)

time: 175 us -> 172 us (0.983)
  waiting for transfers between devices: 93.9 us -> 73.2 us
  starting transfers between devices: 42.2 us -> 52.8 us
  Pallas kernels: 21 us -> 28.9 us
    ppermute x8, waiting for transfers between devices: 49.1 us -> 15.7 us  [cols_of(): return lax.ppermute(x, 'col', pairs('col', first))]
    ppermute x4, waiting for transfers between devices: 3.65 us -> 28.9 us  [rows_of(): return lax.ppermute(x, 'row', pairs('row', first))]
    ppermute x4, waiting for transfers between devices: 41.1 us -> 28.5 us  [the longest x2 18.4 us: routed(): return (got, lax.ppermute(got, 'row', over), *others)]
    ppermute x4, starting transfers between devices: 15.9 us -> 22 us  [rows_of(): return lax.ppermute(x, 'row', pairs('row', first))]
    pallas_call x1, Pallas kernels: 12 us -> 17.3 us  [window_gradients(): pl.pallas_call(gradient_kernel, out_shape=shapes, in_specs=[scalars] * 3...]
    ppermute x4, starting transfers between devices: 6.04 us -> 10.4 us  [the longest x2 7.85 us: routed(): lax.ppermute(x, 'row', detour)]
    pallas_call x0 -> x1, Pallas kernels: none -> 3.06 us  [parted_measurements(): pl.pallas_call(part_kernel, out_shape=jax.ShapeDtypeStruct((POS, HALF, 2...]
    unnamed x19 -> x21, local copies, waits for them, and re-layouts: 2.94 us -> 3.97 us
  transfers between devices with their start and end apart: 16 -> 16, of which waited for: 9 -> 8; matrix products, arithmetic and copies ran while one was open for 6% -> 6% of each run, Pallas kernels for 3% -> 4%
where the time goes in v4:
time: 172 us
  waiting for transfers between devices  73.2 us (43%)
  starting transfers between devices  52.8 us (31%)
  Pallas kernels  28.9 us (17%)
  other arithmetic  12.1 us (7%)
  local copies, waits for them, and re-layouts  4.13 us (2%)
    ppermute x4, waiting for transfers between devices, rows_of(): return lax.ppermute(x, 'row', pairs('row', first))  28.9 us
    ppermute x4, starting transfers between devices, rows_of(): return lax.ppermute(x, 'row', pairs('row', first))  22 us
    ppermute x8, starting transfers between devices, cols_of(): return lax.ppermute(x, 'col', pairs('col', first))  20.4 us
    ppermute x2, waiting for transfers between devices, routed(): return (got, lax.ppermute(got, 'row', over), *others)  18.4 us
    pallas_call x1, Pallas kernels, window_gradients(): pl.pallas_call(gradient_kernel, out_shape=shapes, in_specs=[scalars] * 3...  17.3 us
    ppermute x8, waiting for transfers between devices, cols_of(): return lax.ppermute(x, 'col', pairs('col', first))  15.7 us
    ppermute x2, waiting for transfers between devices, routed(): lax.ppermute(x, 'row', detour)  10.2 us
    pallas_call x2, Pallas kernels, add_in_place(): pl.pallas_call(kernel, out_shape=jax.ShapeDtypeStruct(out.shape, out.dtyp...  8.59 us
  transfers between devices with their start and end apart: 16, of which 8 were waited for; matrix products, arithmetic and copies ran while one was open for 6% of the time, Pallas kernels for 4%

profile of v4, /device:TPU:60, one launch (start us, length us, event | category | flops | bytes accessed | tf_op | source)
XLA Modules:
  0.0 172.1 jit_solution(4792812282462177307)
XLA Ops:
  0.0 2.7 %slice_select_fusion = (f32[2,2,512,128]{3,2,1,0:T(8,128)}, f32[2,2,512,128]{3,2,1,0:T(8,128)S(1)}) fusion(f32[2,2,512,512]{3,2,1,0:T(8,128)} %refs_0_.1, pred[]{:T(512)S(6)} %eq.19), kind=kLoop, calls=%fused_computation | loop fusion | flops 524288 | bytes 4194305 | tf_op jit(solution)/shard_map/jit(_where)/select_n | solution.py:420
  2.7 1.9 %collective-permute-start.3 = (f32[2,2,512,128]{3,2,1,0:T(8,128)S(1)}, f32[2,2,512,128]{3,2,1,0:T(8,128)}, u32[]{:S(2)}, u32[]{:S(2)}) collective-permute-start(f32[2,2,512,128]{3,2,1,0:T(8,128)S(1)} %get-tuple-element.101), channel_id=1, source_target_pairs={{8,16},{24,32},{40,48},{56,64},{72,80},{88,96},{104,112},{120,128}... | collective-permute-start | bytes 3145736 | tf_op jit(solution)/shard_map/ppermute | solution.py:412
  4.6 2.8 %slice_select_fusion.2 = (f32[2,2,128,512]{3,2,1,0:T(8,128)S(1)}, f32[2,2,128,512]{3,2,1,0:T(8,128)}) fusion(f32[2,2,512,512]{3,2,1,0:T(8,128)} %refs_0_.1, pred[]{:T(512)S(6)} %eq.18), kind=kLoop, calls=%fused_computation.2 | loop fusion | flops 524288 | bytes 4194305 | tf_op jit(solution)/shard_map/jit(_where)/select_n | solution.py:423
  7.5 2.2 %collective-permute-start.2 = (f32[1,2,128,512]{3,2,1,0:T(8,128)S(1)}, f32[1,2,128,512]{3,2,1,0:T(8,128)S(1)}, u32[]{:S(2)}, u32[]{:S(2)}) collective-permute-start(f32[1,2,128,512]{3,2,1,0:T(8,128)S(1)} %get-tuple-element.106), channel_id=1, source_target_pairs={{1,2},{5,6},{2,1},{6,5},{3,0},{4,7},{9,10},{13,14},{10,9},{14,13},... | collective-permute-start | bytes 1572872 | tf_op jit(solution)/shard_map/ppermute | solution.py:415
  10.7 10.2 %collective-permute-done.2.refs_3_ = f32[1,2,128,512]{3,2,1,0:T(8,128)S(1)} collective-permute-done((f32[1,2,128,512]{3,2,1,0:T(8,128)S(1)}, f32[1,2,128,512]{3,2,1,0:T(8,128)S(1)}, u32[]{:S(2)}, u32[]{:S(2)}) %collective-permute-start.2) | collective-permute-done | bytes 524320 | tf_op jit(solution)/shard_map/ppermute | solution.py:415
  20.9 6.5 %collective-permute-done.3.refs_6_ = f32[2,2,512,128]{3,2,1,0:T(8,128)} collective-permute-done((f32[2,2,512,128]{3,2,1,0:T(8,128)S(1)}, f32[2,2,512,128]{3,2,1,0:T(8,128)}, u32[]{:S(2)}, u32[]{:S(2)}) %collective-permute-start.3) | collective-permute-done | bytes 1048608 | tf_op jit(solution)/shard_map/ppermute | solution.py:412
  28.7 9.7 %collective-permute-start.1 = (f32[1,2,128,512]{3,2,1,0:T(8,128)S(1)}, f32[1,2,128,512]{3,2,1,0:T(8,128)S(1)}, u32[]{:S(2)}, u32[]{:S(2)}) collective-permute-start(f32[1,2,128,512]{3,2,1,0:T(8,128)S(1)} %get-tuple-element.107), channel_id=1, source_target_pairs={{1,2},{3,4},{5,6},{2,1},{4,3},{6,5},{9,10},{11,12},{13,14},{10,9},... | collective-permute-start | bytes 1572872 | tf_op jit(solution)/shard_map/ppermute | solution.py:409
  38.5 18.3 %collective-permute-done.4.refs_4_ = f32[1,2,128,512]{3,2,1,0:T(8,128)S(1)} collective-permute-done((f32[1,2,128,512]{3,2,1,0:T(8,128)S(1)}, f32[1,2,128,512]{3,2,1,0:T(8,128)S(1)}, u32[]{:S(2)}, u32[]{:S(2)}) %collective-permute-start.4) | collective-permute-done | bytes 524320 | tf_op jit(solution)/shard_map/ppermute | solution.py:416
  57.0 2.1 %collective-permute-done.1.refs_2_ = f32[1,2,128,512]{3,2,1,0:T(8,128)S(1)} collective-permute-done((f32[1,2,128,512]{3,2,1,0:T(8,128)S(1)}, f32[1,2,128,512]{3,2,1,0:T(8,128)S(1)}, u32[]{:S(2)}, u32[]{:S(2)}) %collective-permute-start.1) | collective-permute-done | bytes 524320 | tf_op jit(solution)/shard_map/ppermute | solution.py:409
  59.1 2.0 %broadcast_select_fusion.2 = (f32[2,2,256,128]{3,2,1,0:T(8,128)}, f32[2,2,256,128]{3,2,1,0:T(8,128)S(1)}, f32[2,2,256,128]{3,2,1,0:T(8,128)S(1)}) fusion(pred[]{:T(512)S(6)} %eq.19, f32[1,2,128,512]{3,2,1,0:T(8,128)S(1)} %select_select_fusion, f32[1,2,128,512]{3,2,1,0:T(8,128)S(1)} %collective-permute-done.1.refs_2_, ...), kind=kLoop, calls=%fused_computation.14 | loop fusion | flops 655360 | bytes 3670017 | tf_op jit(solution)/shard_map/jit(_where)/select_n | solution.py:420
  62.9 2.5 %collective-permute-start.7 = (f32[2,2,256,128]{3,2,1,0:T(8,128)}, f32[2,2,256,128]{3,2,1,0:T(8,128)S(1)}, u32[]{:S(2)}, u32[]{:S(2)}) collective-permute-start(f32[2,2,256,128]{3,2,1,0:T(8,128)} %get-tuple-element.97), channel_id=1, source_target_pairs={{8,16},{24,32},{40,48},{56,64},{72,80},{88,96},{104,112},{120,128}... | collective-permute-start | bytes 1572872 | tf_op jit(solution)/shard_map/ppermute | solution.py:412
  66.2 3.1 %shard_map.82.refs_10_ = f32[3,128,512]{2,1,0:T(8,128)} custom-call(f32[3,256,256]{2,1,0:T(8,128)} %bitcast.5, bf16[256,256]{1,0:T(8,128)(2,1)} %constant.167.clone.order), custom_call_target="tpu_custom_call" | custom-call | flops 1000000000 | bytes 1000000 | tf_op jit(solution)/shard_map/pallas_call | solution.py:182
  69.4 5.8 %collective-permute-done.7.refs_8_ = f32[2,2,256,128]{3,2,1,0:T(8,128)S(1)} collective-permute-done((f32[2,2,256,128]{3,2,1,0:T(8,128)}, f32[2,2,256,128]{3,2,1,0:T(8,128)S(1)}, u32[]{:S(2)}, u32[]{:S(2)}) %collective-permute-start.7) | collective-permute-done | bytes 524320 | tf_op jit(solution)/shard_map/ppermute | solution.py:412
  78.1 17.3 %shard_map.83 = (f32[2,2,512,512]{3,2,1,0:T(8,128)}, f32[2,2,128,512]{3,2,1,0:T(8,128)}, f32[1,2,128,512]{3,2,1,0:T(8,128)S(1)}, f32[1,2,128,512]{3,2,1,0:T(8,12...) custom-call(s32[3]{0:T(128)S(1)} %pad_add_fusion.place, ...), custom_call_target="tpu_custom_call" | custom-call | flops 10000000000 | bytes 30000000 | tf_op jit(solution)/shard_map/pallas_call | solution.py:302
  96.0 6.2 %collective-permute-start.9 = (f32[2,2,256,128]{3,2,1,0:T(8,128)S(1)}, f32[2,2,256,128]{3,2,1,0:T(8,128)S(1)}, u32[]{:S(2)}, u32[]{:S(2)}) collective-permute-start(f32[2,2,256,128]{3,2,1,0:T(8,128)S(1)} %get-tuple-element.91), channel_id=1, source_target_pairs={{8,16},{24,32},{40,48},{56,64},{72,80},{88,96},{104,112},{120,128}... | collective-permute-start | bytes 1572872 | tf_op jit(solution)/shard_map/ppermute | solution.py:412
  102.6 7.7 %collective-permute-start.15 = (f32[2,2,512,128]{3,2,1,0:T(8,128)}, f32[2,2,512,128]{3,2,1,0:T(8,128)S(1)}, u32[]{:S(2)}, u32[]{:S(2)}) collective-permute-start(f32[2,2,512,128]{3,2,1,0:T(8,128)} %get-tuple-element.95), channel_id=1, source_target_pairs={{8,16},{24,32},{40,48},{56,64},{72,80},{88,96},{104,112},{120,128}... | collective-permute-start | bytes 3145736 | tf_op jit(solution)/shard_map/ppermute | solution.py:412
  110.9 1.7 %fusion.1 = f32[2,2,128,512]{3,2,1,0:T(8,128)} fusion(f32[2,2,128,512]{3,2,1,0:T(8,128)} %get-tuple-element.89, f32[2,2,256,128]{3,2,1,0:T(8,128)S(1)} %get-tuple-element.105), kind=kLoop, calls=%fused_computation.11 | loop fusion | flops 65536 | bytes 786432 | tf_op jit(solution)/shard_map/scatter-add | solution.py:446
  112.7 5.7 %collective-permute-start.12 = (f32[1,2,128,512]{3,2,1,0:T(8,128)S(1)}, f32[1,2,128,512]{3,2,1,0:T(8,128)S(1)}, u32[]{:S(2)}, u32[]{:S(2)}) collective-permute-start(f32[1,2,128,512]{3,2,1,0:T(8,128)S(1)} %get-tuple-element.108), channel_id=1, source_target_pairs={{1,2},{5,6},{2,1},{6,5},{3,0},{4,7},{9,10},{13,14},{10,9},{14,13},... | collective-permute-start | bytes 1572872 | tf_op jit(solution)/shard_map/ppermute | solution.py:415
  118.4 1.7 %fusion = f32[2,2,128,512]{3,2,1,0:T(8,128)} fusion(f32[2,2,128,512]{3,2,1,0:T(8,128)} %fusion.1, f32[2,2,256,128]{3,2,1,0:T(8,128)S(1)} %get-tuple-element.104), kind=kLoop, calls=%fused_computation.9 | loop fusion | flops 65536 | bytes 786432 | tf_op jit(solution)/shard_map/scatter-add | solution.py:447
  120.1 11.2 %collective-permute-start.11 = (f32[1,2,128,512]{3,2,1,0:T(8,128)S(1)}, f32[1,2,128,512]{3,2,1,0:T(8,128)}, u32[]{:S(2)}, u32[]{:S(2)}) collective-permute-start(f32[1,2,128,512]{3,2,1,0:T(8,128)S(1)} %get-tuple-element.109), channel_id=1, source_target_pairs={{1,2},{3,4},{5,6},{2,1},{4,3},{6,5},{9,10},{11,12},{13,14},{10,9},... | collective-permute-start | bytes 1572872 | tf_op jit(solution)/shard_map/ppermute | solution.py:409
  132.7 2.9 %collective-permute-done.15.side_b = f32[2,2,512,128]{3,2,1,0:T(8,128)S(1)} collective-permute-done((f32[2,2,512,128]{3,2,1,0:T(8,128)}, f32[2,2,512,128]{3,2,1,0:T(8,128)S(1)}, u32[]{:S(2)}, u32[]{:S(2)}) %collective-permute-start.15) | collective-permute-done | bytes 1048608 | tf_op jit(solution)/shard_map/ppermute | solution.py:412
  136.6 4.4 %shard_map.84.held = f32[2,2,512,512]{3,2,1,0:T(8,128)} custom-call(s32[3]{0:T(128)} %copy-done, f32[2,2,512,128]{3,2,1,0:T(8,128)} %copy-done.6, f32[2,2,512,128]{3,2,1,0:T(8,128)} %copy-done.7, f32[2,2,512,512]{3,2,1,0:T(8,128)} %get-tuple-element.96.held), custom_call_target="tpu_custom_call", output_to_operand_aliasing={{}: (3, {})} | custom-call | flops 1000000 | bytes 6000000 | tf_op jit(solution)/shard_map/pallas_call | solution.py:379
  141.0 26.9 %collective-permute-done.11.strip_b0 = f32[1,2,128,512]{3,2,1,0:T(8,128)} collective-permute-done((f32[1,2,128,512]{3,2,1,0:T(8,128)S(1)}, f32[1,2,128,512]{3,2,1,0:T(8,128)}, u32[]{:S(2)}, u32[]{:S(2)}) %collective-permute-start.11) | collective-permute-done | bytes 524320 | tf_op jit(solution)/shard_map/ppermute | solution.py:409
  167.9 4.2 %shard_map.85 = f32[2,2,512,512]{3,2,1,0:T(8,128)} custom-call(s32[3]{0:T(128)} %copy-done, f32[2,2,128,512]{3,2,1,0:T(8,128)} %collective-permute-done.10.strip_a, f32[1,2,128,512]{3,2,1,0:T(8,128)} %collective-permute-done.11.strip_b0, f32[1,2,128,512]{3,2,1,0:T(8,128)} %copy-done.8, ...), custom_call_target="tpu_custom_call", output_to_operand_aliasing={{}: (5, {})} | custom-call | flops 1000000 | bytes 6000000 | tf_op jit(solution)/shard_map/pallas_call | solution.py:379
  (46 shorter events, 11.6 us)
Async XLA Ops:
  2.7 24.7 %collective-permute-start.3 = (f32[2,2,512,128]{3,2,1,0:T(8,128)S(1)}, f32[2,2,512,128]{3,2,1,0:T(8,128)}, u32[]{:S(2)}, u32[]{:S(2)}) collective-permute-start(f32[2,2,512,128]{3,2,1,0:T(8,128)S(1)} %get-tuple-element.101), channel_id=1, source_target_pairs={{8,16},{24,32},{40,48},{56,64},{72,80},{88,96},{104,112},{120,128}... | collective-permute-start | bytes 3145736 | tf_op jit(solution)/shard_map/ppermute | solution.py:412
  7.4 58.6 %copy-start.9 = (s32[1,1,3,2]{2,3,1,0:T(2,128)S(1)}, s32[1,1,3,2]{2,3,1,0:T(2,128)}, u32[]{:S(2)}) copy-start(s32[1,1,3,2]{2,3,1,0:T(2,128)} %param.23) | copy-start | bytes 76
  7.5 13.4 %collective-permute-start.2 = (f32[1,2,128,512]{3,2,1,0:T(8,128)S(1)}, f32[1,2,128,512]{3,2,1,0:T(8,128)S(1)}, u32[]{:S(2)}, u32[]{:S(2)}) collective-permute-start(f32[1,2,128,512]{3,2,1,0:T(8,128)S(1)} %get-tuple-element.106), channel_id=1, source_target_pairs={{1,2},{5,6},{2,1},{6,5},{3,0},{4,7},{9,10},{13,14},{10,9},{14,13},... | collective-permute-start | bytes 1572872 | tf_op jit(solution)/shard_map/ppermute | solution.py:415
  9.7 49.4 %collective-permute-start = (f32[2,2,128,512]{3,2,1,0:T(8,128)}, f32[2,2,128,512]{3,2,1,0:T(8,128)}, u32[]{:S(2)}, u32[]{:S(2)}) collective-permute-start(f32[2,2,128,512]{3,2,1,0:T(8,128)} %get-tuple-element.103), channel_id=1, source_target_pairs={{0,1},{2,3},{4,5},{6,7},{1,0},{3,2},{5,4},{7,6},{8,9},{10,11},{12,... | collective-permute-start | bytes 3145736 | tf_op jit(solution)/shard_map/ppermute | solution.py:409
  27.4 29.5 %collective-permute-start.4 = (f32[1,2,128,512]{3,2,1,0:T(8,128)S(1)}, f32[1,2,128,512]{3,2,1,0:T(8,128)S(1)}, u32[]{:S(2)}, u32[]{:S(2)}) collective-permute-start(f32[1,2,128,512]{3,2,1,0:T(8,128)S(1)} %collective-permute-done.2.refs_3_), channel_id=1, source_target_pairs={{0,4},{7,3},{8,12},{15,11},{16,20},{23,19},{24,28},{31,27},{32,36}... | collective-permute-start | bytes 1572872 | tf_op jit(solution)/shard_map/ppermute | solution.py:416
  28.7 30.4 %collective-permute-start.1 = (f32[1,2,128,512]{3,2,1,0:T(8,128)S(1)}, f32[1,2,128,512]{3,2,1,0:T(8,128)S(1)}, u32[]{:S(2)}, u32[]{:S(2)}) collective-permute-start(f32[1,2,128,512]{3,2,1,0:T(8,128)S(1)} %get-tuple-element.107), channel_id=1, source_target_pairs={{1,2},{3,4},{5,6},{2,1},{4,3},{6,5},{9,10},{11,12},{13,14},{10,9},... | collective-permute-start | bytes 1572872 | tf_op jit(solution)/shard_map/ppermute | solution.py:409
  38.4 31.0 %collective-permute-start.5 = (f32[2,2,512,128]{3,2,1,0:T(8,128)}, f32[2,2,512,128]{3,2,1,0:T(8,128)}, u32[]{:S(2)}, u32[]{:S(2)}) collective-permute-start(f32[2,2,512,128]{3,2,1,0:T(8,128)} %get-tuple-element.100), channel_id=1, source_target_pairs={{0,8},{16,24},{32,40},{48,56},{64,72},{80,88},{96,104},{112,120},{... | collective-permute-start | bytes 3145736 | tf_op jit(solution)/shard_map/ppermute | solution.py:412
  57.0 19.0 %copy-start.1 = (f32[2,256,256]{2,1,0:T(8,128)S(1)}, f32[2,256,256]{2,1,0:T(8,128)}, u32[]{:S(2)}) copy-start(f32[2,256,256]{2,1,0:T(8,128)} %refs_9_.1) | copy-start | bytes 1572868
  57.0 19.0 %copy-start.5 = (f32[4,128,128]{2,1,0:T(8,128)S(1)}, f32[4,128,128]{2,1,0:T(8,128)}, u32[]{:S(2)}) copy-start(f32[4,128,128]{2,1,0:T(8,128)} %constant.169.clone.refs_12_) | copy-start | bytes 786436
  61.9 7.5 %collective-permute-start.6 = (f32[2,2,256,128]{3,2,1,0:T(8,128)}, f32[2,2,256,128]{3,2,1,0:T(8,128)S(1)}, u32[]{:S(2)}, u32[]{:S(2)}) collective-permute-start(f32[2,2,256,128]{3,2,1,0:T(8,128)} %broadcast_select_fusion.3), channel_id=1, source_target_pairs={{0,8},{16,24},{32,40},{48,56},{64,72},{80,88},{96,104},{112,120},{... | collective-permute-start | bytes 1572872 | tf_op jit(solution)/shard_map/ppermute | solution.py:412
  62.9 12.3 %collective-permute-start.7 = (f32[2,2,256,128]{3,2,1,0:T(8,128)}, f32[2,2,256,128]{3,2,1,0:T(8,128)S(1)}, u32[]{:S(2)}, u32[]{:S(2)}) collective-permute-start(f32[2,2,256,128]{3,2,1,0:T(8,128)} %get-tuple-element.97), channel_id=1, source_target_pairs={{8,16},{24,32},{40,48},{56,64},{72,80},{88,96},{104,112},{120,128}... | collective-permute-start | bytes 1572872 | tf_op jit(solution)/shard_map/ppermute | solution.py:412
  69.4 26.0 %copy-start = (s32[3]{0:T(128)}, s32[3]{0:T(128)S(1)}, u32[]{:S(2)}) copy-start(s32[3]{0:T(128)S(1)} %pad_add_fusion.place) | copy-start | bytes 40
  76.0 1.0 copy-start.3
  77.0 1.0 copy-start.4
  95.4 14.9 %collective-permute-start.8 = (f32[2,2,256,128]{3,2,1,0:T(8,128)S(1)}, f32[2,2,256,128]{3,2,1,0:T(8,128)S(1)}, u32[]{:S(2)}, u32[]{:S(2)}) collective-permute-start(f32[2,2,256,128]{3,2,1,0:T(8,128)S(1)} %get-tuple-element.90), channel_id=1, source_target_pairs={{0,8},{16,24},{32,40},{48,56},{64,72},{80,88},{96,104},{112,120},{... | collective-permute-start | bytes 1572872 | tf_op jit(solution)/shard_map/ppermute | solution.py:412
  96.0 14.8 %collective-permute-start.9 = (f32[2,2,256,128]{3,2,1,0:T(8,128)S(1)}, f32[2,2,256,128]{3,2,1,0:T(8,128)S(1)}, u32[]{:S(2)}, u32[]{:S(2)}) collective-permute-start(f32[2,2,256,128]{3,2,1,0:T(8,128)S(1)} %get-tuple-element.91), channel_id=1, source_target_pairs={{8,16},{24,32},{40,48},{56,64},{72,80},{88,96},{104,112},{120,128}... | collective-permute-start | bytes 1572872 | tf_op jit(solution)/shard_map/ppermute | solution.py:412
  102.2 30.5 %collective-permute-start.14 = (f32[2,2,512,128]{3,2,1,0:T(8,128)}, f32[2,2,512,128]{3,2,1,0:T(8,128)S(1)}, u32[]{:S(2)}, u32[]{:S(2)}) collective-permute-start(f32[2,2,512,128]{3,2,1,0:T(8,128)} %get-tuple-element.94), channel_id=1, source_target_pairs={{0,8},{16,24},{32,40},{48,56},{64,72},{80,88},{96,104},{112,120},{... | collective-permute-start | bytes 3145736 | tf_op jit(solution)/shard_map/ppermute | solution.py:412
  102.6 33.0 %collective-permute-start.15 = (f32[2,2,512,128]{3,2,1,0:T(8,128)}, f32[2,2,512,128]{3,2,1,0:T(8,128)S(1)}, u32[]{:S(2)}, u32[]{:S(2)}) collective-permute-start(f32[2,2,512,128]{3,2,1,0:T(8,128)} %get-tuple-element.95), channel_id=1, source_target_pairs={{8,16},{24,32},{40,48},{56,64},{72,80},{88,96},{104,112},{120,128}... | collective-permute-start | bytes 3145736 | tf_op jit(solution)/shard_map/ppermute | solution.py:412
  112.7 18.7 %collective-permute-start.12 = (f32[1,2,128,512]{3,2,1,0:T(8,128)S(1)}, f32[1,2,128,512]{3,2,1,0:T(8,128)S(1)}, u32[]{:S(2)}, u32[]{:S(2)}) collective-permute-start(f32[1,2,128,512]{3,2,1,0:T(8,128)S(1)} %get-tuple-element.108), channel_id=1, source_target_pairs={{1,2},{5,6},{2,1},{6,5},{3,0},{4,7},{9,10},{13,14},{10,9},{14,13},... | collective-permute-start | bytes 1572872 | tf_op jit(solution)/shard_map/ppermute | solution.py:415
  120.1 47.8 %collective-permute-start.10 = (f32[2,2,128,512]{3,2,1,0:T(8,128)}, f32[2,2,128,512]{3,2,1,0:T(8,128)}, u32[]{:S(2)}, u32[]{:S(2)}) collective-permute-start(f32[2,2,128,512]{3,2,1,0:T(8,128)} %fusion), channel_id=1, source_target_pairs={{0,1},{2,3},{4,5},{6,7},{1,0},{3,2},{5,4},{7,6},{8,9},{10,11},{12,... | collective-permute-start | bytes 3145736 | tf_op jit(solution)/shard_map/ppermute | solution.py:409
  120.1 47.8 %collective-permute-start.11 = (f32[1,2,128,512]{3,2,1,0:T(8,128)S(1)}, f32[1,2,128,512]{3,2,1,0:T(8,128)}, u32[]{:S(2)}, u32[]{:S(2)}) collective-permute-start(f32[1,2,128,512]{3,2,1,0:T(8,128)S(1)} %get-tuple-element.109), channel_id=1, source_target_pairs={{1,2},{3,4},{5,6},{2,1},{4,3},{6,5},{9,10},{11,12},{13,14},{10,9},... | collective-permute-start | bytes 1572872 | tf_op jit(solution)/shard_map/ppermute | solution.py:409
  131.4 36.5 %copy-start.8 = (f32[1,2,128,512]{3,2,1,0:T(8,128)}, f32[1,2,128,512]{3,2,1,0:T(8,128)S(1)}, u32[]{:S(2)}) copy-start(f32[1,2,128,512]{3,2,1,0:T(8,128)S(1)} %collective-permute-done.12.strip_b1) | copy-start | bytes 1572868
  131.4 36.5 %collective-permute-start.13 = (f32[1,2,128,512]{3,2,1,0:T(8,128)S(1)}, f32[1,2,128,512]{3,2,1,0:T(8,128)}, u32[]{:S(2)}, u32[]{:S(2)}) collective-permute-start(f32[1,2,128,512]{3,2,1,0:T(8,128)S(1)} %collective-permute-done.12.strip_b1), channel_id=1, source_target_pairs={{0,4},{7,3},{8,12},{15,11},{16,20},{23,19},{24,28},{31,27},{32,36}... | collective-permute-start | bytes 1572872 | tf_op jit(solution)/shard_map/ppermute | solution.py:416
  132.7 2.9 %copy-start.6 = (f32[2,2,512,128]{3,2,1,0:T(8,128)}, f32[2,2,512,128]{3,2,1,0:T(8,128)S(1)}, u32[]{:S(2)}) copy-start(f32[2,2,512,128]{3,2,1,0:T(8,128)S(1)} %collective-permute-done.14.side_a) | copy-start | bytes 3145732
  (2 other events, 1.8 us)

commit v5 on v4

--- a/solution.py
+++ b/solution.py
@@ -313,7 +313,7 @@
             pltpu.VMEM((4, HALF, HALF), jnp.float32),
             pltpu.SemaphoreType.DMA((20,)),
         ],
-        compiler_params=pltpu.CompilerParams(vmem_limit_bytes=48 * 1024 * 1024),
+        compiler_params=pltpu.CompilerParams(vmem_limit_bytes=58 * 1024 * 1024),
         cost_estimate=pl.CostEstimate(flops=10**10, bytes_accessed=3 * 10**7, transcendentals=0),
     )(place, offsets.reshape(-1), counts.reshape(-1), *pieces, probe, measurements, *tables)
 

time: 172 us -> 171 us (level)
  starting transfers between devices: 52.8 us -> 46.5 us
  waiting for transfers between devices: 73.2 us -> 78.6 us
    ppermute x8, waiting for transfers between devices: 15.7 us -> 38.6 us  [cols_of(): return lax.ppermute(x, 'col', pairs('col', first))]
    ppermute x4, waiting for transfers between devices: 28.9 us -> 8.21 us  [rows_of(): return lax.ppermute(x, 'row', pairs('row', first))]
    ppermute x4, starting transfers between devices: 22 us -> 16.6 us  [rows_of(): return lax.ppermute(x, 'row', pairs('row', first))]
    ppermute x2, waiting for transfers between devices: 10.2 us -> 13.2 us  [routed(): lax.ppermute(x, 'row', detour)]
    ppermute x2, starting transfers between devices: 7.85 us -> 5.05 us  [routed(): lax.ppermute(x, 'row', detour)]
    select_n x3, other arithmetic: 5.54 us -> 3.15 us  [ends(): return (jnp.where(inner, high, low), jnp.where(inner, low, high))]
    unnamed x21 -> x13, local copies, waits for them, and re-layouts: 3.97 us -> 2.09 us
    ppermute x8, starting transfers between devices: 20.4 us -> 22.2 us  [cols_of(): return lax.ppermute(x, 'col', pairs('col', first))]
  transfers between devices with their start and end apart: 16 -> 16, of which waited for: 8 -> 9; matrix products, arithmetic and copies ran while one was open for 6% -> 8% of each run, Pallas kernels for 4% -> 4%
where the time goes in v5:
time: 171 us
  waiting for transfers between devices  78.6 us (46%)
  starting transfers between devices  46.5 us (27%)
  Pallas kernels  27.2 us (16%)
  other arithmetic  13.8 us (8%)
  local copies, waits for them, and re-layouts  3.58 us (2%)
    ppermute x8, waiting for transfers between devices, cols_of(): return lax.ppermute(x, 'col', pairs('col', first))  38.6 us
    ppermute x8, starting transfers between devices, cols_of(): return lax.ppermute(x, 'col', pairs('col', first))  22.2 us
    ppermute x2, waiting for transfers between devices, routed(): return (got, lax.ppermute(got, 'row', over), *others)  18.6 us
    ppermute x4, starting transfers between devices, rows_of(): return lax.ppermute(x, 'row', pairs('row', first))  16.6 us
    pallas_call x1, Pallas kernels, window_gradients(): pl.pallas_call(gradient_kernel, out_shape=shapes, in_specs=[scalars] * 3...  15.5 us
    ppermute x2, waiting for transfers between devices, routed(): lax.ppermute(x, 'row', detour)  13.2 us
    pallas_call x2, Pallas kernels, add_in_place(): pl.pallas_call(kernel, out_shape=jax.ShapeDtypeStruct(out.shape, out.dtyp...  8.58 us
    ppermute x4, waiting for transfers between devices, rows_of(): return lax.ppermute(x, 'row', pairs('row', first))  8.21 us
  transfers between devices with their start and end apart: 16, of which 9 were waited for; matrix products, arithmetic and copies ran while one was open for 8% of the time, Pallas kernels for 4%

profile of v5, /device:TPU:60, one launch (start us, length us, event | category | flops | bytes accessed | tf_op | source)
XLA Modules:
  0.0 170.5 jit_solution(1673335705689973687)
XLA Ops:
  1.7 1.9 %collective-permute-start.3 = (f32[2,2,512,128]{3,2,1,0:T(8,128)S(1)}, f32[2,2,512,128]{3,2,1,0:T(8,128)}, u32[]{:S(2)}, u32[]{:S(2)}) collective-permute-start(f32[2,2,512,128]{3,2,1,0:T(8,128)S(1)} %get-tuple-element.101), channel_id=1, source_target_pairs={{8,16},{24,32},{40,48},{56,64},{72,80},{88,96},{104,112},{120,128}... | collective-permute-start | bytes 3145736 | tf_op jit(solution)/shard_map/ppermute | solution.py:412
  3.7 1.8 %slice_select_fusion.2 = (f32[2,2,128,512]{3,2,1,0:T(8,128)S(1)}, f32[2,2,128,512]{3,2,1,0:T(8,128)S(1)}) fusion(f32[2,2,512,512]{3,2,1,0:T(8,128)} %refs_0_.1, pred[]{:T(512)S(6)} %eq.18), kind=kLoop, calls=%fused_computation.2 | loop fusion | flops 524288 | bytes 4194305 | tf_op jit(solution)/shard_map/jit(_where)/select_n | solution.py:423
  6.3 3.0 %collective-permute-start.2 = (f32[1,2,128,512]{3,2,1,0:T(8,128)S(1)}, f32[1,2,128,512]{3,2,1,0:T(8,128)}, u32[]{:S(2)}, u32[]{:S(2)}) collective-permute-start(f32[1,2,128,512]{3,2,1,0:T(8,128)S(1)} %get-tuple-element.106), channel_id=1, source_target_pairs={{1,2},{5,6},{2,1},{6,5},{3,0},{4,7},{9,10},{13,14},{10,9},{14,13},... | collective-permute-start | bytes 1572872 | tf_op jit(solution)/shard_map/ppermute | solution.py:415
  9.5 10.2 %collective-permute-done.2.refs_3_ = f32[1,2,128,512]{3,2,1,0:T(8,128)} collective-permute-done((f32[1,2,128,512]{3,2,1,0:T(8,128)S(1)}, f32[1,2,128,512]{3,2,1,0:T(8,128)}, u32[]{:S(2)}, u32[]{:S(2)}) %collective-permute-start.2) | collective-permute-done | bytes 524320 | tf_op jit(solution)/shard_map/ppermute | solution.py:415
  19.7 6.7 %collective-permute-done.3.refs_6_ = f32[2,2,512,128]{3,2,1,0:T(8,128)} collective-permute-done((f32[2,2,512,128]{3,2,1,0:T(8,128)S(1)}, f32[2,2,512,128]{3,2,1,0:T(8,128)}, u32[]{:S(2)}, u32[]{:S(2)}) %collective-permute-start.3) | collective-permute-done | bytes 1048608 | tf_op jit(solution)/shard_map/ppermute | solution.py:412
  27.7 9.7 %collective-permute-start.1 = (f32[1,2,128,512]{3,2,1,0:T(8,128)}, f32[1,2,128,512]{3,2,1,0:T(8,128)S(1)}, u32[]{:S(2)}, u32[]{:S(2)}) collective-permute-start(f32[1,2,128,512]{3,2,1,0:T(8,128)} %get-tuple-element.107), channel_id=1, source_target_pairs={{1,2},{3,4},{5,6},{2,1},{4,3},{6,5},{9,10},{11,12},{13,14},{10,9},... | collective-permute-start | bytes 1572872 | tf_op jit(solution)/shard_map/ppermute | solution.py:409
  37.6 18.6 %collective-permute-done.4.refs_4_ = f32[1,2,128,512]{3,2,1,0:T(8,128)S(1)} collective-permute-done((f32[1,2,128,512]{3,2,1,0:T(8,128)}, f32[1,2,128,512]{3,2,1,0:T(8,128)S(1)}, u32[]{:S(2)}, u32[]{:S(2)}) %collective-permute-start.4) | collective-permute-done | bytes 524320 | tf_op jit(solution)/shard_map/ppermute | solution.py:416
  59.9 2.1 %collective-permute-start.6 = (f32[2,2,256,128]{3,2,1,0:T(8,128)S(1)}, f32[2,2,256,128]{3,2,1,0:T(8,128)}, u32[]{:S(2)}, u32[]{:S(2)}) collective-permute-start(f32[2,2,256,128]{3,2,1,0:T(8,128)S(1)} %broadcast_select_fusion.3), channel_id=1, source_target_pairs={{0,8},{16,24},{32,40},{48,56},{64,72},{80,88},{96,104},{112,120},{... | collective-permute-start | bytes 1572872 | tf_op jit(solution)/shard_map/ppermute | solution.py:412
  62.0 1.9 %collective-permute-start.7 = (f32[2,2,256,128]{3,2,1,0:T(8,128)S(1)}, f32[2,2,256,128]{3,2,1,0:T(8,128)}, u32[]{:S(2)}, u32[]{:S(2)}) collective-permute-start(f32[2,2,256,128]{3,2,1,0:T(8,128)S(1)} %get-tuple-element.97), channel_id=1, source_target_pairs={{8,16},{24,32},{40,48},{56,64},{72,80},{88,96},{104,112},{120,128}... | collective-permute-start | bytes 1572872 | tf_op jit(solution)/shard_map/ppermute | solution.py:412
  65.3 3.1 %shard_map.82.refs_10_ = f32[3,128,512]{2,1,0:T(8,128)} custom-call(f32[3,256,256]{2,1,0:T(8,128)} %bitcast.5, bf16[256,256]{1,0:T(8,128)(2,1)} %constant.167.clone.order), custom_call_target="tpu_custom_call" | custom-call | flops 1000000000 | bytes 1000000 | tf_op jit(solution)/shard_map/pallas_call | solution.py:182
  69.0 4.8 %collective-permute-done.7.refs_8_ = f32[2,2,256,128]{3,2,1,0:T(8,128)} collective-permute-done((f32[2,2,256,128]{3,2,1,0:T(8,128)S(1)}, f32[2,2,256,128]{3,2,1,0:T(8,128)}, u32[]{:S(2)}, u32[]{:S(2)}) %collective-permute-start.7) | collective-permute-done | bytes 524320 | tf_op jit(solution)/shard_map/ppermute | solution.py:412
  73.8 15.5 %shard_map.83 = (f32[2,2,512,512]{3,2,1,0:T(8,128)}, f32[2,2,128,512]{3,2,1,0:T(8,128)}, f32[1,2,128,512]{3,2,1,0:T(8,128)}, f32[1,2,128,512]{3,2,1,0:T(8,128)},...) custom-call(s32[3]{0:T(128)} %pad_add_fusion.place, ...), custom_call_target="tpu_custom_call" | custom-call | flops 10000000000 | bytes 30000000 | tf_op jit(solution)/shard_map/pallas_call | solution.py:302
  89.3 9.9 %collective-permute-start.8 = (f32[2,2,256,128]{3,2,1,0:T(8,128)}, f32[2,2,256,128]{3,2,1,0:T(8,128)S(1)}, u32[]{:S(2)}, u32[]{:S(2)}) collective-permute-start(f32[2,2,256,128]{3,2,1,0:T(8,128)} %get-tuple-element.90), channel_id=1, source_target_pairs={{0,8},{16,24},{32,40},{48,56},{64,72},{80,88},{96,104},{112,120},{... | collective-permute-start | bytes 1572872 | tf_op jit(solution)/shard_map/ppermute | solution.py:412
  99.3 3.8 %collective-permute-start.9 = (f32[2,2,256,128]{3,2,1,0:T(8,128)}, f32[2,2,256,128]{3,2,1,0:T(8,128)S(1)}, u32[]{:S(2)}, u32[]{:S(2)}) collective-permute-start(f32[2,2,256,128]{3,2,1,0:T(8,128)} %get-tuple-element.91), channel_id=1, source_target_pairs={{8,16},{24,32},{40,48},{56,64},{72,80},{88,96},{104,112},{120,128}... | collective-permute-start | bytes 1572872 | tf_op jit(solution)/shard_map/ppermute | solution.py:412
  103.2 2.3 %collective-permute-start.15 = (f32[2,2,512,128]{3,2,1,0:T(8,128)}, f32[2,2,512,128]{3,2,1,0:T(8,128)S(1)}, u32[]{:S(2)}, u32[]{:S(2)}) collective-permute-start(f32[2,2,512,128]{3,2,1,0:T(8,128)} %get-tuple-element.95), channel_id=1, source_target_pairs={{8,16},{24,32},{40,48},{56,64},{72,80},{88,96},{104,112},{120,128}... | collective-permute-start | bytes 3145736 | tf_op jit(solution)/shard_map/ppermute | solution.py:412
  105.5 10.1 %collective-permute-done.9 = f32[2,2,256,128]{3,2,1,0:T(8,128)S(1)} collective-permute-done((f32[2,2,256,128]{3,2,1,0:T(8,128)}, f32[2,2,256,128]{3,2,1,0:T(8,128)S(1)}, u32[]{:S(2)}, u32[]{:S(2)}) %collective-permute-start.9) | collective-permute-done | bytes 524320 | tf_op jit(solution)/shard_map/ppermute | solution.py:412
  115.7 1.7 %fusion.1 = f32[2,2,128,512]{3,2,1,0:T(8,128)} fusion(f32[2,2,128,512]{3,2,1,0:T(8,128)} %get-tuple-element.89, f32[2,2,256,128]{3,2,1,0:T(8,128)S(1)} %get-tuple-element.105), kind=kLoop, calls=%fused_computation.11 | loop fusion | flops 65536 | bytes 786432 | tf_op jit(solution)/shard_map/scatter-add | solution.py:446
  120.8 2.1 %collective-permute-start.12 = (f32[1,2,128,512]{3,2,1,0:T(8,128)}, f32[1,2,128,512]{3,2,1,0:T(8,128)}, u32[]{:S(2)}, u32[]{:S(2)}) collective-permute-start(f32[1,2,128,512]{3,2,1,0:T(8,128)} %get-tuple-element.108), channel_id=1, source_target_pairs={{1,2},{5,6},{2,1},{6,5},{3,0},{4,7},{9,10},{13,14},{10,9},{14,13},... | collective-permute-start | bytes 1572872 | tf_op jit(solution)/shard_map/ppermute | solution.py:415
  124.7 6.7 %collective-permute-start.11 = (f32[1,2,128,512]{3,2,1,0:T(8,128)}, f32[1,2,128,512]{3,2,1,0:T(8,128)}, u32[]{:S(2)}, u32[]{:S(2)}) collective-permute-start(f32[1,2,128,512]{3,2,1,0:T(8,128)} %get-tuple-element.109), channel_id=1, source_target_pairs={{1,2},{3,4},{5,6},{2,1},{4,3},{6,5},{9,10},{11,12},{13,14},{10,9},... | collective-permute-start | bytes 1572872 | tf_op jit(solution)/shard_map/ppermute | solution.py:409
  131.4 3.0 %collective-permute-done.12.strip_b1 = f32[1,2,128,512]{3,2,1,0:T(8,128)} collective-permute-done((f32[1,2,128,512]{3,2,1,0:T(8,128)}, f32[1,2,128,512]{3,2,1,0:T(8,128)}, u32[]{:S(2)}, u32[]{:S(2)}) %collective-permute-start.12) | collective-permute-done | bytes 524320 | tf_op jit(solution)/shard_map/ppermute | solution.py:415
  135.7 17.0 %collective-permute-done.15.side_b = f32[2,2,512,128]{3,2,1,0:T(8,128)S(1)} collective-permute-done((f32[2,2,512,128]{3,2,1,0:T(8,128)}, f32[2,2,512,128]{3,2,1,0:T(8,128)S(1)}, u32[]{:S(2)}, u32[]{:S(2)}) %collective-permute-start.15) | collective-permute-done | bytes 1048608 | tf_op jit(solution)/shard_map/ppermute | solution.py:412
  153.7 4.4 %shard_map.84.held = f32[2,2,512,512]{3,2,1,0:T(8,128)} custom-call(s32[3]{0:T(128)} %pad_add_fusion.place, f32[2,2,512,128]{3,2,1,0:T(8,128)} %copy-done, f32[2,2,512,128]{3,2,1,0:T(8,128)} %copy-done.1, f32[2,2,512,512]{3,2,1,0:T(8,128)} %get-tuple-element.96.held), custom_call_target="tpu_custom_call", output_to_operand_aliasing={{}: (3, {})} | custom-call | flops 1000000 | bytes 6000000 | tf_op jit(solution)/shard_map/pallas_call | solution.py:379
  158.1 7.2 %collective-permute-done.11.strip_b0 = f32[1,2,128,512]{3,2,1,0:T(8,128)} collective-permute-done((f32[1,2,128,512]{3,2,1,0:T(8,128)}, f32[1,2,128,512]{3,2,1,0:T(8,128)}, u32[]{:S(2)}, u32[]{:S(2)}) %collective-permute-start.11) | collective-permute-done | bytes 524320 | tf_op jit(solution)/shard_map/ppermute | solution.py:409
  166.4 4.2 %shard_map.85 = f32[2,2,512,512]{3,2,1,0:T(8,128)} custom-call(s32[3]{0:T(128)} %pad_add_fusion.place, f32[2,2,128,512]{3,2,1,0:T(8,128)} %copy-done.2, f32[1,2,128,512]{3,2,1,0:T(8,128)} %collective-permute-done.11.strip_b0, f32[1,2,128,512]{3,2,1,0:T(8,128)} %collective-permute-done.12.strip_b1, ...), custom_call_target="tpu_custom_call", output_to_operand_aliasing={{}: (5, {})} | custom-call | flops 1000000 | bytes 6000000 | tf_op jit(solution)/shard_map/pallas_call | solution.py:379
  (38 shorter events, 17.8 us)
Async XLA Ops:
  1.7 24.7 %collective-permute-start.3 = (f32[2,2,512,128]{3,2,1,0:T(8,128)S(1)}, f32[2,2,512,128]{3,2,1,0:T(8,128)}, u32[]{:S(2)}, u32[]{:S(2)}) collective-permute-start(f32[2,2,512,128]{3,2,1,0:T(8,128)S(1)} %get-tuple-element.101), channel_id=1, source_target_pairs={{8,16},{24,32},{40,48},{56,64},{72,80},{88,96},{104,112},{120,128}... | collective-permute-start | bytes 3145736 | tf_op jit(solution)/shard_map/ppermute | solution.py:412
  5.5 59.1 %copy-start.5 = (s32[1,1,3,2]{2,3,1,0:T(2,128)S(1)}, s32[1,1,3,2]{2,3,1,0:T(2,128)}, u32[]{:S(2)}) copy-start(s32[1,1,3,2]{2,3,1,0:T(2,128)} %param.23) | copy-start | bytes 76
  6.3 13.4 %collective-permute-start.2 = (f32[1,2,128,512]{3,2,1,0:T(8,128)S(1)}, f32[1,2,128,512]{3,2,1,0:T(8,128)}, u32[]{:S(2)}, u32[]{:S(2)}) collective-permute-start(f32[1,2,128,512]{3,2,1,0:T(8,128)S(1)} %get-tuple-element.106), channel_id=1, source_target_pairs={{1,2},{5,6},{2,1},{6,5},{3,0},{4,7},{9,10},{13,14},{10,9},{14,13},... | collective-permute-start | bytes 1572872 | tf_op jit(solution)/shard_map/ppermute | solution.py:415
  9.3 49.1 %collective-permute-start = (f32[2,2,128,512]{3,2,1,0:T(8,128)S(1)}, f32[2,2,128,512]{3,2,1,0:T(8,128)}, u32[]{:S(2)}, u32[]{:S(2)}) collective-permute-start(f32[2,2,128,512]{3,2,1,0:T(8,128)S(1)} %get-tuple-element.103), channel_id=1, source_target_pairs={{0,1},{2,3},{4,5},{6,7},{1,0},{3,2},{5,4},{7,6},{8,9},{10,11},{12,... | collective-permute-start | bytes 3145736 | tf_op jit(solution)/shard_map/ppermute | solution.py:409
  26.4 29.7 %collective-permute-start.4 = (f32[1,2,128,512]{3,2,1,0:T(8,128)}, f32[1,2,128,512]{3,2,1,0:T(8,128)S(1)}, u32[]{:S(2)}, u32[]{:S(2)}) collective-permute-start(f32[1,2,128,512]{3,2,1,0:T(8,128)} %collective-permute-done.2.refs_3_), channel_id=1, source_target_pairs={{0,4},{7,3},{8,12},{15,11},{16,20},{23,19},{24,28},{31,27},{32,36}... | collective-permute-start | bytes 1572872 | tf_op jit(solution)/shard_map/ppermute | solution.py:416
  27.7 30.7 %collective-permute-start.1 = (f32[1,2,128,512]{3,2,1,0:T(8,128)}, f32[1,2,128,512]{3,2,1,0:T(8,128)S(1)}, u32[]{:S(2)}, u32[]{:S(2)}) collective-permute-start(f32[1,2,128,512]{3,2,1,0:T(8,128)} %get-tuple-element.107), channel_id=1, source_target_pairs={{1,2},{3,4},{5,6},{2,1},{4,3},{6,5},{9,10},{11,12},{13,14},{10,9},... | collective-permute-start | bytes 1572872 | tf_op jit(solution)/shard_map/ppermute | solution.py:409
  37.5 31.5 %collective-permute-start.5 = (f32[2,2,512,128]{3,2,1,0:T(8,128)S(1)}, f32[2,2,512,128]{3,2,1,0:T(8,128)}, u32[]{:S(2)}, u32[]{:S(2)}) collective-permute-start(f32[2,2,512,128]{3,2,1,0:T(8,128)S(1)} %get-tuple-element.100), channel_id=1, source_target_pairs={{0,8},{16,24},{32,40},{48,56},{64,72},{80,88},{96,104},{112,120},{... | collective-permute-start | bytes 3145736 | tf_op jit(solution)/shard_map/ppermute | solution.py:412
  56.1 12.2 %copy-start.3 = (f32[1,2,128,512]{3,2,1,0:T(8,128)}, f32[1,2,128,512]{3,2,1,0:T(8,128)S(1)}, u32[]{:S(2)}) copy-start(f32[1,2,128,512]{3,2,1,0:T(8,128)S(1)} %collective-permute-done.4.refs_4_) | copy-start | bytes 1572868
  58.4 10.0 %copy-start.4 = (f32[1,2,128,512]{3,2,1,0:T(8,128)}, f32[1,2,128,512]{3,2,1,0:T(8,128)S(1)}, u32[]{:S(2)}) copy-start(f32[1,2,128,512]{3,2,1,0:T(8,128)S(1)} %collective-permute-done.1.refs_2_) | copy-start | bytes 1572868
  59.9 9.1 %collective-permute-start.6 = (f32[2,2,256,128]{3,2,1,0:T(8,128)S(1)}, f32[2,2,256,128]{3,2,1,0:T(8,128)}, u32[]{:S(2)}, u32[]{:S(2)}) collective-permute-start(f32[2,2,256,128]{3,2,1,0:T(8,128)S(1)} %broadcast_select_fusion.3), channel_id=1, source_target_pairs={{0,8},{16,24},{32,40},{48,56},{64,72},{80,88},{96,104},{112,120},{... | collective-permute-start | bytes 1572872 | tf_op jit(solution)/shard_map/ppermute | solution.py:412
  62.0 11.8 %collective-permute-start.7 = (f32[2,2,256,128]{3,2,1,0:T(8,128)S(1)}, f32[2,2,256,128]{3,2,1,0:T(8,128)}, u32[]{:S(2)}, u32[]{:S(2)}) collective-permute-start(f32[2,2,256,128]{3,2,1,0:T(8,128)S(1)} %get-tuple-element.97), channel_id=1, source_target_pairs={{8,16},{24,32},{40,48},{56,64},{72,80},{88,96},{104,112},{120,128}... | collective-permute-start | bytes 1572872 | tf_op jit(solution)/shard_map/ppermute | solution.py:412
  89.3 16.2 %collective-permute-start.8 = (f32[2,2,256,128]{3,2,1,0:T(8,128)}, f32[2,2,256,128]{3,2,1,0:T(8,128)S(1)}, u32[]{:S(2)}, u32[]{:S(2)}) collective-permute-start(f32[2,2,256,128]{3,2,1,0:T(8,128)} %get-tuple-element.90), channel_id=1, source_target_pairs={{0,8},{16,24},{32,40},{48,56},{64,72},{80,88},{96,104},{112,120},{... | collective-permute-start | bytes 1572872 | tf_op jit(solution)/shard_map/ppermute | solution.py:412
  99.3 16.3 %collective-permute-start.9 = (f32[2,2,256,128]{3,2,1,0:T(8,128)}, f32[2,2,256,128]{3,2,1,0:T(8,128)S(1)}, u32[]{:S(2)}, u32[]{:S(2)}) collective-permute-start(f32[2,2,256,128]{3,2,1,0:T(8,128)} %get-tuple-element.91), channel_id=1, source_target_pairs={{8,16},{24,32},{40,48},{56,64},{72,80},{88,96},{104,112},{120,128}... | collective-permute-start | bytes 1572872 | tf_op jit(solution)/shard_map/ppermute | solution.py:412
  103.1 32.6 %collective-permute-start.14 = (f32[2,2,512,128]{3,2,1,0:T(8,128)}, f32[2,2,512,128]{3,2,1,0:T(8,128)S(1)}, u32[]{:S(2)}, u32[]{:S(2)}) collective-permute-start(f32[2,2,512,128]{3,2,1,0:T(8,128)} %get-tuple-element.94), channel_id=1, source_target_pairs={{0,8},{16,24},{32,40},{48,56},{64,72},{80,88},{96,104},{112,120},{... | collective-permute-start | bytes 3145736 | tf_op jit(solution)/shard_map/ppermute | solution.py:412
  103.2 49.5 %collective-permute-start.15 = (f32[2,2,512,128]{3,2,1,0:T(8,128)}, f32[2,2,512,128]{3,2,1,0:T(8,128)S(1)}, u32[]{:S(2)}, u32[]{:S(2)}) collective-permute-start(f32[2,2,512,128]{3,2,1,0:T(8,128)} %get-tuple-element.95), channel_id=1, source_target_pairs={{8,16},{24,32},{40,48},{56,64},{72,80},{88,96},{104,112},{120,128}... | collective-permute-start | bytes 3145736 | tf_op jit(solution)/shard_map/ppermute | solution.py:412
  120.8 13.6 %collective-permute-start.12 = (f32[1,2,128,512]{3,2,1,0:T(8,128)}, f32[1,2,128,512]{3,2,1,0:T(8,128)}, u32[]{:S(2)}, u32[]{:S(2)}) collective-permute-start(f32[1,2,128,512]{3,2,1,0:T(8,128)} %get-tuple-element.108), channel_id=1, source_target_pairs={{1,2},{5,6},{2,1},{6,5},{3,0},{4,7},{9,10},{13,14},{10,9},{14,13},... | collective-permute-start | bytes 1572872 | tf_op jit(solution)/shard_map/ppermute | solution.py:415
  124.7 40.7 %collective-permute-start.10 = (f32[2,2,128,512]{3,2,1,0:T(8,128)}, f32[2,2,128,512]{3,2,1,0:T(8,128)S(1)}, u32[]{:S(2)}, u32[]{:S(2)}) collective-permute-start(f32[2,2,128,512]{3,2,1,0:T(8,128)} %fusion), channel_id=1, source_target_pairs={{0,1},{2,3},{4,5},{6,7},{1,0},{3,2},{5,4},{7,6},{8,9},{10,11},{12,... | collective-permute-start | bytes 3145736 | tf_op jit(solution)/shard_map/ppermute | solution.py:409
  124.7 40.7 %collective-permute-start.11 = (f32[1,2,128,512]{3,2,1,0:T(8,128)}, f32[1,2,128,512]{3,2,1,0:T(8,128)}, u32[]{:S(2)}, u32[]{:S(2)}) collective-permute-start(f32[1,2,128,512]{3,2,1,0:T(8,128)} %get-tuple-element.109), channel_id=1, source_target_pairs={{1,2},{3,4},{5,6},{2,1},{4,3},{6,5},{9,10},{11,12},{13,14},{10,9},... | collective-permute-start | bytes 1572872 | tf_op jit(solution)/shard_map/ppermute | solution.py:409
  134.4 31.0 %collective-permute-start.13 = (f32[1,2,128,512]{3,2,1,0:T(8,128)}, f32[1,2,128,512]{3,2,1,0:T(8,128)}, u32[]{:S(2)}, u32[]{:S(2)}) collective-permute-start(f32[1,2,128,512]{3,2,1,0:T(8,128)} %collective-permute-done.12.strip_b1), channel_id=1, source_target_pairs={{0,4},{7,3},{8,12},{15,11},{16,20},{23,19},{24,28},{31,27},{32,36}... | collective-permute-start | bytes 1572872 | tf_op jit(solution)/shard_map/ppermute | solution.py:416
  135.7 17.0 %copy-start = (f32[2,2,512,128]{3,2,1,0:T(8,128)}, f32[2,2,512,128]{3,2,1,0:T(8,128)S(1)}, u32[]{:S(2)}) copy-start(f32[2,2,512,128]{3,2,1,0:T(8,128)S(1)} %collective-permute-done.14.side_a) | copy-start | bytes 3145732
  152.7 1.0 copy-start.1
  165.4 1.0 copy-start.2
